TPU v7x, 128 devices: a whole 4x4x4 slice. The times are simulated.
128 devices in a mesh: grp: 4 (over y), dev: 32 (over z, x, core).
Axes of the slice: x: 4, y: 4, z: 4, core: 2. Of those that a mesh axis runs over, the one named last changes fastest.
Arguments:
- face_owner: int32 [524288, 1], P(('grp', 'dev')), may hold values from 0 to 127; in each aligned block of 4096 rows (0 to 4095, 4096 to 8191, ...) at most 64 rows name the same one
- face_element: int32 [524288], P(('grp', 'dev')), may hold values from 0 to 16383
- element_state: bfloat16 [110, 524288], P(None, ('grp', 'dev')), may hold values from -6 to 6
- lift: bfloat16 [30, 110], replicated, may hold values from -0.5 to 0.5
- face_scale: float32 [524288], P(('grp', 'dev')), may hold values from 0.5 to 2
- transfer: float32 [4, 10], replicated, may hold values from 0.05 to 0.5
- stiffness_ref: float32 [12, 12], replicated, may hold values from -0.18 to 5, as said below
- element_scale: float32 [256, 8192], P('grp', 'dev'), may hold values from 1 to 1.1
- displacement_prev: float32 [4, 3, 256, 8192], P(None, None, 'grp', 'dev'), may hold values from -6 to 6
Outputs:
- shell_displacement: float32 [4, 3, 256, 8192], P(None, None, 'grp', 'dev')
- face_displacement: float32 [3, 10, 524288], P(None, None, ('grp', 'dev'))
Inputs may be any that keep to these rules, and one draw needn't show every extreme that they name: `face_owner`: among the 4096 faces of one device (aligned blocks), at most 64 name the same owner, and in every draw some device has exactly 64 faces on one owner. `stiffness_ref`: every diagonal entry is 5 and the off-diagonal entries of each row have absolute values summing to at most 2.
All inputs are finite; a program needn't handle non-finite values.
Results may differ from a plain program's by a relative error of at most 0.0003.
Values sent between devices are 32-bit elements; how exact they have to be, the bound alone decides.
No kernel may reach another device: no remote copies, remote signals or barrier semaphores. Data moves between devices by JAX's collectives and lax.ppermute only.
A program may use at most 128 MiB of HBM per device.

v0:
```python
import jax
import jax.numpy as jnp
from jax import lax
from jax.sharding import PartitionSpec as P

NODES_F = 10
SWEEPS = 8


coupling_weight = 2.2
highest = lax.Precision.HIGHEST


def with_halo(block, sides, width):
    for axis, dim in sides:
        count = lax.axis_size(axis)
        forward = [(i, i + 1) for i in range(count - 1)]
        backward = [(target, source) for source, target in forward]
        low = lax.ppermute(
            lax.slice_in_dim(block, block.shape[dim] - width, None, axis=dim), axis, forward
        )
        high = lax.ppermute(lax.slice_in_dim(block, 0, width, axis=dim), axis, backward)
        block = jnp.concatenate([low, block, high], axis=dim)
    return block


def invert_block(stiffness_ref):
    identity = jnp.eye(12, dtype=jnp.float32)
    approx = identity / 5.0
    for turn_index in range(8):
        product = jnp.dot(
            stiffness_ref, approx, precision=highest, preferred_element_type=jnp.float32
        )
        approx = jnp.dot(
            approx, 2.0 * identity - product, precision=highest, preferred_element_type=jnp.float32
        )
    return approx


def relax(padded, shell_load, block_inverse, scale):
    east_side = padded[:, :, 1:-1, 2:]
    west_side = padded[:, :, 1:-1, :-2]
    north_side = padded[:, :, 2:, 1:-1]
    south_side = padded[:, :, :-2, 1:-1]
    sources = [
        shell_load[0] + coupling_weight * (west_side[1] + south_side[2]),
        shell_load[1] + coupling_weight * (east_side[0] + south_side[3]),
        shell_load[2] + coupling_weight * (west_side[3] + north_side[0]),
        shell_load[3] + coupling_weight * (east_side[2] + north_side[1]),
    ]
    outputs = []
    for row_index in range(12):
        total = block_inverse[row_index, 0] * sources[0][0]
        for col_index in range(1, 12):
            total = (
                total + block_inverse[row_index, col_index] * sources[col_index // 3][col_index % 3]
            )
        outputs.append(total / scale)
    return jnp.stack(outputs).reshape(
        padded.shape[0], padded.shape[1], padded.shape[2] - 2, padded.shape[3] - 2
    )


def project(transfer, traction):
    return jnp.einsum("nk,ckf->ncf", transfer, traction, precision=highest).reshape(12, -1)


def local(
    face_owner,
    face_element,
    element_state,
    lift,
    face_scale,
    transfer,
    stiffness_ref,
    element_scale,
    displacement_prev,
):
    groups = lax.axis_size("grp")
    members = lax.axis_size("dev")
    devices = groups * members
    faces_dev = face_owner.shape[0]
    capacity = 2 * faces_dev // devices
    slot_total = devices * capacity
    grid_rows, grid_cols = element_scale.shape
    traces = jnp.dot(lift, element_state, preferred_element_type=jnp.float32) * face_scale[None, :]
    owners = face_owner[:, 0]
    ordering = jnp.argsort(owners, stable=True)
    sorted_owner = owners[ordering]
    firsts = jnp.searchsorted(sorted_owner, sorted_owner, side="left")
    ranked = jnp.arange(faces_dev, dtype=jnp.int32) - firsts
    slot_index = (
        jnp.zeros((faces_dev,), jnp.int32).at[ordering].set(sorted_owner * capacity + ranked)
    )
    marker = (face_element + 1).astype(jnp.float32)[None, :]
    stacked = jnp.concatenate([traces, marker], axis=0)
    outgoing = jnp.zeros((stacked.shape[0], slot_total), jnp.float32).at[:, slot_index].set(stacked)
    received = lax.all_to_all(outgoing, ("grp", "dev"), split_axis=1, concat_axis=1, tiled=True)
    marker_row = received[-1].astype(jnp.int32) - 1
    live_slot = jnp.maximum(marker_row, 0)
    values = received[:-1]
    values = project(transfer, values.reshape(3, NODES_F, -1))
    shell_load = jnp.zeros((12, grid_rows * grid_cols), jnp.float32).at[:, live_slot].add(values)
    shell_load = shell_load.reshape(4, 3, grid_rows, grid_cols)
    block_inverse = invert_block(stiffness_ref)
    displacement = displacement_prev
    for turn_index in range(SWEEPS):
        padded = with_halo(displacement, (("grp", 2), ("dev", 3)), 1)
        displacement = relax(padded, shell_load, block_inverse, element_scale)
    returning = displacement.reshape(12, -1)[:, live_slot]
    returned = lax.all_to_all(returning, ("grp", "dev"), split_axis=1, concat_axis=1, tiled=True)
    node_disp = returned[:, slot_index].reshape(4, 3, -1)
    face_displacement = jnp.einsum("nk,ncf->ckf", transfer, node_disp, precision=highest)
    return (displacement, face_displacement)


def solution(mesh):
    placed = (
        P(("grp", "dev"), None),
        P(("grp", "dev")),
        P(None, ("grp", "dev")),
        P(),
        P(("grp", "dev")),
        P(),
        P(),
        P("grp", "dev"),
        P(None, None, "grp", "dev"),
    )
    return jax.shard_map(
        local,
        mesh=mesh,
        in_specs=placed,
        out_specs=(P(None, None, "grp", "dev"), P(None, None, ("grp", "dev"))),
        check_vma=False,
    )
```

profile of v0, /device:TPU:1, one launch (start us, length us, event | category | flops | bytes accessed | tf_op | source)
XLA Modules:
  0.0 1556.5 jit_solution(4349303651045862482)
XLA Ops:
  7.3 23.0 %gather_fusion.1 = s32[4096]{0:T(1024)S(1)} fusion(s32[4096]{0:T(1024)S(1)} %bitcast.975, s32[4096]{0:T(1024)S(1)} %get-tuple-element.196), kind=kCustom, calls=%fused_computation.1 | custom fusion | bytes 49152 | tf_op jit(solution)/shard_map/gather | solution.py:89
  30.3 300.6 %while.25 = (s32[]{:T(128)}, u32[4096]{0:T(1024)S(1)}, u32[4096]{0:T(1024)S(1)}, s32[4096]{0:T(1024)S(1)}, s32[]{:T(128)}, /*index=5*/s32[]{:T(128)}, s32[]{}) while((s32[]{:T(128)}, u32[4096]{0:T(1024)S(1)}, u32[4096]{0:T(1024)S(1)}, s32[4096]{0:T(1024)S(1)}, s32[]{:T(128)}, /*index=5*/s32[]{:T(128)}, s32[]{}) %tuple.228), condition=%wide.region_2.3_spmd.clone, body=%wide.region_1.2_spmd.clone.sunk | while | flops 77828 | bytes 270445 | solution.py:90
  30.4 23.0 %gather_fusion = s32[4096]{0:T(1024)S(1)} fusion(s32[4096]{0:T(1024)S(1)} %get-tuple-element.388, u32[4096]{0:T(1024)S(1)} %broadcast_clamp_fusion.5), kind=kCustom, calls=%fused_computation.clone.clone.1 | custom fusion | bytes 49152 | tf_op jit(solution)/shard_map/jit(searchsorted)/jit(_searchsorted_scan_impl)/vmap(jit(_searchsorted_scan_impl))/while/body/eval_jaxpr/gather | solution.py:90
  53.5 23.0 %gather_fusion = s32[4096]{0:T(1024)S(1)} fusion(s32[4096]{0:T(1024)S(1)} %get-tuple-element.388, u32[4096]{0:T(1024)S(1)} %broadcast_clamp_fusion.5), kind=kCustom, calls=%fused_computation.clone.clone.1 | custom fusion | bytes 49152 | tf_op jit(solution)/shard_map/jit(searchsorted)/jit(_searchsorted_scan_impl)/vmap(jit(_searchsorted_scan_impl))/while/body/eval_jaxpr/gather | solution.py:90
  76.6 23.0 %gather_fusion = s32[4096]{0:T(1024)S(1)} fusion(s32[4096]{0:T(1024)S(1)} %get-tuple-element.388, u32[4096]{0:T(1024)S(1)} %broadcast_clamp_fusion.5), kind=kCustom, calls=%fused_computation.clone.clone.1 | custom fusion | bytes 49152 | tf_op jit(solution)/shard_map/jit(searchsorted)/jit(_searchsorted_scan_impl)/vmap(jit(_searchsorted_scan_impl))/while/body/eval_jaxpr/gather | solution.py:90
  99.8 23.0 %gather_fusion = s32[4096]{0:T(1024)S(1)} fusion(s32[4096]{0:T(1024)S(1)} %get-tuple-element.388, u32[4096]{0:T(1024)S(1)} %broadcast_clamp_fusion.5), kind=kCustom, calls=%fused_computation.clone.clone.1 | custom fusion | bytes 49152 | tf_op jit(solution)/shard_map/jit(searchsorted)/jit(_searchsorted_scan_impl)/vmap(jit(_searchsorted_scan_impl))/while/body/eval_jaxpr/gather | solution.py:90
  122.9 23.0 %gather_fusion = s32[4096]{0:T(1024)S(1)} fusion(s32[4096]{0:T(1024)S(1)} %get-tuple-element.388, u32[4096]{0:T(1024)S(1)} %broadcast_clamp_fusion.5), kind=kCustom, calls=%fused_computation.clone.clone.1 | custom fusion | bytes 49152 | tf_op jit(solution)/shard_map/jit(searchsorted)/jit(_searchsorted_scan_impl)/vmap(jit(_searchsorted_scan_impl))/while/body/eval_jaxpr/gather | solution.py:90
  146.0 23.0 %gather_fusion = s32[4096]{0:T(1024)S(1)} fusion(s32[4096]{0:T(1024)S(1)} %get-tuple-element.388, u32[4096]{0:T(1024)S(1)} %broadcast_clamp_fusion.5), kind=kCustom, calls=%fused_computation.clone.clone.1 | custom fusion | bytes 49152 | tf_op jit(solution)/shard_map/jit(searchsorted)/jit(_searchsorted_scan_impl)/vmap(jit(_searchsorted_scan_impl))/while/body/eval_jaxpr/gather | solution.py:90
  169.1 23.0 %gather_fusion = s32[4096]{0:T(1024)S(1)} fusion(s32[4096]{0:T(1024)S(1)} %get-tuple-element.388, u32[4096]{0:T(1024)S(1)} %broadcast_clamp_fusion.5), kind=kCustom, calls=%fused_computation.clone.clone.1 | custom fusion | bytes 49152 | tf_op jit(solution)/shard_map/jit(searchsorted)/jit(_searchsorted_scan_impl)/vmap(jit(_searchsorted_scan_impl))/while/body/eval_jaxpr/gather | solution.py:90
  192.3 23.0 %gather_fusion = s32[4096]{0:T(1024)S(1)} fusion(s32[4096]{0:T(1024)S(1)} %get-tuple-element.388, u32[4096]{0:T(1024)S(1)} %broadcast_clamp_fusion.5), kind=kCustom, calls=%fused_computation.clone.clone.1 | custom fusion | bytes 49152 | tf_op jit(solution)/shard_map/jit(searchsorted)/jit(_searchsorted_scan_impl)/vmap(jit(_searchsorted_scan_impl))/while/body/eval_jaxpr/gather | solution.py:90
  215.4 23.0 %gather_fusion = s32[4096]{0:T(1024)S(1)} fusion(s32[4096]{0:T(1024)S(1)} %get-tuple-element.388, u32[4096]{0:T(1024)S(1)} %broadcast_clamp_fusion.5), kind=kCustom, calls=%fused_computation.clone.clone.1 | custom fusion | bytes 49152 | tf_op jit(solution)/shard_map/jit(searchsorted)/jit(_searchsorted_scan_impl)/vmap(jit(_searchsorted_scan_impl))/while/body/eval_jaxpr/gather | solution.py:90
  238.5 23.0 %gather_fusion = s32[4096]{0:T(1024)S(1)} fusion(s32[4096]{0:T(1024)S(1)} %get-tuple-element.388, u32[4096]{0:T(1024)S(1)} %broadcast_clamp_fusion.5), kind=kCustom, calls=%fused_computation.clone.clone.1 | custom fusion | bytes 49152 | tf_op jit(solution)/shard_map/jit(searchsorted)/jit(_searchsorted_scan_impl)/vmap(jit(_searchsorted_scan_impl))/while/body/eval_jaxpr/gather | solution.py:90
  261.6 23.0 %gather_fusion = s32[4096]{0:T(1024)S(1)} fusion(s32[4096]{0:T(1024)S(1)} %get-tuple-element.388, u32[4096]{0:T(1024)S(1)} %broadcast_clamp_fusion.5), kind=kCustom, calls=%fused_computation.clone.clone.1 | custom fusion | bytes 49152 | tf_op jit(solution)/shard_map/jit(searchsorted)/jit(_searchsorted_scan_impl)/vmap(jit(_searchsorted_scan_impl))/while/body/eval_jaxpr/gather | solution.py:90
  284.8 23.0 %gather_fusion = s32[4096]{0:T(1024)S(1)} fusion(s32[4096]{0:T(1024)S(1)} %get-tuple-element.388, u32[4096]{0:T(1024)S(1)} %broadcast_clamp_fusion.5), kind=kCustom, calls=%fused_computation.clone.clone.1 | custom fusion | bytes 49152 | tf_op jit(solution)/shard_map/jit(searchsorted)/jit(_searchsorted_scan_impl)/vmap(jit(_searchsorted_scan_impl))/while/body/eval_jaxpr/gather | solution.py:90
  307.9 23.0 %gather_fusion = s32[4096]{0:T(1024)S(1)} fusion(s32[4096]{0:T(1024)S(1)} %get-tuple-element.388, u32[4096]{0:T(1024)S(1)} %broadcast_clamp_fusion.5), kind=kCustom, calls=%fused_computation.clone.clone.1 | custom fusion | bytes 49152 | tf_op jit(solution)/shard_map/jit(searchsorted)/jit(_searchsorted_scan_impl)/vmap(jit(_searchsorted_scan_impl))/while/body/eval_jaxpr/gather | solution.py:90
  331.0 15.5 scatter_custom_fusion
  348.1 12.8 scatter_custom_fusion.1
  368.7 11.5 all-to-all-start
  426.5 53.4 %scatter_custom_fusion.2 = f32[12,16384]{0,1:T(8,128)} fusion(s32[8192]{0:T(1024)S(1)} %reshape.3233, f32[8192,12]{1,0:T(8,128)} %copy.102, f32[]{:T(128)} %constant.50.clone.1), kind=kCustom, calls=%fused_computation.14 | custom fusion | flops 98304 | bytes 786944 | tf_op jit(solution)/shard_map/scatter-add | solution.py:103
  480.0 28.1 %fusion.142 = (f32[3,16384]{0,1:T(8,128)}, f32[3,16384]{0,1:T(8,128)}, f32[3,16384]{0,1:T(8,128)}, f32[3,16384]{0,1:T(8,128)}) fusion(f32[12,16384]{0,1:T(8,128)} %scatter_custom_fusion.2), kind=kLoop, calls=%fused_computation.455 | loop fusion | bytes 1572864 | tf_op jit(solution)/shard_map/slice | solution.py:46
  646.8 8.1 constant_dynamic-update-slice_fusion.24
  662.9 8.2 constant_dynamic-update-slice_fusion.22
  671.1 8.2 constant_dynamic-update-slice_fusion.21
  679.4 8.2 constant_dynamic-update-slice_fusion.20
  703.8 8.1 constant_dynamic-update-slice_fusion.17
  711.9 8.2 constant_dynamic-update-slice_fusion.16
  736.2 8.2 constant_dynamic-update-slice_fusion.13
  769.3 8.1 constant_dynamic-update-slice_fusion.36
  785.4 8.2 constant_dynamic-update-slice_fusion.34
  793.6 8.2 constant_dynamic-update-slice_fusion.33
  801.9 8.2 constant_dynamic-update-slice_fusion.32
  826.3 8.1 constant_dynamic-update-slice_fusion.29
  834.4 8.2 constant_dynamic-update-slice_fusion.28
  858.7 8.2 constant_dynamic-update-slice_fusion.25
  889.8 8.1 constant_dynamic-update-slice_fusion.48
  905.9 8.2 constant_dynamic-update-slice_fusion.46
  914.1 8.2 constant_dynamic-update-slice_fusion.45
  922.4 8.2 constant_dynamic-update-slice_fusion.44
  946.8 8.1 constant_dynamic-update-slice_fusion.41
  954.9 8.2 constant_dynamic-update-slice_fusion.40
  979.2 8.2 constant_dynamic-update-slice_fusion.37
  1010.3 8.1 constant_dynamic-update-slice_fusion.60
  1026.5 8.2 constant_dynamic-update-slice_fusion.58
  1034.7 8.2 constant_dynamic-update-slice_fusion.57
  1042.9 8.2 constant_dynamic-update-slice_fusion.56
  1067.3 8.1 constant_dynamic-update-slice_fusion.53
  1075.4 8.2 constant_dynamic-update-slice_fusion.52
  1099.8 8.2 constant_dynamic-update-slice_fusion.49
  1130.8 8.1 constant_dynamic-update-slice_fusion.72
  1147.0 8.2 constant_dynamic-update-slice_fusion.70
  1155.2 8.2 constant_dynamic-update-slice_fusion.69
  1163.4 8.2 constant_dynamic-update-slice_fusion.68
  1187.8 8.1 constant_dynamic-update-slice_fusion.65
  1195.9 8.2 constant_dynamic-update-slice_fusion.64
  1220.3 8.2 constant_dynamic-update-slice_fusion.61
  1251.3 8.1 constant_dynamic-update-slice_fusion.84
  1267.5 8.2 constant_dynamic-update-slice_fusion.82
  1275.7 8.2 constant_dynamic-update-slice_fusion.81
  1283.9 8.2 constant_dynamic-update-slice_fusion.80
  1316.4 8.2 constant_dynamic-update-slice_fusion.76
  1340.8 8.2 constant_dynamic-update-slice_fusion.73
  1467.8 31.1 %gather_fusion.2 = f32[8192,12]{1,0:T(8,128)} fusion(f32[12,16384]{0,1:T(8,128)} %copy.135, s32[8192]{0:T(1024)S(1)} %broadcast_clamp_fusion.1), kind=kCustom, calls=%fused_computation.2 | custom fusion | bytes 819200 | tf_op jit(solution)/shard_map/gather | solution.py:110
  1502.4 33.3 %all_to_all.21 = f32[128,1,768]{2,1,0:T(1,128)S(1)} all-to-all(f32[128,1,768]{2,1,0:T(1,128)S(1)} %reshape.3649), channel_id=1, replica_groups=mesh['grp'=4,'dev'=32] {'grp','dev'}, dimensions={0} | all-to-all | bytes 786432 | tf_op jit(solution)/shard_map/all_to_all | solution.py:111
  1540.3 13.0 gather_fusion.3
  (324 shorter events, 696.9 us)
Async XLA Ops:
  0.6 346.5 %copy-start = (bf16[110,4096]{1,0:T(8,128)(2,1)S(1)}, bf16[110,4096]{1,0:T(8,128)(2,1)}, u32[]{:S(2)}) copy-start(bf16[110,4096]{1,0:T(8,128)(2,1)} %param.13) | copy-start | bytes 2703364
  0.6 6.6 copy-start.2
  30.3 316.8 %copy-start.13 = (s32[4096]{0:T(1024)S(1)}, s32[4096]{0:T(1024)}, u32[]{:S(2)}) copy-start(s32[4096]{0:T(1024)} %param.12) | copy-start | bytes 49156
  30.3 316.8 %copy-start.12 = (f32[4096]{0:T(1024)S(1)}, f32[4096]{0:T(1024)}, u32[]{:S(2)}) copy-start(f32[4096]{0:T(1024)} %param.15) | copy-start | bytes 49156
  30.3 316.8 %copy-start.14 = (bf16[30,110]{1,0:T(8,128)(2,1)S(1)}, bf16[30,110]{1,0:T(8,128)(2,1)}, u32[]{:S(2)}) copy-start(bf16[30,110]{1,0:T(8,128)(2,1)} %param.14) | copy-start | bytes 19804
  364.9 15.3 copy-start.4
  364.9 20.6 %copy-start.8 = (f32[12,12]{1,0:T(8,128)S(1)}, f32[12,12]{1,0:T(8,128)}, u32[]{:S(2)}) copy-start(f32[12,12]{1,0:T(8,128)} %param.17) | copy-start | bytes 1732
  368.7 35.8 %all-to-all-start = ((f32[128,1,1984]{2,1,0:T(1,128)}), f32[128,1,1984]{2,1,0:T(1,128)S(1)}, u32[]{:S(2)}, u32[]{:S(2)}) async-start(f32[128,1,1984]{2,1,0:T(1,128)} %reshape.3647), calls=%async_computation | async-start | bytes 2097152 | tf_op jit(solution)/shard_map/all_to_all | solution.py:98
  380.2 14.9 collective-permute-start.1
  381.5 13.6 collective-permute-start
  395.1 118.2 %copy-start.9 = (f32[4,3,1,256]{3,2,1,0:T(1,128)}, f32[4,3,1,256]{3,2,1,0:T(1,128)S(1)}, u32[]{:S(2)}) copy-start(f32[4,3,1,256]{3,2,1,0:T(1,128)S(1)} %collective-permute-done) | copy-start | bytes 36868
  396.3 117.0 %collective-permute-start.2 = (f32[4,3,66,1]{3,2,1,0:T(8,128)}, f32[4,3,66,1]{3,2,1,0:T(8,128)}, u32[]{:S(2)}, u32[]{:S(2)}) collective-permute-start(f32[4,3,66,1]{3,2,1,0:T(8,128)} %get-tuple-element.176), channel_id=1, source_target_pairs={{0,1},{1,2},{2,3},{3,4},{4,5},{5,6},{6,7},{7,8},{8,9},{9,10},{10,1... | collective-permute-start | bytes 9512 | tf_op jit(solution)/shard_map/ppermute | solution.py:19
  400.4 129.7 %collective-permute-start.3 = (f32[4,3,66,1]{3,2,1,0:T(8,128)}, f32[4,3,66,1]{3,2,1,0:T(8,128)}, u32[]{:S(2)}, u32[]{:S(2)}) collective-permute-start(f32[4,3,66,1]{3,2,1,0:T(8,128)} %get-tuple-element.177), channel_id=1, source_target_pairs={{1,0},{2,1},{3,2},{4,3},{5,4},{6,5},{7,6},{8,7},{9,8},{10,9},{11,1... | collective-permute-start | bytes 9512 | tf_op jit(solution)/shard_map/ppermute | solution.py:22
  404.4 1.0 copy-start.7
  412.4 8.4 copy-start.15
  524.8 5.3 copy-start.10
  524.8 6.8 copy-start.3
  621.8 0.9 copy-start.5
  623.6 4.6 collective-permute-start.4
  626.9 4.4 collective-permute-start.5
  632.8 11.1 collective-permute-start.7
  634.7 10.7 collective-permute-start.6
  745.4 4.9 collective-permute-start.8
  749.0 4.4 collective-permute-start.9
  754.9 11.5 collective-permute-start.11
  756.8 11.0 collective-permute-start.10
  867.9 3.0 collective-permute-start.12
  869.5 4.4 collective-permute-start.13
  875.4 11.5 collective-permute-start.15
  877.3 11.0 collective-permute-start.14
  988.4 3.0 collective-permute-start.16
  990.0 4.4 collective-permute-start.17
  995.9 11.5 collective-permute-start.19
  997.8 11.0 collective-permute-start.18
  1108.9 3.0 collective-permute-start.20
  1110.5 4.4 collective-permute-start.21
  1116.4 11.5 collective-permute-start.23
  1118.3 11.0 collective-permute-start.22
  1229.4 3.0 collective-permute-start.24
  1231.0 4.4 collective-permute-start.25
  1236.9 11.5 collective-permute-start.27
  1238.8 11.0 collective-permute-start.26
  1348.9 21.5 %copy-start.6 = (f32[12,64,256]{2,1,0:T(8,128)S(1)}, f32[12,64,256]{2,1,0:T(8,128)}, u32[]{:S(2)}) copy-start(f32[12,64,256]{2,1,0:T(8,128)} %constant_dynamic-update-slice_fusion.73) | copy-start | bytes 2359300
  1350.0 3.0 collective-permute-start.28
  1351.6 4.4 collective-permute-start.29
  1357.5 11.5 collective-permute-start.31
  1359.4 11.0 collective-permute-start.30
  1460.8 6.9 copy-start.16
  1502.4 37.9 %copy-start.11 = (s32[4096]{0:T(1024)S(1)}, s32[4096]{0:T(1024)}, u32[]{:S(2)}) copy-start(s32[4096]{0:T(1024)} %get-tuple-element.194) | copy-start | bytes 49156
  1537.5 18.6 %copy-start.1 = (bf16[110,4096]{1,0:T(8,128)(2,1)S(1)}, bf16[110,4096]{1,0:T(8,128)(2,1)}, u32[]{:S(2)}) copy-start(bf16[110,4096]{1,0:T(8,128)(2,1)} %param.13) | copy-start | bytes 2703364
where the time goes:
time: 1580 us; the launch traced here: 1560 us
  other arithmetic  864 us (55%)
  local copies, waits for them, and re-layouts  500 us (32%)
  starting transfers between devices  99.6 us (6%)
  waiting for transfers between devices  49.8 us (3%)
  blocking collectives  33.3 us (2%)
    unnamed x90, other arithmetic  702 us
    gather x13, local copies, waits for them, and re-layouts, local(): firsts = jnp.searchsorted(sorted_owner, sorted_owner, side='left')  299 us
    another operation x8, other arithmetic, relax(): jnp.stack(outputs)  64.2 us
    ppermute x16, starting transfers between devices, with_halo(): lax.ppermute(lax.slice_in_dim(block, block.shape[dim] - width, None, axis...  62 us
    scatter-add x1, other arithmetic, local(): jnp.zeros((12, grid_rows * grid_cols), jnp.float32).at[:, live_slot]  53.4 us
    ppermute x16, waiting for transfers between devices, with_halo(): lax.ppermute(lax.slice_in_dim(block, 0, width, axis=dim), axis, backward)  49.7 us
    all_to_all x1, blocking collectives, local(): lax.all_to_all(returning, ('grp', 'dev'), split_axis=1, concat_axis=1, ti...  33.3 us
  transfers between devices with their start and end apart: 33, of which 14 were waited for; matrix products, arithmetic and copies ran while one was open for 9% of the time, Pallas kernels for 0%

commit v1 on v0

v1 whole, which is shorter than its diff:
```python
import functools

import jax
import jax.numpy as jnp
from jax import lax
from jax.experimental import pallas as pl
from jax.experimental.pallas import tpu as pltpu
from jax.sharding import PartitionSpec as P

SWEEPS = 8
WEIGHT = 2.2
HIGHEST = lax.Precision.HIGHEST
F32 = jnp.float32
BF16 = jnp.bfloat16
I32 = jnp.int32

OWNERS = 128
CAP = 64
COLS = 256
ROWS = 64
PAD_R = 80
PAD_C = 384
FACES = 4096
CHUNK = 256
NT = (((1,), (1,)), ((), ()))


def iota(shape, dim):
    return lax.broadcasted_iota(I32, shape, dim)


def dot(a, b):
    return jnp.dot(a, b, preferred_element_type=F32)


def dot_nt(a, b):
    return lax.dot_general(a, b, NT, preferred_element_type=F32)


def exact(a, b):
    return jnp.dot(a, b, precision=HIGHEST, preferred_element_type=F32)


def one_hot(flag):
    return flag.astype(F32).astype(BF16)


def split(x):
    high = x.astype(BF16)
    return high, (x - high.astype(F32)).astype(BF16)


def face_kernel(owner_ref, elem_ref, state_ref, scale_ref, lift_ref, transfer_ref, msg_ref, rank_ref, x_ref, acc_ref):
    by_node = exact((iota((12, 4), 0) // 3 == iota((12, 4), 1)).astype(F32), transfer_ref[...])
    spread = exact(by_node, (iota((10, 30), 1) % 10 == iota((10, 30), 0)).astype(F32))
    spread = jnp.where(iota((12, 30), 0) % 3 == iota((12, 30), 1) // 10, spread, 0.0)
    weights = exact(spread, lift_ref[...].astype(F32))
    high, low = split(weights)
    x_ref[...] = jnp.zeros_like(x_ref)
    acc_ref[...] = jnp.zeros_like(acc_ref)
    before = iota((CHUNK, 2 * CHUNK), 0)
    upper = iota((CHUNK, 2 * CHUNK), 1)
    upper = one_hot((before < upper) | (upper >= CHUNK))

    def body(i, base):
        part = pl.ds(pl.multiple_of(i * CHUNK, CHUNK), CHUNK)
        hot = (iota((OWNERS, CHUNK), 0) == owner_ref[:, part]).astype(F32)
        hot16 = hot.astype(BF16)
        counts = dot(hot16, upper)
        rank = jnp.sum(hot * (counts[:, :CHUNK] + base), axis=0, keepdims=True)
        rank_ref[:, part] = rank
        place = one_hot(iota((CAP, CHUNK), 0).astype(F32) == rank)
        state = state_ref[:, part]
        load = (dot(high, state) + dot(low, state)) * scale_ref[:, part]
        marker = (elem_ref[:, part] + 1).astype(F32)
        for c in range(13):
            row = load[c:c + 1] if c < 12 else marker
            top, rest = split(jnp.broadcast_to(row, (16, CHUNK)))
            for k in range(CAP // 16):
                at = c * CAP + 16 * k
                x_ref[at:at + 16, :CHUNK] = place[16 * k:16 * k + 16] * top
                x_ref[at:at + 16, CHUNK:] = place[16 * k:16 * k + 16] * rest
        acc_ref[...] += dot_nt(jnp.concatenate([hot16, hot16], axis=1), x_ref[...])
        return base + counts[:, CHUNK:]

    lax.fori_loop(0, FACES // CHUNK, body, jnp.zeros((OWNERS, CHUNK), F32))
    for j in range(7):
        msg_ref[:, j, :] = acc_ref[:, 128 * j:128 * j + 128]
    msg_ref[:, 7, :] = jnp.zeros((OWNERS, 128), F32)


def pair_up(a, b):
    first = iota((8, 128), 1) < 64
    even = jnp.where(first, a, pltpu.roll(b, 64, 1))
    odd = jnp.where(first, pltpu.roll(a, 64, 1), b)
    return even, odd


def element_of(marker):
    element = marker.astype(I32) - 1
    return element >> 8, element & 255


def edge_sends(comps, west_ref, east_ref):
    lane = iota((ROWS, 128), 1)
    west = jnp.zeros((ROWS, 128), F32)
    east = jnp.zeros((ROWS, 128), F32)
    for i, comp in enumerate(comps):
        here = lane // 8 == i
        low = comp(0)
        high = comp(128)
        west = jnp.where(here, pltpu.roll(low, 8 * i, 1) if i else low, west)
        east = jnp.where(here, pltpu.roll(high, (8 * i + 8) % 128, 1), east)
    west_ref[...] = west
    east_ref[...] = east


PAIRS = 4


def scatter_kernel(msg_ref, load_ref, west_ref, east_ref, a_ref, col_ref, acc_ref):
    acc_ref[...] = jnp.zeros_like(acc_ref)

    def body(i, carry):
        for q in range(PAIRS):
            even, odd = pair_up(msg_ref[2 * (i * PAIRS + q)], msg_ref[2 * (i * PAIRS + q) + 1])
            row, col = element_of(even[6:7])
            row_hot = one_hot(iota((ROWS, 128), 0) == row)
            col_hot = one_hot(iota((COLS, 128), 0) == col)
            lanes = 256 * q
            col_ref[:, lanes:lanes + 128] = col_hot
            col_ref[:, lanes + 128:lanes + 256] = col_hot
            for c in range(12):
                value = (odd if c % 2 else even)[c // 2:c // 2 + 1] * (1.0 / WEIGHT)
                top, rest = split(jnp.broadcast_to(value, (16, 128)))
                for k in range(ROWS // 16):
                    at = c * ROWS + 16 * k
                    a_ref[at:at + 16, lanes:lanes + 128] = row_hot[16 * k:16 * k + 16] * top
                    a_ref[at:at + 16, lanes + 128:lanes + 256] = row_hot[16 * k:16 * k + 16] * rest
        acc_ref[...] += dot_nt(a_ref[...], col_ref[...])
        return carry

    lax.fori_loop(0, OWNERS // 2 // PAIRS, body, 0)
    for c in range(12):
        load_ref[c] = acc_ref[c * ROWS:(c + 1) * ROWS]
    edge_sends(
        [(lambda lane, c=c: acc_ref[c * ROWS:(c + 1) * ROWS, lane:lane + 128]) for c in range(12)],
        west_ref, east_ref,
    )


def edge_kernel(prev_ref, scale_ref, stiff_ref, west_ref, east_ref, mat_ref):
    comps = [(lambda lane, c=c: prev_ref[c, :, lane:lane + 128]) for c in range(12)]
    comps.append(lambda lane: scale_ref[:, lane:lane + 128])
    edge_sends(comps, west_ref, east_ref)
    eye = (iota((12, 12), 0) == iota((12, 12), 1)).astype(F32)
    approx = eye / 5.0
    rest = eye - exact(stiff_ref[...], approx)
    for turn in range(8):
        approx = approx + exact(approx, rest)
        if turn < 7:
            rest = exact(rest, rest)
    tall = (iota((192, 12), 0) // 16 == iota((192, 12), 1)).astype(F32)
    wide = (iota((12, 192), 1) // 16 == iota((12, 192), 0)).astype(F32)
    big = exact(exact(tall, approx * WEIGHT), wide)
    big = jnp.where(iota((192, 192), 0) % 16 == iota((192, 192), 1) % 16, big, 0.0)
    high, low = split(big)
    mat_ref[0] = high
    mat_ref[1] = low


def rows_kernel(count, refs):
    cores, (from_east_ref, from_west_ref, side_ref, north_ref, south_ref) = refs[:count], refs[count:]
    at = 0
    lane = iota((ROWS, 128), 1)
    dev = lax.axis_index("dev")
    from_east = jnp.where(dev < lax.axis_size("dev") - 1, from_east_ref[...], 0.0)
    from_west = jnp.where(dev > 0, from_west_ref[...], 0.0)
    for core in cores:
        planes = core.shape[0] if len(core.shape) == 3 else 1
        for c in range(planes):
            view = core.at[c] if len(core.shape) == 3 else core
            low = pltpu.roll(from_east, (128 - 8 * at) % 128, 1) if at else from_east
            high = pltpu.roll(from_west, (120 - 8 * at) % 128, 1)
            side = jnp.where(lane < 8, low, jnp.where(lane >= 120, high, 0.0))
            side_ref[at] = side
            north_ref[at, :, :COLS] = view[0:8, :]
            north_ref[at, :, COLS:] = side[0:8]
            south_ref[at, :, :COLS] = view[ROWS - 8:ROWS, :]
            south_ref[at, :, COLS:] = side[ROWS - 8:ROWS]
            at += 1


def sweep_kernel(prev_ref, scale_ref, prev_side_ref, prev_south_ref, prev_north_ref,
                 load_ref, load_side_ref, load_south_ref, load_north_ref, mat_ref, msg_ref,
                 out_ref, ret_ref, u_ref, f_ref, inv_ref, x_ref, hl_ref):
    for dst, core, side, south, north in (
        (u_ref, prev_ref, prev_side_ref, prev_south_ref, prev_north_ref),
        (f_ref, load_ref, load_side_ref, load_south_ref, load_north_ref),
    ):
        dst[:, 0:ROWS, 0:COLS] = core[...]
        dst[:, 0:ROWS, COLS:PAD_C] = side[0:12]
        dst[:, ROWS:ROWS + 8, :] = south[0:12]
        dst[:, ROWS + 8:PAD_R, :] = north[0:12]
    inv_ref[0:ROWS, 0:COLS] = scale_ref[...]
    inv_ref[0:ROWS, COLS:PAD_C] = prev_side_ref[12]
    inv_ref[ROWS:ROWS + 8, :] = prev_south_ref[12]
    inv_ref[ROWS + 8:PAD_R, :] = prev_north_ref[12]
    grp, dev = lax.axis_index("grp"), lax.axis_index("dev")
    row, col = iota((PAD_R, PAD_C), 0), iota((PAD_R, PAD_C), 1)
    row_ok = (row < ROWS) | ((row < ROWS + 8) & (grp < lax.axis_size("grp") - 1)) | ((row >= ROWS + 8) & (grp > 0))
    col_ok = (col < COLS) | ((col < COLS + 8) & (dev < lax.axis_size("dev") - 1)) | ((col >= PAD_C - 8) & (dev > 0))
    ok = row_ok & col_ok
    inv_ref[...] = jnp.where(ok, 1.0 / jnp.where(ok, inv_ref[...], 1.0), 0.0)
    for c in range(12):
        u_ref[c] = jnp.where(ok, u_ref[c], 0.0)
    along = ((1, 1), (0, PAD_C - 1), (3, 1), (2, PAD_C - 1))
    across = ((2, 1), (3, 1), (0, PAD_R - 1), (1, PAD_R - 1))

    def sweep(turn, carry):
        for n in range(4):
            for c in range(3):
                at = 3 * n + c
                right = (
                    f_ref[at]
                    + pltpu.roll(u_ref[3 * along[n][0] + c], along[n][1], 1)
                    + pltpu.roll(u_ref[3 * across[n][0] + c], across[n][1], 0)
                )
                top, rest = split(right)
                for b in range(PAD_R // 16):
                    x_ref[b, 16 * at:16 * at + 16] = top[16 * b:16 * b + 16]
                    x_ref[b, 192 + 16 * at:192 + 16 * at + 16] = rest[16 * b:16 * b + 16]
        high = mat_ref[0]
        both = jnp.concatenate([high, high], axis=1)
        for b in range(PAD_R // 16):
            solved = dot(both, x_ref[b]) + dot(mat_ref[1], x_ref[b, 0:192])
            factor = inv_ref[16 * b:16 * b + 16]
            for at in range(12):
                u_ref[at, 16 * b:16 * b + 16] = solved[16 * at:16 * at + 16] * factor
        return carry

    lax.fori_loop(0, SWEEPS, sweep, 0)
    for c in range(12):
        value = u_ref[c, 0:ROWS, 0:COLS]
        out_ref[c] = value
        top, rest = split(value)
        hl_ref[c * ROWS:(c + 1) * ROWS, :COLS] = top
        hl_ref[c * ROWS:(c + 1) * ROWS, COLS:] = rest
    first = iota((8, 128), 1) < 64

    def gather(i, carry):
        markers = []
        for q in range(2):
            even, _ = pair_up(msg_ref[4 * i + 2 * q], msg_ref[4 * i + 2 * q + 1])
            markers.append(even[6:7])
        row, col = element_of(jnp.concatenate(markers, axis=1))
        col_hot = one_hot(iota((COLS, 256), 0) == col)
        row_hot = iota((ROWS, 256), 0) == row
        found = dot(hl_ref[...], jnp.concatenate([col_hot, col_hot], axis=0))
        values = [
            jnp.sum(jnp.where(row_hot, found[c * ROWS:(c + 1) * ROWS], 0.0), axis=0, keepdims=True)
            for c in range(12)
        ]
        for q in range(2):
            lanes = slice(128 * q, 128 * q + 128)
            blank = jnp.zeros((2, 128), F32)
            even = jnp.concatenate([values[c][:, lanes] for c in range(0, 12, 2)] + [blank], axis=0)
            odd = jnp.concatenate([values[c][:, lanes] for c in range(1, 12, 2)] + [blank], axis=0)
            ret_ref[4 * i + 2 * q] = jnp.where(first, even, pltpu.roll(odd, 64, 1))
            ret_ref[4 * i + 2 * q + 1] = jnp.where(first, pltpu.roll(even, 64, 1), odd)
        return carry

    lax.fori_loop(0, OWNERS // 4, gather, 0)


def return_kernel(ret_ref, owner_ref, rank_ref, transfer_ref, out_ref, l_ref):
    for j in range(6):
        top, rest = split(jnp.transpose(ret_ref[:, j, :]))
        l_ref[128 * j:128 * j + 128, :128] = top
        l_ref[128 * j:128 * j + 128, 128:] = rest
    pick = (iota((48, 10), 0) % 16 == iota((48, 10), 1)).astype(F32)
    spread = lax.dot_general(pick, transfer_ref[...], NT, precision=HIGHEST, preferred_element_type=F32)
    spread = exact(spread, (iota((4, 12), 1) // 3 == iota((4, 12), 0)).astype(F32))
    spread = jnp.where(iota((48, 12), 0) // 16 == iota((48, 12), 1) % 3, spread, 0.0)

    def body(i, carry):
        part = pl.ds(pl.multiple_of(i * CHUNK, CHUNK), CHUNK)
        hot = one_hot(iota((OWNERS, CHUNK), 0) == owner_ref[:, part])
        place = iota((CAP, CHUNK), 0).astype(F32) == rank_ref[:, part]
        found = dot(l_ref[...], jnp.concatenate([hot, hot], axis=0))
        node = jnp.concatenate(
            [
                jnp.sum(jnp.where(place, found[c * CAP:(c + 1) * CAP], 0.0), axis=0, keepdims=True)
                for c in range(12)
            ],
            axis=0,
        )
        result = exact(spread, node)
        for c in range(3):
            out_ref[c, :, part] = result[16 * c:16 * c + 10]
        return carry

    lax.fori_loop(0, FACES // CHUNK, body, 0)


def call(kernel, outs, scratch, *args):
    single = not isinstance(outs, (list, tuple))
    shapes = [outs] if single else list(outs)
    result = pl.pallas_call(
        kernel,
        out_shape=shapes,
        in_specs=[pl.BlockSpec(memory_space=pltpu.VMEM)] * len(args),
        out_specs=[pl.BlockSpec(memory_space=pltpu.VMEM)] * len(shapes),
        scratch_shapes=scratch,
        compiler_params=pltpu.CompilerParams(vmem_limit_bytes=48 * 1024 * 1024),
    )(*args)
    return result[0] if single else result


def arr(*shape, dtype=F32):
    return jax.ShapeDtypeStruct(shape, dtype)


def ring(axis, step):
    count = lax.axis_size(axis)
    return [(i, (i + step) % count) for i in range(count)]


def shift_pair(toward_low, toward_high, axis):
    return lax.ppermute(toward_low, axis, ring(axis, -1)), lax.ppermute(toward_high, axis, ring(axis, 1))


def rows_call(count, cores, from_east, from_west):
    def kernel(*refs):
        rows_kernel(len(cores), refs)

    return call(
        kernel, [arr(count, ROWS, 128), arr(count, 8, PAD_C), arr(count, 8, PAD_C)], [], *cores, from_east, from_west
    )


def local(face_owner, face_element, element_state, lift, face_scale, transfer, stiffness_ref, element_scale, displacement_prev):
    owner = face_owner.reshape(1, FACES)
    element = face_element.reshape(1, FACES)
    scale = face_scale.reshape(1, FACES)
    prev = displacement_prev.reshape(12, ROWS, COLS)

    msg, rank = call(
        face_kernel,
        [arr(OWNERS, 8, 128), arr(1, FACES)],
        [pltpu.VMEM((14 * CAP, 2 * CHUNK), BF16), pltpu.VMEM((OWNERS, 14 * CAP), F32)],
        owner, element, element_state, scale, lift, transfer,
    )
    got = lax.all_to_all(msg, ("grp", "dev"), split_axis=0, concat_axis=0)

    west, east, mat = call(
        edge_kernel, [arr(ROWS, 128), arr(ROWS, 128), arr(2, 192, 192, dtype=BF16)], [], prev, element_scale, stiffness_ref
    )
    from_east, from_west = shift_pair(west, east, "dev")
    prev_side, north, south = rows_call(13, [prev, element_scale], from_east, from_west)
    prev_south, prev_north = shift_pair(north, south, "grp")

    load, west, east = call(
        scatter_kernel,
        [arr(12, ROWS, COLS), arr(ROWS, 128), arr(ROWS, 128)],
        [
            pltpu.VMEM((12 * ROWS, 256 * PAIRS), BF16),
            pltpu.VMEM((COLS, 256 * PAIRS), BF16),
            pltpu.VMEM((12 * ROWS, COLS), F32),
        ],
        got,
    )
    from_east, from_west = shift_pair(west, east, "dev")
    load_side, north, south = rows_call(12, [load], from_east, from_west)
    load_south, load_north = shift_pair(north, south, "grp")

    shell, back = call(
        sweep_kernel,
        [arr(12, ROWS, COLS), arr(OWNERS, 8, 128)],
        [
            pltpu.VMEM((12, PAD_R, PAD_C), F32),
            pltpu.VMEM((12, PAD_R, PAD_C), F32),
            pltpu.VMEM((PAD_R, PAD_C), F32),
            pltpu.VMEM((PAD_R // 16, 384, PAD_C), BF16),
            pltpu.VMEM((12 * ROWS, 2 * COLS), BF16),
        ],
        prev, element_scale, prev_side, prev_south, prev_north,
        load, load_side, load_south, load_north, mat, got,
    )
    returned = lax.all_to_all(back, ("grp", "dev"), split_axis=0, concat_axis=0)
    faces = call(
        return_kernel, arr(3, 10, FACES), [pltpu.VMEM((12 * CAP, 256), BF16)], returned, owner, rank, transfer
    )
    return shell.reshape(4, 3, ROWS, COLS), faces


def solution(mesh):
    placed = (
        P(("grp", "dev"), None),
        P(("grp", "dev")),
        P(None, ("grp", "dev")),
        P(),
        P(("grp", "dev")),
        P(),
        P(),
        P("grp", "dev"),
        P(None, None, "grp", "dev"),
    )
    return jax.shard_map(
        local,
        mesh=mesh,
        in_specs=placed,
        out_specs=(P(None, None, "grp", "dev"), P(None, None, ("grp", "dev"))),
        check_vma=False,
    )
```

time: 1580 us -> 128 us (0.08); the launches traced: 1560 us -> 128 us
  other arithmetic: 864 us -> 0 us
  local copies, waits for them, and re-layouts: 500 us -> 5.9 us
  starting transfers between devices: 99.6 us -> 18.4 us
  Pallas kernels: 0 us -> 65.9 us
  waiting for transfers between devices: 49.8 us -> 15.5 us
    unnamed x90 -> x0, other arithmetic: 702 us -> none
    gather x17 -> x0, local copies, waits for them, and re-layouts: 367 us -> none  [the longest x13 299 us: local(): firsts = jnp.searchsorted(sorted_owner, sorted_owner, side='left')]
    ppermute x32 -> x8, starting transfers between devices: 88.1 us -> 6.95 us  [the longest x4 4.78 us: shift_pair(): lax.ppermute(toward_low, axis, ring(axis, -1))]
    pallas_call x0 -> x7, Pallas kernels: none -> 65.9 us  [call(): pl.pallas_call(kernel, out_shape=shapes, in_specs=[pl.BlockSpec(memory_sp...]
    another operation x8 -> x0, other arithmetic: 64.2 us -> none  [relax(): jnp.stack(outputs)]
    scatter-add x1 -> x0, other arithmetic: 53.4 us -> none  [local(): jnp.zeros((12, grid_rows * grid_cols), jnp.float32).at[:, live_slot]]
    slice x26 -> x0, local copies, waits for them, and re-layouts: 47 us -> none  [the longest x1 28.1 us: relax(): shell_load[0] + coupling_weight * (west_side[1] + south_side[2])]
    ppermute x32 -> x8, waiting for transfers between devices: 49.8 us -> 5.61 us  [the longest x4 2.8 us: shift_pair(): lax.ppermute(toward_high, axis, ring(axis, 1))]
  transfers between devices with their start and end apart: 33 -> 9, of which waited for: 14 -> 5; matrix products, arithmetic and copies ran while one was open for 9% -> 0% of each run, Pallas kernels for 0% -> 15%
where the time goes in v1:
time: 128 us
  Pallas kernels  65.9 us (51%)
  blocking collectives  21.3 us (17%)
  starting transfers between devices  18.4 us (14%)
  waiting for transfers between devices  15.5 us (12%)
  local copies, waits for them, and re-layouts  5.9 us (5%)
    pallas_call x7, Pallas kernels, call(): pl.pallas_call(kernel, out_shape=shapes, in_specs=[pl.BlockSpec(memory_sp...  65.9 us
    all_to_all x1, blocking collectives, local(): returned = lax.all_to_all(back, ('grp', 'dev'), split_axis=0, concat_axis=0)  21.3 us
    all_to_all x1, starting transfers between devices, local(): got = lax.all_to_all(msg, ('grp', 'dev'), split_axis=0, concat_axis=0)  11.5 us
    all_to_all x1, waiting for transfers between devices, local(): got = lax.all_to_all(msg, ('grp', 'dev'), split_axis=0, concat_axis=0)  9.92 us
    unnamed x21, local copies, waits for them, and re-layouts  5.9 us
    ppermute x4, starting transfers between devices, shift_pair(): lax.ppermute(toward_low, axis, ring(axis, -1))  4.78 us
    ppermute x4, waiting for transfers between devices, shift_pair(): lax.ppermute(toward_high, axis, ring(axis, 1))  2.8 us
    ppermute x4, waiting for transfers between devices, shift_pair(): lax.ppermute(toward_low, axis, ring(axis, -1))  2.8 us
  transfers between devices with their start and end apart: 9, of which 5 were waited for; matrix products, arithmetic and copies ran while one was open for 0% of the time, Pallas kernels for 15%

profile of v1, /device:TPU:1, one launch (start us, length us, event | category | flops | bytes accessed | tf_op | source)
XLA Modules:
  0.0 127.8 jit_solution(8596163608610837816)
XLA Ops:
  0.6 0.0 copy-start.9
  0.6 0.7 copy-done.9
  1.3 0.0 copy-start.1
  1.3 1.2 copy-done.1
  2.5 0.0 copy-start.3
  2.5 0.7 copy-done.3
  3.2 0.0 copy-start.5
  3.2 0.7 copy-done.5
  3.9 0.0 copy-start.6
  3.9 0.7 copy-done.6
  4.6 0.0 copy-start.7
  4.7 0.7 copy-done.7
  5.3 0.0 copy-start
  5.3 12.8 %shard_map.106 = (f32[128,8,128]{2,1,0:T(8,128)}, f32[1,4096]{1,0:T(1,128)S(1)}) custom-call(s32[1,4096]{1,0:T(1,128)S(1)} %bitcast.8, s32[1,4096]{1,0:T(1,128)S(1)} %bitcast.10, bf16[110,4096]{1,0:T(8,128)(2,1)S(1)} %copy-done.1, f32[1,4096]{1,0:T(1,128)S(1)} %bitcast.11, bf16[30,110]{1,0:T(8,128)(2,1)S(1)} %copy-done.7, f32[4,10]{1,0:T(4,128)S(1)} %copy-done.9), custom_call_target="tpu_custom_call" | custom-call | tf_op jit(solution)/shard_map/pallas_call | solution.py:309
  18.2 0.0 copy-start.2
  18.2 0.0 copy-start.8
  18.2 11.5 %all-to-all-start = ((f32[128,8,128]{2,1,0:T(8,128)}), f32[128,8,128]{2,1,0:T(8,128)S(1)}, u32[]{:S(2)}, u32[]{:S(2)}) async-start(f32[128,8,128]{2,1,0:T(8,128)} %get-tuple-element.23), calls=%async_computation | async-start | bytes 1048576 | tf_op jit(solution)/shard_map/all_to_all | solution.py:354
  29.7 0.0 copy-done
  29.7 0.0 copy-done.2
  29.7 0.0 copy-done.8
  29.7 2.0 %shard_map.104 = (f32[64,128]{1,0:T(8,128)S(1)}, f32[64,128]{1,0:T(8,128)S(1)}, bf16[2,192,192]{2,1,0:T(8,128)(2,1)S(1)}) custom-call(f32[12,64,256]{2,1,0:T(8,128)S(1)} %bitcast.5, f32[64,256]{1,0:T(8,128)S(1)} %copy-done.2, f32[12,12]{1,0:T(8,128)S(1)} %copy-done.8), custom_call_target="tpu_custom_call" | custom-call | tf_op jit(solution)/shard_map/pallas_call | solution.py:309
  31.7 1.1 collective-permute-start
  32.8 0.7 collective-permute-start.1
  33.5 9.9 %all-to-all-done.msg_ref = f32[128,8,128]{2,1,0:T(8,128)S(1)} async-done(((f32[128,8,128]{2,1,0:T(8,128)}), f32[128,8,128]{2,1,0:T(8,128)S(1)}, u32[]{:S(2)}, u32[]{:S(2)}) %all-to-all-start) | async-done | bytes 524320 | tf_op jit(solution)/shard_map/all_to_all | solution.py:354
  43.4 16.3 %shard_map.107 = (f32[12,64,256]{2,1,0:T(8,128)S(1)}, f32[64,128]{1,0:T(8,128)S(1)}, f32[64,128]{1,0:T(8,128)S(1)}) custom-call(f32[128,8,128]{2,1,0:T(8,128)S(1)} %all-to-all-done.msg_ref), custom_call_target="tpu_custom_call" | custom-call | tf_op jit(solution)/shard_map/pallas_call | solution.py:309
  59.8 1.3 %collective-permute-start.4 = (f32[64,128]{1,0:T(8,128)S(1)}, f32[64,128]{1,0:T(8,128)S(1)}, u32[]{:S(2)}, u32[]{:S(2)}) collective-permute-start(f32[64,128]{1,0:T(8,128)S(1)} %get-tuple-element.25), channel_id=1, source_target_pairs={{0,31},{1,0},{2,1},{3,2},{4,3},{5,4},{6,5},{7,6},{8,7},{9,8},{10,9... | collective-permute-start | bytes 98312 | tf_op jit(solution)/shard_map/ppermute | solution.py:330
  61.1 0.5 collective-permute-start.5
  61.6 0.0 collective-permute-done.refs_2_
  61.6 0.0 collective-permute-done.1.refs_3_
  61.6 0.3 shard_map.105
  61.9 0.6 collective-permute-start.2
  62.5 1.0 collective-permute-start.3
  63.4 0.0 collective-permute-done.4.refs_1_
  63.4 0.0 collective-permute-done.5.refs_2_
  63.4 0.3 shard_map.108
  63.7 1.8 %collective-permute-start.6 = (f32[12,8,384]{2,1,0:T(8,128)S(1)}, f32[12,8,384]{2,1,0:T(8,128)S(1)}, u32[]{:S(2)}, u32[]{:S(2)}) collective-permute-start(f32[12,8,384]{2,1,0:T(8,128)S(1)} %get-tuple-element.28), channel_id=1, source_target_pairs={{0,96},{32,0},{64,32},{96,64},{1,97},{33,1},{65,33},{97,65},{2,98}... | collective-permute-start | bytes 442376 | tf_op jit(solution)/shard_map/ppermute | solution.py:330
  65.5 0.0 collective-permute-start.7
  65.5 2.2 %collective-permute-done.2.prev_south_ref = f32[13,8,384]{2,1,0:T(8,128)S(1)} collective-permute-done((f32[13,8,384]{2,1,0:T(8,128)S(1)}, f32[13,8,384]{2,1,0:T(8,128)S(1)}, u32[]{:S(2)}, u32[]{:S(2)}) %collective-permute-start.2) | collective-permute-done | bytes 159776 | tf_op jit(solution)/shard_map/ppermute | solution.py:330
  67.7 1.4 %collective-permute-done.3.prev_north_ref = f32[13,8,384]{2,1,0:T(8,128)S(1)} collective-permute-done((f32[13,8,384]{2,1,0:T(8,128)S(1)}, f32[13,8,384]{2,1,0:T(8,128)S(1)}, u32[]{:S(2)}, u32[]{:S(2)}) %collective-permute-start.3) | collective-permute-done | bytes 159776 | tf_op jit(solution)/shard_map/ppermute | solution.py:330
  69.1 0.6 collective-permute-done.6.load_south_ref
  69.7 1.4 %collective-permute-done.7.load_north_ref = f32[12,8,384]{2,1,0:T(8,128)S(1)} collective-permute-done((f32[12,8,384]{2,1,0:T(8,128)S(1)}, f32[12,8,384]{2,1,0:T(8,128)S(1)}, u32[]{:S(2)}, u32[]{:S(2)}) %collective-permute-start.7) | collective-permute-done | bytes 147488 | tf_op jit(solution)/shard_map/ppermute | solution.py:330
  71.1 25.8 %shard_map.109 = (f32[12,64,256]{2,1,0:T(8,128)}, f32[128,8,128]{2,1,0:T(8,128)S(1)}) custom-call(f32[12,64,256]{2,1,0:T(8,128)S(1)} %bitcast.7, f32[64,256]{1,0:T(8,128)S(1)} %copy-done.2, f32[13,64,128]{2,1,0:T(8,128)S(1)} %get-tuple-element.20.prev_side_ref, f32[13,8,384]{2,1,0:T(8,128)S(1)} %collective-permute-done.2.prev_south_ref, ...), custom_call_target="tpu_custom_call" | custom-call | tf_op jit(solution)/shard_map/pallas_call | solution.py:309
  96.8 0.0 copy-start.4
  96.8 21.3 %all_to_all.10.ret_ref = f32[128,8,128]{2,1,0:T(8,128)S(1)} all-to-all(f32[128,8,128]{2,1,0:T(8,128)S(1)} %get-tuple-element.32), channel_id=1, replica_groups=mesh['grp'=4,'dev'=32] {'grp','dev'}, dimensions={0} | all-to-all | bytes 1048576 | tf_op jit(solution)/shard_map/all_to_all | solution.py:390
  118.1 0.0 copy-done.4
  118.1 8.5 %shard_map.110 = f32[3,10,4096]{2,1,0:T(8,128)S(1)} custom-call(f32[128,8,128]{2,1,0:T(8,128)S(1)} %all_to_all.10.ret_ref, s32[1,4096]{1,0:T(1,128)S(1)} %bitcast.9, f32[1,4096]{1,0:T(1,128)S(1)} %get-tuple-element.33.rank_ref, f32[4,10]{1,0:T(4,128)S(1)} %copy-done.9), custom_call_target="tpu_custom_call" | custom-call | tf_op jit(solution)/shard_map/pallas_call | solution.py:309
  126.6 1.2 copy.11
Async XLA Ops:
  0.6 0.7 copy-start.9
  1.3 1.2 copy-start.1
  2.5 0.7 copy-start.3
  3.2 0.7 copy-start.5
  3.9 0.7 copy-start.6
  4.6 0.7 copy-start.7
  5.3 24.3 %copy-start = (f32[4,3,64,256]{3,2,1,0:T(8,128)S(1)}, f32[4,3,64,256]{3,2,1,0:T(8,128)}, u32[]{:S(2)}) copy-start(f32[4,3,64,256]{3,2,1,0:T(8,128)} %param.17) | copy-start | bytes 2359300
  18.2 11.5 %copy-start.2 = (f32[64,256]{1,0:T(8,128)S(1)}, f32[64,256]{1,0:T(8,128)}, u32[]{:S(2)}) copy-start(f32[64,256]{1,0:T(8,128)} %scale_ref.3) | copy-start | bytes 196612
  18.2 11.5 %copy-start.8 = (f32[12,12]{1,0:T(8,128)S(1)}, f32[12,12]{1,0:T(8,128)}, u32[]{:S(2)}) copy-start(f32[12,12]{1,0:T(8,128)} %stiff_ref.1) | copy-start | bytes 1732
  18.2 25.2 %all-to-all-start = ((f32[128,8,128]{2,1,0:T(8,128)}), f32[128,8,128]{2,1,0:T(8,128)S(1)}, u32[]{:S(2)}, u32[]{:S(2)}) async-start(f32[128,8,128]{2,1,0:T(8,128)} %get-tuple-element.23), calls=%async_computation | async-start | bytes 1048576 | tf_op jit(solution)/shard_map/all_to_all | solution.py:354
  31.7 29.9 %collective-permute-start = (f32[64,128]{1,0:T(8,128)S(1)}, f32[64,128]{1,0:T(8,128)S(1)}, u32[]{:S(2)}, u32[]{:S(2)}) collective-permute-start(f32[64,128]{1,0:T(8,128)S(1)} %get-tuple-element.18), channel_id=1, source_target_pairs={{0,31},{1,0},{2,1},{3,2},{4,3},{5,4},{6,5},{7,6},{8,7},{9,8},{10,9... | collective-permute-start | bytes 98312 | tf_op jit(solution)/shard_map/ppermute | solution.py:330
  32.8 28.8 %collective-permute-start.1 = (f32[64,128]{1,0:T(8,128)S(1)}, f32[64,128]{1,0:T(8,128)S(1)}, u32[]{:S(2)}, u32[]{:S(2)}) collective-permute-start(f32[64,128]{1,0:T(8,128)S(1)} %get-tuple-element.19), channel_id=1, source_target_pairs={{0,1},{1,2},{2,3},{3,4},{4,5},{5,6},{6,7},{7,8},{8,9},{9,10},{10,1... | collective-permute-start | bytes 98312 | tf_op jit(solution)/shard_map/ppermute | solution.py:330
  59.8 3.7 %collective-permute-start.4 = (f32[64,128]{1,0:T(8,128)S(1)}, f32[64,128]{1,0:T(8,128)S(1)}, u32[]{:S(2)}, u32[]{:S(2)}) collective-permute-start(f32[64,128]{1,0:T(8,128)S(1)} %get-tuple-element.25), channel_id=1, source_target_pairs={{0,31},{1,0},{2,1},{3,2},{4,3},{5,4},{6,5},{7,6},{8,7},{9,8},{10,9... | collective-permute-start | bytes 98312 | tf_op jit(solution)/shard_map/ppermute | solution.py:330
  61.1 2.4 %collective-permute-start.5 = (f32[64,128]{1,0:T(8,128)S(1)}, f32[64,128]{1,0:T(8,128)S(1)}, u32[]{:S(2)}, u32[]{:S(2)}) collective-permute-start(f32[64,128]{1,0:T(8,128)S(1)} %get-tuple-element.26), channel_id=1, source_target_pairs={{0,1},{1,2},{2,3},{3,4},{4,5},{5,6},{6,7},{7,8},{8,9},{9,10},{10,1... | collective-permute-start | bytes 98312 | tf_op jit(solution)/shard_map/ppermute | solution.py:330
  61.9 5.8 %collective-permute-start.2 = (f32[13,8,384]{2,1,0:T(8,128)S(1)}, f32[13,8,384]{2,1,0:T(8,128)S(1)}, u32[]{:S(2)}, u32[]{:S(2)}) collective-permute-start(f32[13,8,384]{2,1,0:T(8,128)S(1)} %get-tuple-element.21), channel_id=1, source_target_pairs={{0,96},{32,0},{64,32},{96,64},{1,97},{33,1},{65,33},{97,65},{2,98}... | collective-permute-start | bytes 479240 | tf_op jit(solution)/shard_map/ppermute | solution.py:330
  62.5 6.6 %collective-permute-start.3 = (f32[13,8,384]{2,1,0:T(8,128)S(1)}, f32[13,8,384]{2,1,0:T(8,128)S(1)}, u32[]{:S(2)}, u32[]{:S(2)}) collective-permute-start(f32[13,8,384]{2,1,0:T(8,128)S(1)} %get-tuple-element.22), channel_id=1, source_target_pairs={{0,32},{32,64},{64,96},{96,0},{1,33},{33,65},{65,97},{97,1},{2,34}... | collective-permute-start | bytes 479240 | tf_op jit(solution)/shard_map/ppermute | solution.py:330
  63.7 6.0 %collective-permute-start.6 = (f32[12,8,384]{2,1,0:T(8,128)S(1)}, f32[12,8,384]{2,1,0:T(8,128)S(1)}, u32[]{:S(2)}, u32[]{:S(2)}) collective-permute-start(f32[12,8,384]{2,1,0:T(8,128)S(1)} %get-tuple-element.28), channel_id=1, source_target_pairs={{0,96},{32,0},{64,32},{96,64},{1,97},{33,1},{65,33},{97,65},{2,98}... | collective-permute-start | bytes 442376 | tf_op jit(solution)/shard_map/ppermute | solution.py:330
  65.5 5.6 %collective-permute-start.7 = (f32[12,8,384]{2,1,0:T(8,128)S(1)}, f32[12,8,384]{2,1,0:T(8,128)S(1)}, u32[]{:S(2)}, u32[]{:S(2)}) collective-permute-start(f32[12,8,384]{2,1,0:T(8,128)S(1)} %get-tuple-element.29), channel_id=1, source_target_pairs={{0,32},{32,64},{64,96},{96,0},{1,33},{33,65},{65,97},{97,1},{2,34}... | collective-permute-start | bytes 442376 | tf_op jit(solution)/shard_map/ppermute | solution.py:330
  96.8 21.3 %copy-start.4 = (s32[4096,1]{0,1:T(1,128)S(1)}, s32[4096,1]{0,1:T(1,128)}, u32[]{:S(2)}) copy-start(s32[4096,1]{0,1:T(1,128)} %param.9) | copy-start | bytes 49156

commit v2 on v1

v2 whole, which is shorter than its diff:
```python
import functools

import jax
import jax.numpy as jnp
from jax import lax
from jax.experimental import pallas as pl
from jax.experimental.pallas import tpu as pltpu
from jax.sharding import PartitionSpec as P

SWEEPS = 8
WEIGHT = 2.2
HIGHEST = lax.Precision.HIGHEST
F32 = jnp.float32
BF16 = jnp.bfloat16
I32 = jnp.int32

OWNERS = 128
CAP = 64
COLS = 256
ROWS = 64
PAD_R = 80
PAD_C = 384
FACES = 4096
CHUNK = 256
STEP = 1024
HALF = 32
NT = (((1,), (1,)), ((), ()))


def iota(shape, dim):
    return lax.broadcasted_iota(I32, shape, dim)


def dot(a, b):
    return jnp.dot(a, b, preferred_element_type=F32)


def dot_nt(a, b):
    return lax.dot_general(a, b, NT, preferred_element_type=F32)


def exact(a, b):
    return jnp.dot(a, b, precision=HIGHEST, preferred_element_type=F32)


def one_hot(flag):
    return flag.astype(F32).astype(BF16)


def split(x):
    high = x.astype(BF16)
    return high, (x - high.astype(F32)).astype(BF16)


def hot_rows(row, count):
    wide = jnp.broadcast_to(row, (16, row.shape[1]))
    step = iota((16, row.shape[1]), 0).astype(F32)
    return jnp.concatenate([one_hot(step == wide - 16.0 * k) for k in range(count // 16)], axis=0)


def quarters(hot, quarter):
    wide = jnp.broadcast_to(quarter, (16, quarter.shape[1]))
    return [hot * jnp.concatenate([one_hot(wide == q)] * (OWNERS // 16), axis=0) for q in range(4)]


def face_kernel(owner_ref, elem_ref, state_ref, scale_ref, lift_ref, transfer_ref, west_ref, msg_ref, rank_ref,
                x_ref, hot_ref, acc_ref):
    del west_ref
    by_node = exact((iota((12, 4), 0) // 3 == iota((12, 4), 1)).astype(F32), transfer_ref[...])
    spread = exact(by_node, (iota((10, 30), 1) % 10 == iota((10, 30), 0)).astype(F32))
    spread = jnp.where(iota((12, 30), 0) % 3 == iota((12, 30), 1) // 10, spread, 0.0)
    weights = exact(spread, lift_ref[...].astype(F32))
    high, low = split(weights)
    x_ref[...] = jnp.zeros_like(x_ref)
    acc_ref[...] = jnp.zeros_like(acc_ref)
    before = iota((CHUNK, 2 * CHUNK), 0)
    upper = iota((CHUNK, 2 * CHUNK), 1)
    upper = one_hot((before < upper) | (upper >= CHUNK))

    def ranks(i, base):
        part = pl.ds(pl.multiple_of(i * CHUNK, CHUNK), CHUNK)
        hot = (iota((OWNERS, CHUNK), 0) == owner_ref[:, part]).astype(F32)
        counts = dot(hot.astype(BF16), upper)
        rank_ref[:, part] = jnp.sum(hot * (counts[:, :CHUNK] + base), axis=0, keepdims=True)
        return base + counts[:, CHUNK:]

    lax.fori_loop(0, FACES // CHUNK, ranks, jnp.zeros((OWNERS, CHUNK), F32), unroll=4)

    def body(i, carry):
        part = pl.ds(pl.multiple_of(i * STEP, STEP), STEP)
        rank = rank_ref[:, part].astype(I32)
        hot = hot_rows(owner_ref[:, part].astype(F32), OWNERS)
        for q, piece in enumerate(quarters(hot, rank >> 4)):
            hot_ref[q * OWNERS:(q + 1) * OWNERS, :] = piece
        place = hot_rows((rank & 15).astype(F32), 16)
        state = state_ref[:, part]
        load = (dot(high, state) + dot(low, state)) * scale_ref[:, part]
        marker = (elem_ref[:, part] + 1).astype(F32)
        for c in range(13):
            row = load[c:c + 1] if c < 12 else marker
            top, rest = split(jnp.broadcast_to(row, (16, STEP)))
            x_ref[16 * c:16 * c + 16, :STEP] = place * top
            x_ref[16 * c:16 * c + 16, STEP:] = place * rest
        acc_ref[...] += dot_nt(hot_ref[...], x_ref[:, :STEP]) + dot_nt(hot_ref[...], x_ref[:, STEP:])
        return carry

    lax.fori_loop(0, FACES // STEP, body, 0)
    for q in range(4):
        for t in range(2):
            msg_ref[:, 2 * q + t, :] = acc_ref[q * OWNERS:(q + 1) * OWNERS, 128 * t:128 * t + 128]


def places(marker):
    element = marker.astype(I32) - 1
    row, col = element >> 8, (element & 255).astype(F32)
    columns = jnp.concatenate(
        [hot_rows(jnp.where(row < HALF, col, -1.0), COLS), hot_rows(jnp.where(row < HALF, -1.0, col), COLS)], axis=0
    )
    return (row & (HALF - 1)).astype(F32), columns


def edge_sends(comps, west_ref, east_ref):
    lane = iota((ROWS, 128), 1)
    west = jnp.zeros((ROWS, 128), F32)
    east = jnp.zeros((ROWS, 128), F32)
    for i, comp in enumerate(comps):
        here = lane // 8 == i
        low = comp(0)
        high = comp(128)
        west = jnp.where(here, pltpu.roll(low, 8 * i, 1) if i else low, west)
        east = jnp.where(here, pltpu.roll(high, (8 * i + 8) % 128, 1), east)
    west_ref[...] = west
    east_ref[...] = east


def scatter_kernel(msg_ref, load_ref, west_ref, east_ref, mark_ref, a_ref, col_ref, acc_ref, turned_ref):
    acc_ref[...] = jnp.zeros_like(acc_ref)
    for j in range(8):
        turned_ref[j] = jnp.transpose(msg_ref[:, j, :])
    for q in range(4):
        mark_ref[16 * q:16 * q + 16, :] = turned_ref[2 * q + 1, 64:80, :]

    def body(g, carry):
        q, h = g >> 1, pl.multiple_of(8 * (g & 1), 8)
        markers = mark_ref[pl.ds(pl.multiple_of(8 * g, 8), 8), :]
        for k in range(8):
            lanes = slice(128 * k, 128 * k + 128)
            row, columns = places(markers[k:k + 1])
            col_ref[:, lanes] = columns
            row_hot = hot_rows(row, HALF)
            for c in range(12):
                values = turned_ref[2 * q + c // 8, pl.ds(16 * (c % 8) + h, 8), :]
                top, rest = split(jnp.broadcast_to(values[k:k + 1] * (1.0 / WEIGHT), (16, 128)))
                for b in range(HALF // 16):
                    at = c * HALF + 16 * b
                    a_ref[at:at + 16, lanes] = row_hot[16 * b:16 * b + 16] * top
                    a_ref[at:at + 16, 1024 + 128 * k:1024 + 128 * k + 128] = row_hot[16 * b:16 * b + 16] * rest
        acc_ref[...] += dot_nt(a_ref[:, :1024], col_ref[...]) + dot_nt(a_ref[:, 1024:], col_ref[...])
        return carry

    lax.fori_loop(0, 8, body, 0)
    for c in range(12):
        for b in range(2):
            load_ref[c, HALF * b:HALF * (b + 1), :] = acc_ref[c * HALF:(c + 1) * HALF, COLS * b:COLS * (b + 1)]
    edge_sends([(lambda lane, c=c: load_ref[c, :, lane:lane + 128]) for c in range(12)], west_ref, east_ref)


def edge_kernel(prev_ref, scale_ref, west_ref, east_ref):
    comps = [(lambda lane, c=c: prev_ref[c, :, lane:lane + 128]) for c in range(12)]
    comps.append(lambda lane: scale_ref[:, lane:lane + 128])
    edge_sends(comps, west_ref, east_ref)


def matrix_kernel(stiff_ref, mat_ref):
    eye = (iota((12, 12), 0) == iota((12, 12), 1)).astype(F32)
    approx = eye / 5.0
    rest = eye - exact(stiff_ref[...], approx)
    for turn in range(8):
        approx = approx + exact(approx, rest)
        if turn < 7:
            rest = exact(rest, rest)
    tall = (iota((192, 12), 0) // 16 == iota((192, 12), 1)).astype(F32)
    wide = (iota((12, 192), 1) // 16 == iota((12, 192), 0)).astype(F32)
    big = exact(exact(tall, approx * WEIGHT), wide)
    big = jnp.where(iota((192, 192), 0) % 16 == iota((192, 192), 1) % 16, big, 0.0)
    high, low = split(big)
    mat_ref[0] = high
    mat_ref[1] = low


def rows_kernel(count, refs):
    cores, (from_east_ref, from_west_ref, side_ref, north_ref, south_ref) = refs[:count], refs[count:]
    at = 0
    lane = iota((ROWS, 128), 1)
    dev = lax.axis_index("dev")
    from_east = jnp.where(dev < lax.axis_size("dev") - 1, from_east_ref[...], 0.0)
    from_west = jnp.where(dev > 0, from_west_ref[...], 0.0)
    for core in cores:
        planes = core.shape[0] if len(core.shape) == 3 else 1
        for c in range(planes):
            view = core.at[c] if len(core.shape) == 3 else core
            low = pltpu.roll(from_east, (128 - 8 * at) % 128, 1) if at else from_east
            high = pltpu.roll(from_west, (120 - 8 * at) % 128, 1)
            side = jnp.where(lane < 8, low, jnp.where(lane >= 120, high, 0.0))
            side_ref[at] = side
            north_ref[at, :, :COLS] = view[0:8, :]
            north_ref[at, :, COLS:] = side[0:8]
            south_ref[at, :, :COLS] = view[ROWS - 8:ROWS, :]
            south_ref[at, :, COLS:] = side[ROWS - 8:ROWS]
            at += 1


def sweep_kernel(prev_ref, scale_ref, prev_side_ref, prev_south_ref, prev_north_ref,
                 load_ref, load_side_ref, load_south_ref, load_north_ref, mat_ref, mark_ref,
                 out_ref, ret_ref, u_ref, f_ref, inv_ref, x_ref, hl_ref, turned_ref):
    for dst, core, side, south, north in (
        (u_ref, prev_ref, prev_side_ref, prev_south_ref, prev_north_ref),
        (f_ref, load_ref, load_side_ref, load_south_ref, load_north_ref),
    ):
        dst[:, 0:ROWS, 0:COLS] = core[...]
        dst[:, 0:ROWS, COLS:PAD_C] = side[0:12]
        dst[:, ROWS:ROWS + 8, :] = south[0:12]
        dst[:, ROWS + 8:PAD_R, :] = north[0:12]
    inv_ref[0:ROWS, 0:COLS] = scale_ref[...]
    inv_ref[0:ROWS, COLS:PAD_C] = prev_side_ref[12]
    inv_ref[ROWS:ROWS + 8, :] = prev_south_ref[12]
    inv_ref[ROWS + 8:PAD_R, :] = prev_north_ref[12]
    grp, dev = lax.axis_index("grp"), lax.axis_index("dev")
    row, col = iota((PAD_R, PAD_C), 0), iota((PAD_R, PAD_C), 1)
    row_ok = (row < ROWS) | ((row < ROWS + 8) & (grp < lax.axis_size("grp") - 1)) | ((row >= ROWS + 8) & (grp > 0))
    col_ok = (col < COLS) | ((col < COLS + 8) & (dev < lax.axis_size("dev") - 1)) | ((col >= PAD_C - 8) & (dev > 0))
    ok = row_ok & col_ok
    inv_ref[...] = jnp.where(ok, 1.0 / jnp.where(ok, inv_ref[...], 1.0), 0.0)
    for c in range(12):
        u_ref[c] = jnp.where(ok, u_ref[c], 0.0)
    along = ((1, 1), (0, PAD_C - 1), (3, 1), (2, PAD_C - 1))
    across = ((2, 1), (3, 1), (0, PAD_R - 1), (1, PAD_R - 1))

    def sweep(turn, carry):
        for n in range(4):
            for c in range(3):
                at = 3 * n + c
                right = (
                    f_ref[at]
                    + pltpu.roll(u_ref[3 * along[n][0] + c], along[n][1], 1)
                    + pltpu.roll(u_ref[3 * across[n][0] + c], across[n][1], 0)
                )
                top, rest = split(right)
                for b in range(PAD_R // 16):
                    x_ref[b, 16 * at:16 * at + 16] = top[16 * b:16 * b + 16]
                    x_ref[b, 192 + 16 * at:192 + 16 * at + 16] = rest[16 * b:16 * b + 16]
        high = mat_ref[0]
        both = jnp.concatenate([high, high], axis=1)
        for b in range(PAD_R // 16):
            solved = dot(both, x_ref[b]) + dot(mat_ref[1], x_ref[b, 0:192])
            factor = inv_ref[16 * b:16 * b + 16]
            for at in range(12):
                u_ref[at, 16 * b:16 * b + 16] = solved[16 * at:16 * at + 16] * factor
        return carry

    lax.fori_loop(0, SWEEPS, sweep, 0)
    for c in range(12):
        value = u_ref[c, 0:ROWS, 0:COLS]
        out_ref[c] = value
        top, rest = split(value)
        for b in range(2):
            part = slice(HALF * b, HALF * (b + 1))
            hl_ref[c * HALF:(c + 1) * HALF, COLS * b:COLS * (b + 1)] = top[part]
            hl_ref[c * HALF:(c + 1) * HALF, 512 + COLS * b:512 + COLS * (b + 1)] = rest[part]

    def gather(g, carry):
        q, h = g >> 1, pl.multiple_of(8 * (g & 1), 8)
        markers = mark_ref[pl.ds(pl.multiple_of(8 * g, 8), 8), :]
        for s in range(2):
            row, columns = places(jnp.concatenate([markers[4 * s + k:4 * s + k + 1] for k in range(4)], axis=1))
            found = dot(hl_ref[:, :512], columns) + dot(hl_ref[:, 512:], columns)
            here = iota((HALF, 512), 0).astype(F32) == row
            for c in range(12):
                value = jnp.sum(jnp.where(here, found[c * HALF:(c + 1) * HALF], 0.0), axis=0, keepdims=True)
                value = jnp.concatenate([value[:, 128 * k:128 * k + 128] for k in range(4)], axis=0)
                turned_ref[2 * q + c // 8, pl.ds(16 * (c % 8) + h + 4 * s, 4), :] = value
        return carry

    lax.fori_loop(0, 8, gather, 0)
    for j in range(8):
        ret_ref[:, j, :] = jnp.transpose(turned_ref[j])


def return_kernel(ret_ref, owner_ref, rank_ref, transfer_ref, out_ref, l_ref, hot_ref, faces_ref, sems):
    for q in range(4):
        for t in range(2):
            count = 128 if t == 0 else 64
            top, rest = split(jnp.transpose(ret_ref[:, 2 * q + t, :])[:count])
            l_ref[128 * t:128 * t + count, 128 * q:128 * q + 128] = top
            l_ref[128 * t:128 * t + count, 512 + 128 * q:512 + 128 * q + 128] = rest
    pick = (iota((48, 10), 0) % 16 == iota((48, 10), 1)).astype(F32)
    spread = lax.dot_general(pick, transfer_ref[...], NT, precision=HIGHEST, preferred_element_type=F32)
    spread = exact(spread, (iota((4, 16), 1) // 3 == iota((4, 16), 0)).astype(F32))
    spread = jnp.where(iota((48, 16), 0) // 16 == iota((48, 16), 1) % 3, spread, 0.0)
    high, low = split(spread)
    copies = []
    for i in range(FACES // STEP):
        part = slice(i * STEP, (i + 1) * STEP)
        rank = rank_ref[:, part].astype(I32)
        hot = hot_rows(owner_ref[:, part].astype(F32), OWNERS)
        for q, piece in enumerate(quarters(hot, rank >> 4)):
            hot_ref[q * OWNERS:(q + 1) * OWNERS, :] = piece
        found = dot(l_ref[:, :512], hot_ref[...]) + dot(l_ref[:, 512:], hot_ref[...])
        here = iota((16, STEP), 0) == (rank & 15)
        node = jnp.concatenate(
            [jnp.sum(jnp.where(here, found[16 * c:16 * c + 16], 0.0), axis=0, keepdims=True) for c in range(12)]
            + [jnp.zeros((4, STEP), F32)],
            axis=0,
        )
        top, rest = split(node)
        result = dot(high, top) + (dot(high, rest) + dot(low, top))
        for c in range(3):
            faces_ref[c, :, part] = result[16 * c:16 * c + 10]
        copy = pltpu.make_async_copy(faces_ref.at[:, :, part], out_ref.at[:, :, part], sems.at[i])
        copy.start()
        copies.append(copy)
    for copy in copies:
        copy.wait()


VMEM = pl.BlockSpec(memory_space=pltpu.VMEM)
HBM = pl.BlockSpec(memory_space=pl.ANY)
AUTO = pl.BlockSpec()


def call(kernel, outs, scratch, *args, auto=(), out_specs=None):
    single = not isinstance(outs, (list, tuple))
    shapes = [outs] if single else list(outs)
    result = pl.pallas_call(
        kernel,
        out_shape=shapes,
        in_specs=[AUTO if i in auto else VMEM for i in range(len(args))],
        out_specs=out_specs or [VMEM] * len(shapes),
        scratch_shapes=scratch,
        compiler_params=pltpu.CompilerParams(vmem_limit_bytes=48 * 1024 * 1024),
    )(*args)
    return result[0] if single else result


def arr(*shape, dtype=F32):
    return jax.ShapeDtypeStruct(shape, dtype)


def ring(axis, step):
    count = lax.axis_size(axis)
    return [(i, (i + step) % count) for i in range(count)]


def shift_pair(toward_low, toward_high, axis):
    return lax.ppermute(toward_low, axis, ring(axis, -1)), lax.ppermute(toward_high, axis, ring(axis, 1))


def rows_call(count, cores, from_east, from_west):
    def kernel(*refs):
        rows_kernel(len(cores), refs)

    return call(
        kernel, [arr(count, ROWS, 128), arr(count, 8, PAD_C), arr(count, 8, PAD_C)], [], *cores, from_east, from_west
    )


def local(face_owner, face_element, element_state, lift, face_scale, transfer, stiffness_ref, element_scale, displacement_prev):
    owner = face_owner.reshape(1, FACES)
    element = face_element.reshape(1, FACES)
    scale = face_scale.reshape(1, FACES)
    prev = displacement_prev.reshape(12, ROWS, COLS)

    west, east = call(edge_kernel, [arr(ROWS, 128), arr(ROWS, 128)], [], prev, element_scale, auto=(0, 1))
    from_east, from_west = shift_pair(west, east, "dev")
    msg, rank = call(
        face_kernel,
        [arr(OWNERS, 8, 128), arr(1, FACES)],
        [pltpu.VMEM((256, 2 * STEP), BF16), pltpu.VMEM((4 * OWNERS, STEP), BF16), pltpu.VMEM((4 * OWNERS, 256), F32)],
        owner, element, element_state, scale, lift, transfer, west,
        auto=(0, 1, 2, 3, 4, 5),
    )
    prev_side, north, south = rows_call(13, [prev, element_scale], from_east, from_west)
    msg, north, south = lax.optimization_barrier((msg, north, south))
    prev_south, prev_north = shift_pair(north, south, "grp")
    got = lax.all_to_all(msg, ("grp", "dev"), split_axis=0, concat_axis=0)
    mat = call(matrix_kernel, arr(2, 192, 192, dtype=BF16), [], stiffness_ref)

    load, west, east, mark = call(
        scatter_kernel,
        [arr(12, ROWS, COLS), arr(ROWS, 128), arr(ROWS, 128), arr(64, 128)],
        [
            pltpu.VMEM((12 * HALF, 2048), BF16),
            pltpu.VMEM((2 * COLS, 1024), BF16),
            pltpu.VMEM((12 * HALF, 2 * COLS), F32),
            pltpu.VMEM((8, 128, 128), F32),
        ],
        got,
    )
    from_east, from_west = shift_pair(west, east, "dev")
    load_side, north, south = rows_call(12, [load], from_east, from_west)
    load_south, load_north = shift_pair(north, south, "grp")

    shell, back = call(
        sweep_kernel,
        [arr(12, ROWS, COLS), arr(OWNERS, 8, 128)],
        [
            pltpu.VMEM((12, PAD_R, PAD_C), F32),
            pltpu.VMEM((12, PAD_R, PAD_C), F32),
            pltpu.VMEM((PAD_R, PAD_C), F32),
            pltpu.VMEM((PAD_R // 16, 384, PAD_C), BF16),
            pltpu.VMEM((12 * HALF, 1024), BF16),
            pltpu.VMEM((8, 128, 128), F32),
        ],
        prev, element_scale, prev_side, prev_south, prev_north,
        load, load_side, load_south, load_north, mat, mark,
    )
    returned = lax.all_to_all(back, ("grp", "dev"), split_axis=0, concat_axis=0)
    faces = call(
        return_kernel,
        arr(3, 10, FACES),
        [
            pltpu.VMEM((192, 1024), BF16),
            pltpu.VMEM((4 * OWNERS, STEP), BF16),
            pltpu.VMEM((3, 10, FACES), F32),
            pltpu.SemaphoreType.DMA((FACES // STEP,)),
        ],
        returned, owner, rank, transfer,
        out_specs=[HBM],
    )
    return shell.reshape(4, 3, ROWS, COLS), faces


def solution(mesh):
    placed = (
        P(("grp", "dev"), None),
        P(("grp", "dev")),
        P(None, ("grp", "dev")),
        P(),
        P(("grp", "dev")),
        P(),
        P(),
        P("grp", "dev"),
        P(None, None, "grp", "dev"),
    )
    return jax.shard_map(
        local,
        mesh=mesh,
        in_specs=placed,
        out_specs=(P(None, None, "grp", "dev"), P(None, None, ("grp", "dev"))),
        check_vma=False,
    )
```

time: 128 us -> 104 us (0.81)
  Pallas kernels: 65.9 us -> 41.5 us
  blocking collectives: 21.3 us -> 45.6 us
  waiting for transfers between devices: 15.5 us -> 3.78 us
  starting transfers between devices: 18.4 us -> 7.64 us
  local copies, waits for them, and re-layouts: 5.9 us -> 4.35 us
    pallas_call x7 -> x8, Pallas kernels: 65.9 us -> 41.5 us  [call(): pl.pallas_call(kernel, out_shape=shapes, in_specs=[AUTO if i in auto else...]
    all_to_all x0 -> x1, blocking collectives: none -> 24.2 us  [local(): got = lax.all_to_all(msg, ('grp', 'dev'), split_axis=0, concat_axis=0)]
    all_to_all x1 -> x0, starting transfers between devices: 11.5 us -> none  [local(): got = lax.all_to_all(msg, ('grp', 'dev'), split_axis=0, concat_axis=0)]
    all_to_all x1 -> x0, waiting for transfers between devices: 9.92 us -> none  [local(): got = lax.all_to_all(msg, ('grp', 'dev'), split_axis=0, concat_axis=0)]
    ppermute x4, starting transfers between devices: 2.17 us -> 4.5 us  [shift_pair(): lax.ppermute(toward_high, axis, ring(axis, 1))]
    ppermute x4, waiting for transfers between devices: 2.8 us -> 0.92 us  [shift_pair(): lax.ppermute(toward_low, axis, ring(axis, -1))]
    ppermute x4, starting transfers between devices: 4.78 us -> 3.14 us  [shift_pair(): lax.ppermute(toward_low, axis, ring(axis, -1))]
    unnamed x21 -> x23, local copies, waits for them, and re-layouts: 5.9 us -> 4.35 us
  transfers between devices with their start and end apart: 9 -> 8, of which waited for: 5 -> 5; matrix products, arithmetic and copies ran while one was open for 0% -> 0% of each run, Pallas kernels for 15% -> 8%
where the time goes in v2:
time: 104 us
  blocking collectives  45.6 us (44%)
  Pallas kernels  41.5 us (40%)
  starting transfers between devices  7.64 us (7%)
  local copies, waits for them, and re-layouts  4.35 us (4%)
  waiting for transfers between devices  3.78 us (4%)
    pallas_call x8, Pallas kernels, call(): pl.pallas_call(kernel, out_shape=shapes, in_specs=[AUTO if i in auto else...  41.5 us
    all_to_all x1, blocking collectives, local(): got = lax.all_to_all(msg, ('grp', 'dev'), split_axis=0, concat_axis=0)  24.2 us
    all_to_all x1, blocking collectives, local(): returned = lax.all_to_all(back, ('grp', 'dev'), split_axis=0, concat_axis=0)  21.4 us
    ppermute x4, starting transfers between devices, shift_pair(): lax.ppermute(toward_high, axis, ring(axis, 1))  4.5 us
    unnamed x23, local copies, waits for them, and re-layouts  4.35 us
    ppermute x4, starting transfers between devices, shift_pair(): lax.ppermute(toward_low, axis, ring(axis, -1))  3.14 us
    ppermute x4, waiting for transfers between devices, shift_pair(): lax.ppermute(toward_high, axis, ring(axis, 1))  2.85 us
  transfers between devices with their start and end apart: 8, of which 5 were waited for; matrix products, arithmetic and copies ran while one was open for 0% of the time, Pallas kernels for 8%

profile of v2, /device:TPU:1, one launch (start us, length us, event | category | flops | bytes accessed | tf_op | source)
XLA Modules:
  0.0 103.7 jit_solution(9625957503387870600)
XLA Ops:
  0.6 0.0 copy-start
  0.6 1.1 %copy-done = f32[4,3,64,256]{3,2,1,0:T(8,128)S(1)} copy-done((f32[4,3,64,256]{3,2,1,0:T(8,128)S(1)}, f32[4,3,64,256]{3,2,1,0:T(8,128)}, u32[]{:S(2)}) %copy-start) | copy-done | bytes 786456
  1.8 0.0 copy-start.3
  1.8 0.8 copy-done.3
  2.6 0.0 copy-start.5
  2.6 0.0 copy-start.6
  2.6 0.0 copy-start.7
  2.6 0.0 copy-start.9
  2.6 0.0 copy-start.1
  2.6 0.3 shard_map.104
  2.9 0.0 copy-start.8
  2.9 2.7 %collective-permute-start.1 = (f32[64,128]{1,0:T(8,128)S(1)}, f32[64,128]{1,0:T(8,128)S(1)}, u32[]{:S(2)}, u32[]{:S(2)}) collective-permute-start(f32[64,128]{1,0:T(8,128)S(1)} %get-tuple-element.22), channel_id=1, source_target_pairs={{0,1},{1,2},{2,3},{3,4},{4,5},{5,6},{6,7},{7,8},{8,9},{9,10},{10,1... | collective-permute-start | bytes 98312 | tf_op jit(solution)/shard_map/ppermute | solution.py:355
  5.6 0.0 collective-permute-start
  5.6 0.0 copy-done.5
  5.6 0.0 copy-done.6
  5.6 0.0 copy-done.7
  5.6 0.0 copy-done.9
  5.6 0.0 copy-done.8
  5.6 0.0 copy-start.2
  5.6 1.2 %copy-done.2 = bf16[110,4096]{1,0:T(8,128)(2,1)S(1)} copy-done((bf16[110,4096]{1,0:T(8,128)(2,1)S(1)}, bf16[110,4096]{1,0:T(8,128)(2,1)}, u32[]{:S(2)}) %copy-start.2) | copy-done | bytes 901144
  6.8 0.0 copy-start.4
  6.8 5.9 %shard_map.106 = (f32[128,8,128]{2,1,0:T(8,128)S(1)}, f32[1,4096]{1,0:T(1,128)S(1)}) custom-call(s32[1,4096]{1,0:T(1,128)S(1)} %bitcast.8, s32[1,4096]{1,0:T(1,128)S(1)} %bitcast.10, bf16[110,4096]{1,0:T(8,128)(2,1)S(1)} %copy-done.2, f32[1,4096]{1,0:T(1,128)S(1)} %bitcast.11, bf16[30,110]{1,0:T(8,128)(2,1)S(1)} %copy-done.8, f32[4,10]{1,0:T(4,128)S(1)} %copy-done.9, ...), custom_call_target="tpu_custom_call" | custom-call | tf_op jit(solution)/shard_map/pallas_call | solution.py:334
  12.7 0.0 collective-permute-done.1.refs_3_
  12.7 0.0 collective-permute-done.refs_2_
  12.7 0.0 copy-done.1
  12.7 0.0 copy-done.4
  12.7 0.3 shard_map.105
  13.0 24.2 %all_to_all.10.msg_ref = f32[128,8,128]{2,1,0:T(8,128)S(1)} all-to-all(f32[128,8,128]{2,1,0:T(8,128)S(1)} %get-tuple-element.29), channel_id=1, replica_groups=mesh['grp'=4,'dev'=32] {'grp','dev'}, dimensions={0} | all-to-all | bytes 1048576 | tf_op jit(solution)/shard_map/all_to_all | solution.py:385
  37.2 11.0 %shard_map.107 = (f32[12,64,256]{2,1,0:T(8,128)S(1)}, f32[64,128]{1,0:T(8,128)S(1)}, f32[64,128]{1,0:T(8,128)S(1)}, f32[64,128]{1,0:T(8,128)S(1)}) custom-call(f32[128,8,128]{2,1,0:T(8,128)S(1)} %all_to_all.10.msg_ref), custom_call_target="tpu_custom_call" | custom-call | tf_op jit(solution)/shard_map/pallas_call | solution.py:334
  48.2 0.9 collective-permute-start.4
  49.2 0.9 collective-permute-start.5
  50.0 0.5 collective-permute-start.2
  50.6 1.0 collective-permute-start.3
  51.5 0.1 collective-permute-done.4.refs_1_
  51.6 0.0 collective-permute-done.5.refs_2_
  51.6 0.0 copy-start.10
  51.6 0.3 shard_map.108
  51.9 1.7 %collective-permute-start.6 = (f32[12,8,384]{2,1,0:T(8,128)S(1)}, f32[12,8,384]{2,1,0:T(8,128)S(1)}, u32[]{:S(2)}, u32[]{:S(2)}) collective-permute-start(f32[12,8,384]{2,1,0:T(8,128)S(1)} %get-tuple-element.34), channel_id=1, source_target_pairs={{0,96},{32,0},{64,32},{96,64},{1,97},{33,1},{65,33},{97,65},{2,98}... | collective-permute-start | bytes 442376 | tf_op jit(solution)/shard_map/ppermute | solution.py:355
  53.6 0.0 collective-permute-start.7
  53.6 0.0 copy-done.10
  53.6 1.9 %shard_map.109.mat_ref = bf16[2,192,192]{2,1,0:T(8,128)(2,1)S(1)} custom-call(f32[12,12]{1,0:T(8,128)S(1)} %copy-done.10), custom_call_target="tpu_custom_call" | custom-call | tf_op jit(solution)/shard_map/pallas_call | solution.py:334
  55.6 0.5 collective-permute-done.2.prev_south_ref
  56.0 1.4 %collective-permute-done.3.prev_north_ref = f32[13,8,384]{2,1,0:T(8,128)S(1)} collective-permute-done((f32[13,8,384]{2,1,0:T(8,128)S(1)}, f32[13,8,384]{2,1,0:T(8,128)S(1)}, u32[]{:S(2)}, u32[]{:S(2)}) %collective-permute-start.3) | collective-permute-done | bytes 159776 | tf_op jit(solution)/shard_map/ppermute | solution.py:355
  57.5 0.3 collective-permute-done.6.load_south_ref
  57.8 1.4 %collective-permute-done.7.load_north_ref = f32[12,8,384]{2,1,0:T(8,128)S(1)} collective-permute-done((f32[12,8,384]{2,1,0:T(8,128)S(1)}, f32[12,8,384]{2,1,0:T(8,128)S(1)}, u32[]{:S(2)}, u32[]{:S(2)}) %collective-permute-start.7) | collective-permute-done | bytes 147488 | tf_op jit(solution)/shard_map/ppermute | solution.py:355
  59.2 18.1 %shard_map.110 = (f32[12,64,256]{2,1,0:T(8,128)}, f32[128,8,128]{2,1,0:T(8,128)S(1)}) custom-call(f32[12,64,256]{2,1,0:T(8,128)S(1)} %bitcast.7, f32[64,256]{1,0:T(8,128)S(1)} %copy-done.4, f32[13,64,128]{2,1,0:T(8,128)S(1)} %get-tuple-element.23.prev_side_ref, f32[13,8,384]{2,1,0:T(8,128)S(1)} %collective-permute-done.2.prev_south_ref, ...), custom_call_target="tpu_custom_call" | custom-call | tf_op jit(solution)/shard_map/pallas_call | solution.py:334
  77.3 21.4 %all_to_all.11.ret_ref = f32[128,8,128]{2,1,0:T(8,128)S(1)} all-to-all(f32[128,8,128]{2,1,0:T(8,128)S(1)} %get-tuple-element.38), channel_id=1, replica_groups=mesh['grp'=4,'dev'=32] {'grp','dev'}, dimensions={0} | all-to-all | bytes 1048576 | tf_op jit(solution)/shard_map/all_to_all | solution.py:417
  98.7 3.8 %shard_map.111 = f32[3,10,4096]{2,1,0:T(8,128)S(1)} custom-call(f32[128,8,128]{2,1,0:T(8,128)S(1)} %all_to_all.11.ret_ref, s32[1,4096]{1,0:T(1,128)S(1)} %bitcast.9, f32[1,4096]{1,0:T(1,128)S(1)} %get-tuple-element.39.rank_ref, f32[4,10]{1,0:T(4,128)S(1)} %copy-done.9), custom_call_target="tpu_custom_call" | custom-call | tf_op jit(solution)/shard_map/pallas_call | solution.py:334
  102.5 1.2 %copy.11 = f32[3,10,4096]{2,0,1:T(4,128)} copy(f32[3,10,4096]{2,1,0:T(8,128)S(1)} %shard_map.111) | data formatting | bytes 983040
Async XLA Ops:
  0.6 1.1 %copy-start = (f32[4,3,64,256]{3,2,1,0:T(8,128)S(1)}, f32[4,3,64,256]{3,2,1,0:T(8,128)}, u32[]{:S(2)}) copy-start(f32[4,3,64,256]{3,2,1,0:T(8,128)} %param.17) | copy-start | bytes 2359300
  1.8 0.8 copy-start.3
  2.6 3.0 %copy-start.5 = (s32[4096,1]{0,1:T(1,128)S(1)}, s32[4096,1]{0,1:T(1,128)}, u32[]{:S(2)}) copy-start(s32[4096,1]{0,1:T(1,128)} %param.9) | copy-start | bytes 49156
  2.6 3.0 %copy-start.6 = (s32[4096]{0:T(1024)S(1)}, s32[4096]{0:T(1024)}, u32[]{:S(2)}) copy-start(s32[4096]{0:T(1024)} %param.10) | copy-start | bytes 49156
  2.6 3.0 %copy-start.7 = (f32[4096]{0:T(1024)S(1)}, f32[4096]{0:T(1024)}, u32[]{:S(2)}) copy-start(f32[4096]{0:T(1024)} %param.13) | copy-start | bytes 49156
  2.6 3.0 %copy-start.9 = (f32[4,10]{1,0:T(4,128)S(1)}, f32[4,10]{1,0:T(4,128)}, u32[]{:S(2)}) copy-start(f32[4,10]{1,0:T(4,128)} %transfer_ref.3) | copy-start | bytes 484
  2.6 10.1 %copy-start.1 = (f32[4,3,64,256]{3,2,1,0:T(8,128)S(1)}, f32[4,3,64,256]{3,2,1,0:T(8,128)}, u32[]{:S(2)}) copy-start(f32[4,3,64,256]{3,2,1,0:T(8,128)} %param.17) | copy-start | bytes 2359300
  2.9 2.7 %copy-start.8 = (bf16[30,110]{1,0:T(8,128)(2,1)S(1)}, bf16[30,110]{1,0:T(8,128)(2,1)}, u32[]{:S(2)}) copy-start(bf16[30,110]{1,0:T(8,128)(2,1)} %lift_ref.1) | copy-start | bytes 19804
  2.9 9.8 %collective-permute-start.1 = (f32[64,128]{1,0:T(8,128)S(1)}, f32[64,128]{1,0:T(8,128)S(1)}, u32[]{:S(2)}, u32[]{:S(2)}) collective-permute-start(f32[64,128]{1,0:T(8,128)S(1)} %get-tuple-element.22), channel_id=1, source_target_pairs={{0,1},{1,2},{2,3},{3,4},{4,5},{5,6},{6,7},{7,8},{8,9},{9,10},{10,1... | collective-permute-start | bytes 98312 | tf_op jit(solution)/shard_map/ppermute | solution.py:355
  5.6 7.1 %collective-permute-start = (f32[64,128]{1,0:T(8,128)S(1)}, f32[64,128]{1,0:T(8,128)S(1)}, u32[]{:S(2)}, u32[]{:S(2)}) collective-permute-start(f32[64,128]{1,0:T(8,128)S(1)} %get-tuple-element.21.west_ref), channel_id=1, source_target_pairs={{0,31},{1,0},{2,1},{3,2},{4,3},{5,4},{6,5},{7,6},{8,7},{9,8},{10,9... | collective-permute-start | bytes 98312 | tf_op jit(solution)/shard_map/ppermute | solution.py:355
  5.6 1.2 %copy-start.2 = (bf16[110,4096]{1,0:T(8,128)(2,1)S(1)}, bf16[110,4096]{1,0:T(8,128)(2,1)}, u32[]{:S(2)}) copy-start(bf16[110,4096]{1,0:T(8,128)(2,1)} %state_ref.1) | copy-start | bytes 2703364
  6.8 5.9 %copy-start.4 = (f32[64,256]{1,0:T(8,128)S(1)}, f32[64,256]{1,0:T(8,128)}, u32[]{:S(2)}) copy-start(f32[64,256]{1,0:T(8,128)} %scale_ref.3) | copy-start | bytes 196612
  48.2 3.4 %collective-permute-start.4 = (f32[64,128]{1,0:T(8,128)S(1)}, f32[64,128]{1,0:T(8,128)S(1)}, u32[]{:S(2)}, u32[]{:S(2)}) collective-permute-start(f32[64,128]{1,0:T(8,128)S(1)} %get-tuple-element.31), channel_id=1, source_target_pairs={{0,31},{1,0},{2,1},{3,2},{4,3},{5,4},{6,5},{7,6},{8,7},{9,8},{10,9... | collective-permute-start | bytes 98312 | tf_op jit(solution)/shard_map/ppermute | solution.py:355
  49.2 2.5 %collective-permute-start.5 = (f32[64,128]{1,0:T(8,128)S(1)}, f32[64,128]{1,0:T(8,128)S(1)}, u32[]{:S(2)}, u32[]{:S(2)}) collective-permute-start(f32[64,128]{1,0:T(8,128)S(1)} %get-tuple-element.32), channel_id=1, source_target_pairs={{0,1},{1,2},{2,3},{3,4},{4,5},{5,6},{6,7},{7,8},{8,9},{9,10},{10,1... | collective-permute-start | bytes 98312 | tf_op jit(solution)/shard_map/ppermute | solution.py:355
  50.0 6.0 %collective-permute-start.2 = (f32[13,8,384]{2,1,0:T(8,128)S(1)}, f32[13,8,384]{2,1,0:T(8,128)S(1)}, u32[]{:S(2)}, u32[]{:S(2)}) collective-permute-start(f32[13,8,384]{2,1,0:T(8,128)S(1)} %get-tuple-element.27), channel_id=1, source_target_pairs={{0,96},{32,0},{64,32},{96,64},{1,97},{33,1},{65,33},{97,65},{2,98}... | collective-permute-start | bytes 479240 | tf_op jit(solution)/shard_map/ppermute | solution.py:355
  50.6 6.9 %collective-permute-start.3 = (f32[13,8,384]{2,1,0:T(8,128)S(1)}, f32[13,8,384]{2,1,0:T(8,128)S(1)}, u32[]{:S(2)}, u32[]{:S(2)}) collective-permute-start(f32[13,8,384]{2,1,0:T(8,128)S(1)} %get-tuple-element.28), channel_id=1, source_target_pairs={{0,32},{32,64},{64,96},{96,0},{1,33},{33,65},{65,97},{97,1},{2,34}... | collective-permute-start | bytes 479240 | tf_op jit(solution)/shard_map/ppermute | solution.py:355
  51.6 2.0 %copy-start.10 = (f32[12,12]{1,0:T(8,128)S(1)}, f32[12,12]{1,0:T(8,128)}, u32[]{:S(2)}) copy-start(f32[12,12]{1,0:T(8,128)} %stiff_ref.1) | copy-start | bytes 1732
  51.9 5.8 %collective-permute-start.6 = (f32[12,8,384]{2,1,0:T(8,128)S(1)}, f32[12,8,384]{2,1,0:T(8,128)S(1)}, u32[]{:S(2)}, u32[]{:S(2)}) collective-permute-start(f32[12,8,384]{2,1,0:T(8,128)S(1)} %get-tuple-element.34), channel_id=1, source_target_pairs={{0,96},{32,0},{64,32},{96,64},{1,97},{33,1},{65,33},{97,65},{2,98}... | collective-permute-start | bytes 442376 | tf_op jit(solution)/shard_map/ppermute | solution.py:355
  53.6 5.6 %collective-permute-start.7 = (f32[12,8,384]{2,1,0:T(8,128)S(1)}, f32[12,8,384]{2,1,0:T(8,128)S(1)}, u32[]{:S(2)}, u32[]{:S(2)}) collective-permute-start(f32[12,8,384]{2,1,0:T(8,128)S(1)} %get-tuple-element.35), channel_id=1, source_target_pairs={{0,32},{32,64},{64,96},{96,0},{1,33},{33,65},{65,97},{97,1},{2,34}... | collective-permute-start | bytes 442376 | tf_op jit(solution)/shard_map/ppermute | solution.py:355

commit v3 on v2

--- a/solution.py
+++ b/solution.py
@@ -24,6 +24,8 @@
 CHUNK = 256
 STEP = 1024
 HALF = 32
+PLANES = 25
+LIMIT = 60
 NT = (((1,), (1,)), ((), ()))
 
 
@@ -63,19 +65,23 @@
     return [hot * jnp.concatenate([one_hot(wide == q)] * (OWNERS // 16), axis=0) for q in range(4)]
 
 
-def face_kernel(owner_ref, elem_ref, state_ref, scale_ref, lift_ref, transfer_ref, west_ref, msg_ref, rank_ref,
-                x_ref, hot_ref, acc_ref):
-    del west_ref
-    by_node = exact((iota((12, 4), 0) // 3 == iota((12, 4), 1)).astype(F32), transfer_ref[...])
-    spread = exact(by_node, (iota((10, 30), 1) % 10 == iota((10, 30), 0)).astype(F32))
-    spread = jnp.where(iota((12, 30), 0) % 3 == iota((12, 30), 1) // 10, spread, 0.0)
-    weights = exact(spread, lift_ref[...].astype(F32))
-    high, low = split(weights)
+def face_kernel(owner_hbm, elem_hbm, state_hbm, scale_hbm, lift_hbm, transfer_hbm, msg_ref, rank_ref,
+                owner_ref, elem_ref, state_ref, scale_ref, lift_ref, transfer_ref, x_ref, hot_ref, acc_ref, sems):
+    copies = [
+        pltpu.make_async_copy(src, dst, sems.at[i])
+        for i, (src, dst) in enumerate((
+            (owner_hbm, owner_ref), (transfer_hbm, transfer_ref), (lift_hbm, lift_ref),
+            (elem_hbm, elem_ref), (scale_hbm, scale_ref), (state_hbm, state_ref),
+        ))
+    ]
+    for copy in copies:
+        copy.start()
     x_ref[...] = jnp.zeros_like(x_ref)
     acc_ref[...] = jnp.zeros_like(acc_ref)
     before = iota((CHUNK, 2 * CHUNK), 0)
     upper = iota((CHUNK, 2 * CHUNK), 1)
     upper = one_hot((before < upper) | (upper >= CHUNK))
+    copies[0].wait()
 
     def ranks(i, base):
         part = pl.ds(pl.multiple_of(i * CHUNK, CHUNK), CHUNK)
@@ -85,6 +91,13 @@
         return base + counts[:, CHUNK:]
 
     lax.fori_loop(0, FACES // CHUNK, ranks, jnp.zeros((OWNERS, CHUNK), F32), unroll=4)
+    for copy in copies[1:]:
+        copy.wait()
+    by_node = exact((iota((12, 4), 0) // 3 == iota((12, 4), 1)).astype(F32), transfer_ref[...])
+    spread = exact(by_node, (iota((10, 30), 1) % 10 == iota((10, 30), 0)).astype(F32))
+    spread = jnp.where(iota((12, 30), 0) % 3 == iota((12, 30), 1) // 10, spread, 0.0)
+    weights = exact(spread, lift_ref[...].astype(F32))
+    high, low = split(weights)
 
     def body(i, carry):
         part = pl.ds(pl.multiple_of(i * STEP, STEP), STEP)
@@ -121,19 +134,20 @@
 
 def edge_sends(comps, west_ref, east_ref):
     lane = iota((ROWS, 128), 1)
-    west = jnp.zeros((ROWS, 128), F32)
-    east = jnp.zeros((ROWS, 128), F32)
-    for i, comp in enumerate(comps):
-        here = lane // 8 == i
-        low = comp(0)
-        high = comp(128)
-        west = jnp.where(here, pltpu.roll(low, 8 * i, 1) if i else low, west)
-        east = jnp.where(here, pltpu.roll(high, (8 * i + 8) % 128, 1), east)
-    west_ref[...] = west
-    east_ref[...] = east
-
-
-def scatter_kernel(msg_ref, load_ref, west_ref, east_ref, mark_ref, a_ref, col_ref, acc_ref, turned_ref):
+    for tile in range(2):
+        west = jnp.zeros((ROWS, 128), F32)
+        east = jnp.zeros((ROWS, 128), F32)
+        for i, comp in enumerate(comps[16 * tile:16 * tile + 16]):
+            here = lane // 8 == i
+            low = comp(0)
+            high = comp(128)
+            west = jnp.where(here, pltpu.roll(low, 8 * i, 1) if i else low, west)
+            east = jnp.where(here, pltpu.roll(high, (8 * i + 8) % 128, 1), east)
+        west_ref[:, 128 * tile:128 * tile + 128] = west
+        east_ref[:, 128 * tile:128 * tile + 128] = east
+
+
+def scatter_kernel(msg_ref, prev_ref, scale_ref, load_ref, west_ref, east_ref, mark_ref, a_ref, col_ref, acc_ref, turned_ref):
     acc_ref[...] = jnp.zeros_like(acc_ref)
     for j in range(8):
         turned_ref[j] = jnp.transpose(msg_ref[:, j, :])
@@ -162,13 +176,12 @@
     for c in range(12):
         for b in range(2):
             load_ref[c, HALF * b:HALF * (b + 1), :] = acc_ref[c * HALF:(c + 1) * HALF, COLS * b:COLS * (b + 1)]
-    edge_sends([(lambda lane, c=c: load_ref[c, :, lane:lane + 128]) for c in range(12)], west_ref, east_ref)
-
-
-def edge_kernel(prev_ref, scale_ref, west_ref, east_ref):
-    comps = [(lambda lane, c=c: prev_ref[c, :, lane:lane + 128]) for c in range(12)]
-    comps.append(lambda lane: scale_ref[:, lane:lane + 128])
-    edge_sends(comps, west_ref, east_ref)
+    edge_sends(
+        [(lambda lane, c=c: load_ref[c, :, lane:lane + 128]) for c in range(12)]
+        + [(lambda lane, c=c: prev_ref[c, :, lane:lane + 128]) for c in range(12)]
+        + [lambda lane: scale_ref[:, lane:lane + 128]],
+        west_ref, east_ref,
+    )
 
 
 def matrix_kernel(stiff_ref, mat_ref):
@@ -179,52 +192,50 @@
         approx = approx + exact(approx, rest)
         if turn < 7:
             rest = exact(rest, rest)
-    tall = (iota((192, 12), 0) // 16 == iota((192, 12), 1)).astype(F32)
-    wide = (iota((12, 192), 1) // 16 == iota((12, 192), 0)).astype(F32)
+    tall = (iota((96, 12), 0) // 8 == iota((96, 12), 1)).astype(F32)
+    wide = (iota((12, 96), 1) // 8 == iota((12, 96), 0)).astype(F32)
     big = exact(exact(tall, approx * WEIGHT), wide)
-    big = jnp.where(iota((192, 192), 0) % 16 == iota((192, 192), 1) % 16, big, 0.0)
+    big = jnp.where(iota((96, 96), 0) % 8 == iota((96, 96), 1) % 8, big, 0.0)
     high, low = split(big)
-    mat_ref[0] = high
-    mat_ref[1] = low
-
-
-def rows_kernel(count, refs):
-    cores, (from_east_ref, from_west_ref, side_ref, north_ref, south_ref) = refs[:count], refs[count:]
-    at = 0
+    mat_ref[0:96, :] = jnp.concatenate([high, high], axis=1)
+    mat_ref[96:192, :] = jnp.concatenate([low, jnp.zeros_like(low)], axis=1)
+
+
+def rows_kernel(load_ref, prev_ref, scale_ref, from_east_ref, from_west_ref, side_ref, north_ref, south_ref):
     lane = iota((ROWS, 128), 1)
-    dev = lax.axis_index("dev")
-    from_east = jnp.where(dev < lax.axis_size("dev") - 1, from_east_ref[...], 0.0)
-    from_west = jnp.where(dev > 0, from_west_ref[...], 0.0)
-    for core in cores:
-        planes = core.shape[0] if len(core.shape) == 3 else 1
-        for c in range(planes):
-            view = core.at[c] if len(core.shape) == 3 else core
-            low = pltpu.roll(from_east, (128 - 8 * at) % 128, 1) if at else from_east
-            high = pltpu.roll(from_west, (120 - 8 * at) % 128, 1)
-            side = jnp.where(lane < 8, low, jnp.where(lane >= 120, high, 0.0))
-            side_ref[at] = side
-            north_ref[at, :, :COLS] = view[0:8, :]
-            north_ref[at, :, COLS:] = side[0:8]
-            south_ref[at, :, :COLS] = view[ROWS - 8:ROWS, :]
-            south_ref[at, :, COLS:] = side[ROWS - 8:ROWS]
-            at += 1
-
-
-def sweep_kernel(prev_ref, scale_ref, prev_side_ref, prev_south_ref, prev_north_ref,
-                 load_ref, load_side_ref, load_south_ref, load_north_ref, mat_ref, mark_ref,
+    group = iota((8, 128), 1) // 16
+    packed = [[jnp.zeros((8, 128), F32) for _ in range(4)] for _ in range(2)]
+    for p in range(PLANES):
+        tile = slice(128 * (p // 16), 128 * (p // 16) + 128)
+        low = pltpu.roll(from_east_ref[:, tile], (128 - 8 * (p % 16)) % 128, 1)
+        high = pltpu.roll(from_west_ref[:, tile], (248 - 8 * (p % 16)) % 128, 1)
+        side = jnp.where(lane < 8, low, jnp.where(lane >= 120, high, 0.0))
+        side_ref[p] = side
+        core = load_ref.at[p] if p < 12 else prev_ref.at[p - 12] if p < 24 else scale_ref
+        for way, (ref, at) in enumerate(((north_ref, 0), (south_ref, ROWS - 8))):
+            ref[p] = core[at:at + 8, :]
+            turned = pltpu.roll(side[at:at + 8], (8 + 16 * (p % 8)) % 128, 1)
+            packed[way][p // 8] = jnp.where(group == p % 8, turned, packed[way][p // 8])
+    for way, ref in enumerate((north_ref, south_ref)):
+        for t in range(4):
+            ref[PLANES + t // 2, :, 128 * (t % 2):128 * (t % 2) + 128] = packed[way][t]
+
+
+def side_of(rows_ref, p):
+    t = p // 8
+    tile = rows_ref[PLANES + t // 2, :, 128 * (t % 2):128 * (t % 2) + 128]
+    return pltpu.roll(tile, (248 - 16 * (p % 8)) % 128, 1)
+
+
+def sweep_kernel(load_ref, prev_ref, scale_ref, side_ref, south_ref, north_ref, mat_ref, mark_ref,
                  out_ref, ret_ref, u_ref, f_ref, inv_ref, x_ref, hl_ref, turned_ref):
-    for dst, core, side, south, north in (
-        (u_ref, prev_ref, prev_side_ref, prev_south_ref, prev_north_ref),
-        (f_ref, load_ref, load_side_ref, load_south_ref, load_north_ref),
-    ):
-        dst[:, 0:ROWS, 0:COLS] = core[...]
-        dst[:, 0:ROWS, COLS:PAD_C] = side[0:12]
-        dst[:, ROWS:ROWS + 8, :] = south[0:12]
-        dst[:, ROWS + 8:PAD_R, :] = north[0:12]
-    inv_ref[0:ROWS, 0:COLS] = scale_ref[...]
-    inv_ref[0:ROWS, COLS:PAD_C] = prev_side_ref[12]
-    inv_ref[ROWS:ROWS + 8, :] = prev_south_ref[12]
-    inv_ref[ROWS + 8:PAD_R, :] = prev_north_ref[12]
+    for p in range(PLANES):
+        dst = f_ref.at[p] if p < 12 else u_ref.at[p - 12] if p < 24 else inv_ref
+        dst[0:ROWS, 0:COLS] = scale_ref[...] if p == 24 else load_ref[p] if p < 12 else prev_ref[p - 12]
+        dst[0:ROWS, COLS:PAD_C] = side_ref[p]
+        for at, rows in ((ROWS, south_ref), (ROWS + 8, north_ref)):
+            dst[at:at + 8, 0:COLS] = rows[p]
+            dst[at:at + 8, COLS:PAD_C] = side_of(rows, p)
     grp, dev = lax.axis_index("grp"), lax.axis_index("dev")
     row, col = iota((PAD_R, PAD_C), 0), iota((PAD_R, PAD_C), 1)
     row_ok = (row < ROWS) | ((row < ROWS + 8) & (grp < lax.axis_size("grp") - 1)) | ((row >= ROWS + 8) & (grp > 0))
@@ -236,29 +247,36 @@
     along = ((1, 1), (0, PAD_C - 1), (3, 1), (2, PAD_C - 1))
     across = ((2, 1), (3, 1), (0, PAD_R - 1), (1, PAD_R - 1))
 
+    def right_side(at):
+        n, c = divmod(at, 3)
+        return (
+            f_ref[at]
+            + pltpu.roll(u_ref[3 * along[n][0] + c], along[n][1], 1)
+            + pltpu.roll(u_ref[3 * across[n][0] + c], across[n][1], 0)
+        )
+
     def sweep(turn, carry):
-        for n in range(4):
-            for c in range(3):
-                at = 3 * n + c
-                right = (
-                    f_ref[at]
-                    + pltpu.roll(u_ref[3 * along[n][0] + c], along[n][1], 1)
-                    + pltpu.roll(u_ref[3 * across[n][0] + c], across[n][1], 0)
-                )
-                top, rest = split(right)
-                for b in range(PAD_R // 16):
-                    x_ref[b, 16 * at:16 * at + 16] = top[16 * b:16 * b + 16]
-                    x_ref[b, 192 + 16 * at:192 + 16 * at + 16] = rest[16 * b:16 * b + 16]
-        high = mat_ref[0]
-        both = jnp.concatenate([high, high], axis=1)
+        for at in range(0, 12, 2):
+            first, second = right_side(at), right_side(at + 1)
+            for b in range(PAD_R // 8):
+                rows = slice(8 * b, 8 * b + 8)
+                top, rest = split(jnp.concatenate([first[rows], second[rows]], axis=0))
+                lanes = slice(PAD_C * (b % 2), PAD_C * (b % 2) + PAD_C)
+                x_ref[b // 2, 8 * at:8 * at + 16, lanes] = top
+                x_ref[b // 2, 96 + 8 * at:96 + 8 * at + 16, lanes] = rest
         for b in range(PAD_R // 16):
-            solved = dot(both, x_ref[b]) + dot(mat_ref[1], x_ref[b, 0:192])
-            factor = inv_ref[16 * b:16 * b + 16]
-            for at in range(12):
-                u_ref[at, 16 * b:16 * b + 16] = solved[16 * at:16 * at + 16] * factor
+            solved = dot(mat_ref[...], x_ref[b])
+            for h in range(2):
+                rows = slice(16 * b + 8 * h, 16 * b + 8 * h + 8)
+                lanes = slice(PAD_C * h, PAD_C * h + PAD_C)
+                factor = inv_ref[rows]
+                for at in range(12):
+                    u_ref[at, rows] = (
+                        solved[8 * at:8 * at + 8, lanes] + solved[96 + 8 * at:96 + 8 * at + 8, lanes]
+                    ) * factor
         return carry
 
-    lax.fori_loop(0, SWEEPS, sweep, 0)
+    lax.fori_loop(0, SWEEPS, sweep, 0, unroll=2)
     for c in range(12):
         value = u_ref[c, 0:ROWS, 0:COLS]
         out_ref[c] = value
@@ -293,10 +311,10 @@
             top, rest = split(jnp.transpose(ret_ref[:, 2 * q + t, :])[:count])
             l_ref[128 * t:128 * t + count, 128 * q:128 * q + 128] = top
             l_ref[128 * t:128 * t + count, 512 + 128 * q:512 + 128 * q + 128] = rest
-    pick = (iota((48, 10), 0) % 16 == iota((48, 10), 1)).astype(F32)
+    pick = (iota((80, 10), 0) // 8 == iota((80, 10), 1)).astype(F32)
     spread = lax.dot_general(pick, transfer_ref[...], NT, precision=HIGHEST, preferred_element_type=F32)
     spread = exact(spread, (iota((4, 16), 1) // 3 == iota((4, 16), 0)).astype(F32))
-    spread = jnp.where(iota((48, 16), 0) // 16 == iota((48, 16), 1) % 3, spread, 0.0)
+    spread = jnp.where(iota((80, 16), 0) % 8 == iota((80, 16), 1) % 3, spread, 0.0)
     high, low = split(spread)
     copies = []
     for i in range(FACES // STEP):
@@ -314,8 +332,8 @@
         )
         top, rest = split(node)
         result = dot(high, top) + (dot(high, rest) + dot(low, top))
-        for c in range(3):
-            faces_ref[c, :, part] = result[16 * c:16 * c + 10]
+        for k in range(10):
+            faces_ref[k, :, part] = result[8 * k:8 * k + 3]
         copy = pltpu.make_async_copy(faces_ref.at[:, :, part], out_ref.at[:, :, part], sems.at[i])
         copy.start()
         copies.append(copy)
@@ -325,19 +343,18 @@
 
 VMEM = pl.BlockSpec(memory_space=pltpu.VMEM)
 HBM = pl.BlockSpec(memory_space=pl.ANY)
-AUTO = pl.BlockSpec()
-
-
-def call(kernel, outs, scratch, *args, auto=(), out_specs=None):
+
+
+def call(kernel, outs, scratch, *args, hbm=(), out_specs=None, limit=48):
     single = not isinstance(outs, (list, tuple))
     shapes = [outs] if single else list(outs)
     result = pl.pallas_call(
         kernel,
         out_shape=shapes,
-        in_specs=[AUTO if i in auto else VMEM for i in range(len(args))],
+        in_specs=[HBM if i in hbm else VMEM for i in range(len(args))],
         out_specs=out_specs or [VMEM] * len(shapes),
         scratch_shapes=scratch,
-        compiler_params=pltpu.CompilerParams(vmem_limit_bytes=48 * 1024 * 1024),
+        compiler_params=pltpu.CompilerParams(vmem_limit_bytes=limit * 1024 * 1024),
     )(*args)
     return result[0] if single else result
 
@@ -353,15 +370,6 @@
 
 def shift_pair(toward_low, toward_high, axis):
     return lax.ppermute(toward_low, axis, ring(axis, -1)), lax.ppermute(toward_high, axis, ring(axis, 1))
-
-
-def rows_call(count, cores, from_east, from_west):
-    def kernel(*refs):
-        rows_kernel(len(cores), refs)
-
-    return call(
-        kernel, [arr(count, ROWS, 128), arr(count, 8, PAD_C), arr(count, 8, PAD_C)], [], *cores, from_east, from_west
-    )
 
 
 def local(face_owner, face_element, element_state, lift, face_scale, transfer, stiffness_ref, element_scale, displacement_prev):
@@ -370,35 +378,40 @@
     scale = face_scale.reshape(1, FACES)
     prev = displacement_prev.reshape(12, ROWS, COLS)
 
-    west, east = call(edge_kernel, [arr(ROWS, 128), arr(ROWS, 128)], [], prev, element_scale, auto=(0, 1))
-    from_east, from_west = shift_pair(west, east, "dev")
     msg, rank = call(
         face_kernel,
         [arr(OWNERS, 8, 128), arr(1, FACES)],
-        [pltpu.VMEM((256, 2 * STEP), BF16), pltpu.VMEM((4 * OWNERS, STEP), BF16), pltpu.VMEM((4 * OWNERS, 256), F32)],
-        owner, element, element_state, scale, lift, transfer, west,
-        auto=(0, 1, 2, 3, 4, 5),
-    )
-    prev_side, north, south = rows_call(13, [prev, element_scale], from_east, from_west)
-    msg, north, south = lax.optimization_barrier((msg, north, south))
-    prev_south, prev_north = shift_pair(north, south, "grp")
+        [
+            pltpu.VMEM((1, FACES), I32), pltpu.VMEM((1, FACES), I32), pltpu.VMEM((110, FACES), BF16),
+            pltpu.VMEM((1, FACES), F32), pltpu.VMEM((30, 110), BF16), pltpu.VMEM((4, 10), F32),
+            pltpu.VMEM((256, 2 * STEP), BF16), pltpu.VMEM((4 * OWNERS, STEP), BF16), pltpu.VMEM((4 * OWNERS, 256), F32),
+            pltpu.SemaphoreType.DMA((6,)),
+        ],
+        owner, element, element_state, scale, lift, transfer,
+        hbm=(0, 1, 2, 3, 4, 5), limit=LIMIT,
+    )
     got = lax.all_to_all(msg, ("grp", "dev"), split_axis=0, concat_axis=0)
-    mat = call(matrix_kernel, arr(2, 192, 192, dtype=BF16), [], stiffness_ref)
+    mat = call(matrix_kernel, arr(192, 192, dtype=BF16), [], stiffness_ref)
 
     load, west, east, mark = call(
         scatter_kernel,
-        [arr(12, ROWS, COLS), arr(ROWS, 128), arr(ROWS, 128), arr(64, 128)],
+        [arr(12, ROWS, COLS), arr(ROWS, 256), arr(ROWS, 256), arr(64, 128)],
         [
             pltpu.VMEM((12 * HALF, 2048), BF16),
             pltpu.VMEM((2 * COLS, 1024), BF16),
             pltpu.VMEM((12 * HALF, 2 * COLS), F32),
             pltpu.VMEM((8, 128, 128), F32),
         ],
-        got,
+        got, prev, element_scale,
     )
     from_east, from_west = shift_pair(west, east, "dev")
-    load_side, north, south = rows_call(12, [load], from_east, from_west)
-    load_south, load_north = shift_pair(north, south, "grp")
+    side, north, south = call(
+        rows_kernel,
+        [arr(PLANES, ROWS, 128), arr(PLANES + 2, 8, COLS), arr(PLANES + 2, 8, COLS)],
+        [],
+        load, prev, element_scale, from_east, from_west,
+    )
+    south, north = shift_pair(north, south, "grp")
 
     shell, back = call(
         sweep_kernel,
@@ -407,27 +420,26 @@
             pltpu.VMEM((12, PAD_R, PAD_C), F32),
             pltpu.VMEM((12, PAD_R, PAD_C), F32),
             pltpu.VMEM((PAD_R, PAD_C), F32),
-            pltpu.VMEM((PAD_R // 16, 384, PAD_C), BF16),
+            pltpu.VMEM((PAD_R // 16, 192, 2 * PAD_C), BF16),
             pltpu.VMEM((12 * HALF, 1024), BF16),
             pltpu.VMEM((8, 128, 128), F32),
         ],
-        prev, element_scale, prev_side, prev_south, prev_north,
-        load, load_side, load_south, load_north, mat, mark,
+        load, prev, element_scale, side, south, north, mat, mark,
     )
     returned = lax.all_to_all(back, ("grp", "dev"), split_axis=0, concat_axis=0)
     faces = call(
         return_kernel,
-        arr(3, 10, FACES),
+        arr(10, 3, FACES),
         [
             pltpu.VMEM((192, 1024), BF16),
             pltpu.VMEM((4 * OWNERS, STEP), BF16),
-            pltpu.VMEM((3, 10, FACES), F32),
+            pltpu.VMEM((10, 3, FACES), F32),
             pltpu.SemaphoreType.DMA((FACES // STEP,)),
         ],
         returned, owner, rank, transfer,
         out_specs=[HBM],
     )
-    return shell.reshape(4, 3, ROWS, COLS), faces
+    return shell.reshape(4, 3, ROWS, COLS), jnp.transpose(faces, (1, 0, 2))
 
 
 def solution(mesh):

time: 104 us -> 99.8 us (0.960)
  local copies, waits for them, and re-layouts: 4.35 us -> 0.03 us
  starting transfers between devices: 7.64 us -> 3.35 us
  blocking collectives: 45.6 us -> 48.1 us
  waiting for transfers between devices: 3.78 us -> 5.21 us
    unnamed x23 -> x12, local copies, waits for them, and re-layouts: 4.35 us -> 0.03 us
    ppermute x4 -> x2, starting transfers between devices: 4.5 us -> 1.84 us  [shift_pair(): lax.ppermute(toward_high, axis, ring(axis, 1))]
    ppermute x4 -> x2, waiting for transfers between devices: 0.92 us -> 3.49 us  [shift_pair(): lax.ppermute(toward_low, axis, ring(axis, -1))]
    ppermute x4 -> x2, starting transfers between devices: 3.14 us -> 1.51 us  [shift_pair(): lax.ppermute(toward_low, axis, ring(axis, -1))]
    all_to_all x1, blocking collectives: 21.4 us -> 22.9 us  [local(): returned = lax.all_to_all(back, ('grp', 'dev'), split_axis=0, concat_axis=0)]
    ppermute x4 -> x2, waiting for transfers between devices: 2.85 us -> 1.72 us  [shift_pair(): lax.ppermute(toward_high, axis, ring(axis, 1))]
    pallas_call x8 -> x6, Pallas kernels: 41.5 us -> 41.9 us  [call(): pl.pallas_call(kernel, out_shape=shapes, in_specs=[HBM if i in hbm else V...]
  transfers between devices with their start and end apart: 8 -> 4, of which waited for: 5 -> 3; matrix products, arithmetic and copies ran while one was open for 0% -> 0% of each run, Pallas kernels for 8% -> 2%
where the time goes in v3:
time: 99.8 us; the launch traced here: 99.5 us
  blocking collectives  48.1 us (48%)
  Pallas kernels  41.9 us (42%)
  waiting for transfers between devices  5.21 us (5%)
  starting transfers between devices  3.35 us (3%)
    pallas_call x6, Pallas kernels, call(): pl.pallas_call(kernel, out_shape=shapes, in_specs=[HBM if i in hbm else V...  41.9 us
    all_to_all x1, blocking collectives, local(): got = lax.all_to_all(msg, ('grp', 'dev'), split_axis=0, concat_axis=0)  25.2 us
    all_to_all x1, blocking collectives, local(): returned = lax.all_to_all(back, ('grp', 'dev'), split_axis=0, concat_axis=0)  22.9 us
    ppermute x2, waiting for transfers between devices, shift_pair(): lax.ppermute(toward_low, axis, ring(axis, -1))  3.49 us
  transfers between devices with their start and end apart: 4, of which 3 were waited for; matrix products, arithmetic and copies ran while one was open for 0% of the time, Pallas kernels for 2%

profile of v3, /device:TPU:1, one launch (start us, length us, event | category | flops | bytes accessed | tf_op | source)
XLA Modules:
  0.0 99.5 jit_solution(17773904913855536892)
XLA Ops:
  0.6 0.0 copy-start
  0.6 7.5 %shard_map.104 = (f32[128,8,128]{2,1,0:T(8,128)}, f32[1,4096]{1,0:T(1,128)}) custom-call(s32[1,4096]{1,0:T(1,128)} %bitcast.9, s32[1,4096]{1,0:T(1,128)} %bitcast.12, bf16[110,4096]{1,0:T(8,128)(2,1)} %state_hbm.1, f32[1,4096]{1,0:T(1,128)} %bitcast.13, bf16[30,110]{1,0:T(8,128)(2,1)} %lift_hbm.1, f32[4,10]{1,0:T(4,128)} %transfer_ref.1), custom_call_target="tpu_custom_call" | custom-call | tf_op jit(solution)/shard_map/pallas_call | solution.py:351
  8.2 0.0 copy-start.1
  8.2 25.2 %all_to_all.10.msg_ref = f32[128,8,128]{2,1,0:T(8,128)S(1)} all-to-all(f32[128,8,128]{2,1,0:T(8,128)} %get-tuple-element.13), channel_id=1, replica_groups=mesh['grp'=4,'dev'=32] {'grp','dev'}, dimensions={0} | all-to-all | bytes 1048576 | tf_op jit(solution)/shard_map/all_to_all | solution.py:393
  33.4 0.0 copy-done
  33.4 0.0 copy-done.1
  33.4 11.2 %shard_map.105 = (f32[12,64,256]{2,1,0:T(8,128)S(1)}, f32[64,256]{1,0:T(8,128)S(1)}, f32[64,256]{1,0:T(8,128)S(1)}, f32[64,128]{1,0:T(8,128)S(1)}) custom-call(f32[128,8,128]{2,1,0:T(8,128)S(1)} %all_to_all.10.msg_ref, f32[12,64,256]{2,1,0:T(8,128)S(1)} %bitcast.6, f32[64,256]{1,0:T(8,128)S(1)} %copy-done.1), custom_call_target="tpu_custom_call" | custom-call | tf_op jit(solution)/shard_map/pallas_call | solution.py:351
  44.6 0.9 collective-permute-start
  45.6 0.9 collective-permute-start.1
  46.4 1.9 %collective-permute-done.from_east_ref = f32[64,256]{1,0:T(8,128)S(1)} collective-permute-done((f32[64,256]{1,0:T(8,128)S(1)}, f32[64,256]{1,0:T(8,128)S(1)}, u32[]{:S(2)}, u32[]{:S(2)}) %collective-permute-start) | collective-permute-done | bytes 65568 | tf_op jit(solution)/shard_map/ppermute | solution.py:372
  48.4 0.0 collective-permute-done.1.from_west_ref
  48.4 0.0 copy-start.5
  48.4 1.7 %shard_map.106 = (f32[25,64,128]{2,1,0:T(8,128)S(1)}, f32[27,8,256]{2,1,0:T(8,128)S(1)}, f32[27,8,256]{2,1,0:T(8,128)S(1)}) custom-call(f32[12,64,256]{2,1,0:T(8,128)S(1)} %get-tuple-element.14.load_ref, f32[12,64,256]{2,1,0:T(8,128)S(1)} %bitcast.7, f32[64,256]{1,0:T(8,128)S(1)} %copy-done.1, f32[64,256]{1,0:T(8,128)S(1)} %collective-permute-done.from_east_ref, ...), custom_call_target="tpu_custom_call" | custom-call | tf_op jit(solution)/shard_map/pallas_call | solution.py:351
  50.1 0.6 collective-permute-start.2
  50.7 1.0 collective-permute-start.3
  51.7 0.0 copy-done.5
  51.7 1.8 %shard_map.107.mat_ref = bf16[192,192]{1,0:T(8,128)(2,1)S(1)} custom-call(f32[12,12]{1,0:T(8,128)S(1)} %copy-done.5), custom_call_target="tpu_custom_call" | custom-call | tf_op jit(solution)/shard_map/pallas_call | solution.py:351
  53.4 1.5 %collective-permute-done.2.south_ref = f32[27,8,256]{2,1,0:T(8,128)S(1)} collective-permute-done((f32[27,8,256]{2,1,0:T(8,128)S(1)}, f32[27,8,256]{2,1,0:T(8,128)S(1)}, u32[]{:S(2)}, u32[]{:S(2)}) %collective-permute-start.2) | collective-permute-done | bytes 221216 | tf_op jit(solution)/shard_map/ppermute | solution.py:372
  55.0 1.7 %collective-permute-done.3.north_ref = f32[27,8,256]{2,1,0:T(8,128)S(1)} collective-permute-done((f32[27,8,256]{2,1,0:T(8,128)S(1)}, f32[27,8,256]{2,1,0:T(8,128)S(1)}, u32[]{:S(2)}, u32[]{:S(2)}) %collective-permute-start.3) | collective-permute-done | bytes 221216 | tf_op jit(solution)/shard_map/ppermute | solution.py:372
  56.7 15.8 %shard_map.108 = (f32[12,64,256]{2,1,0:T(8,128)}, f32[128,8,128]{2,1,0:T(8,128)S(1)}) custom-call(f32[12,64,256]{2,1,0:T(8,128)S(1)} %get-tuple-element.14.load_ref, f32[12,64,256]{2,1,0:T(8,128)S(1)} %bitcast.8, f32[64,256]{1,0:T(8,128)S(1)} %copy-done.1, f32[25,64,128]{2,1,0:T(8,128)S(1)} %get-tuple-element.17.side_ref, ...), custom_call_target="tpu_custom_call" | custom-call | tf_op jit(solution)/shard_map/pallas_call | solution.py:351
  72.5 0.0 copy-start.2
  72.5 0.0 copy-start.3
  72.5 0.0 copy-start.4
  72.5 22.9 %all_to_all.11.ret_ref = f32[128,8,128]{2,1,0:T(8,128)S(1)} all-to-all(f32[128,8,128]{2,1,0:T(8,128)S(1)} %get-tuple-element.22), channel_id=1, replica_groups=mesh['grp'=4,'dev'=32] {'grp','dev'}, dimensions={0} | all-to-all | bytes 1048576 | tf_op jit(solution)/shard_map/all_to_all | solution.py:429
  95.4 0.0 copy-done.2
  95.4 0.0 copy-done.3
  95.4 0.0 copy-done.4
  95.4 3.9 %shard_map.109 = f32[10,3,4096]{2,1,0:T(4,128)} custom-call(f32[128,8,128]{2,1,0:T(8,128)S(1)} %all_to_all.11.ret_ref, s32[1,4096]{1,0:T(1,128)S(1)} %bitcast.10, f32[1,4096]{1,0:T(1,128)S(1)} %copy-done.3, f32[4,10]{1,0:T(4,128)S(1)} %copy-done.4), custom_call_target="tpu_custom_call" | custom-call | tf_op jit(solution)/shard_map/pallas_call | solution.py:351
Async XLA Ops:
  0.6 32.8 %copy-start = (f32[4,3,64,256]{3,2,1,0:T(8,128)S(1)}, f32[4,3,64,256]{3,2,1,0:T(8,128)}, u32[]{:S(2)}) copy-start(f32[4,3,64,256]{3,2,1,0:T(8,128)} %param.17) | copy-start | bytes 2359300
  8.2 25.2 %copy-start.1 = (f32[64,256]{1,0:T(8,128)S(1)}, f32[64,256]{1,0:T(8,128)}, u32[]{:S(2)}) copy-start(f32[64,256]{1,0:T(8,128)} %scale_ref.5) | copy-start | bytes 196612
  44.6 3.8 %collective-permute-start = (f32[64,256]{1,0:T(8,128)S(1)}, f32[64,256]{1,0:T(8,128)S(1)}, u32[]{:S(2)}, u32[]{:S(2)}) collective-permute-start(f32[64,256]{1,0:T(8,128)S(1)} %get-tuple-element.15), channel_id=1, source_target_pairs={{0,31},{1,0},{2,1},{3,2},{4,3},{5,4},{6,5},{7,6},{8,7},{9,8},{10,9... | collective-permute-start | bytes 196616 | tf_op jit(solution)/shard_map/ppermute | solution.py:372
  45.6 2.8 %collective-permute-start.1 = (f32[64,256]{1,0:T(8,128)S(1)}, f32[64,256]{1,0:T(8,128)S(1)}, u32[]{:S(2)}, u32[]{:S(2)}) collective-permute-start(f32[64,256]{1,0:T(8,128)S(1)} %get-tuple-element.16), channel_id=1, source_target_pairs={{0,1},{1,2},{2,3},{3,4},{4,5},{5,6},{6,7},{7,8},{8,9},{9,10},{10,1... | collective-permute-start | bytes 196616 | tf_op jit(solution)/shard_map/ppermute | solution.py:372
  48.4 3.3 %copy-start.5 = (f32[12,12]{1,0:T(8,128)S(1)}, f32[12,12]{1,0:T(8,128)}, u32[]{:S(2)}) copy-start(f32[12,12]{1,0:T(8,128)} %stiff_ref.1) | copy-start | bytes 1732
  50.1 4.9 %collective-permute-start.2 = (f32[27,8,256]{2,1,0:T(8,128)S(1)}, f32[27,8,256]{2,1,0:T(8,128)S(1)}, u32[]{:S(2)}, u32[]{:S(2)}) collective-permute-start(f32[27,8,256]{2,1,0:T(8,128)S(1)} %get-tuple-element.18), channel_id=1, source_target_pairs={{0,96},{32,0},{64,32},{96,64},{1,97},{33,1},{65,33},{97,65},{2,98}... | collective-permute-start | bytes 663560 | tf_op jit(solution)/shard_map/ppermute | solution.py:372
  50.7 6.0 %collective-permute-start.3 = (f32[27,8,256]{2,1,0:T(8,128)S(1)}, f32[27,8,256]{2,1,0:T(8,128)S(1)}, u32[]{:S(2)}, u32[]{:S(2)}) collective-permute-start(f32[27,8,256]{2,1,0:T(8,128)S(1)} %get-tuple-element.19), channel_id=1, source_target_pairs={{0,32},{32,64},{64,96},{96,0},{1,33},{33,65},{65,97},{97,1},{2,34}... | collective-permute-start | bytes 663560 | tf_op jit(solution)/shard_map/ppermute | solution.py:372
  72.5 23.0 %copy-start.2 = (s32[4096,1]{0,1:T(1,128)S(1)}, s32[4096,1]{0,1:T(1,128)}, u32[]{:S(2)}) copy-start(s32[4096,1]{0,1:T(1,128)} %param.9) | copy-start | bytes 49156
  72.5 23.0 %copy-start.3 = (f32[1,4096]{1,0:T(1,128)S(1)}, f32[1,4096]{1,0:T(1,128)}, u32[]{:S(2)}) copy-start(f32[1,4096]{1,0:T(1,128)} %get-tuple-element.23.rank_ref) | copy-start | bytes 49156
  72.5 23.0 %copy-start.4 = (f32[4,10]{1,0:T(4,128)S(1)}, f32[4,10]{1,0:T(4,128)}, u32[]{:S(2)}) copy-start(f32[4,10]{1,0:T(4,128)} %transfer_ref.1) | copy-start | bytes 484

commit v4 on v3

v4 whole, which is shorter than its diff:
```python
import functools

import jax
import jax.numpy as jnp
from jax import lax
from jax.experimental import pallas as pl
from jax.experimental.pallas import tpu as pltpu
from jax.sharding import PartitionSpec as P

SWEEPS = 8
WEIGHT = 2.2
HIGHEST = lax.Precision.HIGHEST
F32 = jnp.float32
BF16 = jnp.bfloat16
I32 = jnp.int32

OWNERS = 128
CAP = 64
COLS = 256
ROWS = 64
PAD_R = 80
PAD_C = 384
FACES = 4096
CHUNK = 256
STEP = 2048
HALF = 32
PLANES = 25
LIMIT = 60
NT = (((1,), (1,)), ((), ()))


def iota(shape, dim):
    return lax.broadcasted_iota(I32, shape, dim)


def dot(a, b):
    return jnp.dot(a, b, preferred_element_type=F32)


def dot_nt(a, b):
    return lax.dot_general(a, b, NT, preferred_element_type=F32)


def exact(a, b):
    return jnp.dot(a, b, precision=HIGHEST, preferred_element_type=F32)


def one_hot(flag):
    return flag.astype(F32).astype(BF16)


def split(x):
    high = x.astype(BF16)
    return high, (x - high.astype(F32)).astype(BF16)


def hot(flag):
    return jnp.where(flag, jnp.ones((), BF16), jnp.zeros((), BF16))


def spread_row(row):
    return jnp.broadcast_to(row, (16, row.shape[1])).astype(BF16)


def hot_rows(row, count):
    wide = spread_row(row)
    step = iota((16, row.shape[1]), 0).astype(F32).astype(BF16)
    return [hot(step == wide - 16.0 * k) for k in range(count // 16)]


def quarters(owner, quarter):
    pieces = hot_rows(owner, OWNERS)
    wide = spread_row(quarter)
    for q in range(4):
        here = hot(wide == q)
        for k, piece in enumerate(pieces):
            yield q * OWNERS + 16 * k, piece * here


def face_kernel(owner_hbm, elem_hbm, state_hbm, scale_hbm, lift_hbm, transfer_hbm, prev_hbm, shell_hbm,
                msg_ref, rank_ref, strip_ref,
                owner_ref, elem_ref, state_ref, scale_ref, lift_ref, transfer_ref, x_ref, hot_ref, acc_ref, sems):
    copies = [
        pltpu.make_async_copy(src, dst, sems.at[i])
        for i, (src, dst) in enumerate((
            (owner_hbm, owner_ref), (transfer_hbm, transfer_ref), (lift_hbm, lift_ref),
            (elem_hbm, elem_ref), (scale_hbm, scale_ref), (state_hbm, state_ref),
            (prev_hbm.at[:, 0:8, :], strip_ref.at[0, 0:12]),
            (prev_hbm.at[:, ROWS - 8:ROWS, :], strip_ref.at[1, 0:12]),
            (shell_hbm.at[0:8, :], strip_ref.at[0, 12]),
            (shell_hbm.at[ROWS - 8:ROWS, :], strip_ref.at[1, 12]),
        ))
    ]
    for copy in copies:
        copy.start()
    x_ref[...] = jnp.zeros_like(x_ref)
    acc_ref[...] = jnp.zeros_like(acc_ref)
    before = iota((CHUNK, 2 * CHUNK), 0)
    upper = iota((CHUNK, 2 * CHUNK), 1)
    upper = one_hot((before < upper) | (upper >= CHUNK))
    copies[0].wait()

    def ranks(i, base):
        part = pl.ds(pl.multiple_of(i * CHUNK, CHUNK), CHUNK)
        mine = (iota((OWNERS, CHUNK), 0) == owner_ref[:, part]).astype(F32)
        counts = dot(mine.astype(BF16), upper)
        rank_ref[:, part] = jnp.sum(mine * (counts[:, :CHUNK] + base), axis=0, keepdims=True)
        return base + counts[:, CHUNK:]

    lax.fori_loop(0, FACES // CHUNK, ranks, jnp.zeros((OWNERS, CHUNK), F32), unroll=True)
    for copy in copies[1:6]:
        copy.wait()
    spread = jnp.concatenate(
        [jnp.pad(transfer_ref[...], ((0, 0), (10 * c, 20 - 10 * c))) for c in range(3)], axis=0
    )
    weights = exact(spread, lift_ref[...].astype(F32))
    high, low = split(weights)

    def body(i, carry):
        part = pl.ds(pl.multiple_of(i * STEP, STEP), STEP)
        rank = rank_ref[:, part].astype(I32)
        for at, piece in quarters(owner_ref[:, part].astype(F32), (rank >> 4).astype(F32)):
            hot_ref[at:at + 16, :] = piece
        place, = hot_rows((rank & 15).astype(F32), 16)
        state = state_ref[:, part]
        load = (dot(high, state) + dot(low, state)) * scale_ref[:, part]
        marker = (elem_ref[:, part] + 1).astype(F32)
        for c in range(13):
            at = 4 * (c % 3) + c // 3
            row = load[at:at + 1] if c < 12 else marker
            top, rest = split(jnp.broadcast_to(row, (16, STEP)))
            x_ref[16 * c:16 * c + 16, :STEP] = place * top
            x_ref[16 * c:16 * c + 16, STEP:] = place * rest
        acc_ref[...] += dot_nt(hot_ref[...], x_ref[:, :STEP]) + dot_nt(hot_ref[...], x_ref[:, STEP:])
        return carry

    lax.fori_loop(0, FACES // STEP, body, 0)
    for q in range(4):
        for t in range(2):
            msg_ref[:, 2 * q + t, :] = acc_ref[q * OWNERS:(q + 1) * OWNERS, 128 * t:128 * t + 128]
    for copy in copies[6:]:
        copy.wait()


def places(marker):
    element = marker.astype(I32) - 1
    row, col = element >> 8, (element & 255).astype(F32)
    pieces = hot_rows(col, COLS)
    wide = spread_row(row.astype(F32))
    low, high = hot(wide < HALF), hot(wide >= HALF)
    columns = [piece * low for piece in pieces] + [piece * high for piece in pieces]
    return (row & (HALF - 1)).astype(F32), columns


def build(turned_ref, mark_ref, q, count, number, a_ref, col_ref):
    for h in range(2):
        markers = mark_ref[pl.ds(pl.multiple_of(16 * q + 8 * h, 8), 8), :]
        for k in range(8):
            lanes = slice(1024 * h + 128 * k, 1024 * h + 128 * k + 128)
            element = markers[k:k + 1].astype(I32) - 1
            for b, piece in enumerate(hot_rows((element & 255).astype(F32), COLS)):
                col_ref[16 * b:16 * b + 16, lanes] = piece
            row_hot = hot_rows(number(element >> 8).astype(F32), count)
            for part in range(2):
                for c in range(12):
                    first = 16 * (c % 8) + 8 * h
                    values = turned_ref[part, 2 * q + c // 8, first:first + 8, :]
                    value = spread_row(values[k:k + 1])
                    at = (12 * part + c) * count
                    for b, piece in enumerate(row_hot):
                        a_ref[at + 16 * b:at + 16 * b + 16, lanes] = piece * value


def edge_scatter_kernel(msg_ref, strip_ref, north_ref, south_ref, turned_ref, mark_ref, a_ref, col_ref, acc_ref):
    north_ref[12:PLANES] = strip_ref[0]
    south_ref[12:PLANES] = strip_ref[1]
    acc_ref[...] = jnp.zeros_like(acc_ref)
    for j in range(8):
        turned = jnp.transpose(msg_ref[:, j, :])
        if j % 2:
            mark_ref[8 * j - 8:8 * j + 8, :] = turned[64:80]
        turned = turned * (1.0 / WEIGHT)
        top = turned.astype(BF16).astype(F32)
        turned_ref[0, j] = top
        turned_ref[1, j] = turned - top

    def body(q, carry):
        build(
            turned_ref, mark_ref, q, 16,
            lambda row: jnp.where(row < 8, row, jnp.where(row >= ROWS - 8, row - (ROWS - 16), -1)), a_ref, col_ref,
        )
        acc_ref[...] += dot_nt(a_ref[...], col_ref[...])
        return carry

    lax.fori_loop(0, 4, body, 0)
    for c in range(12):
        strip = acc_ref[16 * c:16 * c + 16] + acc_ref[192 + 16 * c:208 + 16 * c]
        north_ref[c] = strip[0:8]
        south_ref[c] = strip[8:16]


INNER = ROWS - 16


def scatter_kernel(turned_ref, mark_ref, north_ref, south_ref, load_ref, a_ref, col_ref, acc_ref):
    acc_ref[...] = jnp.zeros_like(acc_ref)

    def body(q, carry):
        build(turned_ref, mark_ref, q, INNER, lambda row: row - 8, a_ref, col_ref)
        acc_ref[...] += dot_nt(a_ref[...], col_ref[...])
        return carry

    lax.fori_loop(0, 4, body, 0)
    for c in range(12):
        load_ref[c, 0:8, :] = north_ref[c]
        load_ref[c, 8:8 + INNER, :] = acc_ref[INNER * c:INNER * c + INNER] + acc_ref[INNER * (12 + c):INNER * (13 + c)]
        load_ref[c, ROWS - 8:ROWS, :] = south_ref[c]


def matrix_kernel(stiff_ref, mat_ref):
    eye = (iota((12, 12), 0) == iota((12, 12), 1)).astype(F32)
    approx = eye / 5.0
    rest = eye - exact(stiff_ref[...], approx)
    for turn in range(8):
        approx = approx + exact(approx, rest)
        if turn < 7:
            rest = exact(rest, rest)
    tall = (iota((96, 12), 0) // 8 == iota((96, 12), 1)).astype(F32)
    wide = (iota((12, 96), 1) // 8 == iota((12, 96), 0)).astype(F32)
    big = exact(exact(tall, approx * WEIGHT), wide)
    big = jnp.where(iota((96, 96), 0) % 8 == iota((96, 96), 1) % 8, big, 0.0)
    high, low = split(big)
    mat_ref[0:96, :] = jnp.concatenate([high, high], axis=1)
    mat_ref[96:192, :] = jnp.concatenate([low, jnp.zeros_like(low)], axis=1)


def columns_kernel(load_ref, prev_ref, scale_ref, south_ref, north_ref, west_ref, east_ref):
    for at, rows, pick in (
        (0, ROWS, lambda p, lanes: scale_ref[:, lanes] if p == 24 else load_ref[p, :, lanes] if p < 12 else prev_ref[p - 12, :, lanes]),
        (ROWS, 8, lambda p, lanes: south_ref[p, :, lanes]),
        (ROWS + 8, 8, lambda p, lanes: north_ref[p, :, lanes]),
    ):
        group = iota((rows, 128), 1) // 8
        for tile in range(2):
            west = jnp.zeros((rows, 128), F32)
            east = jnp.zeros((rows, 128), F32)
            for p in range(16 * tile, min(PLANES, 16 * tile + 16)):
                i = p % 16
                low = pick(p, slice(0, 128))
                high = pick(p, slice(128, 256))
                west = jnp.where(group == i, pltpu.roll(low, 8 * i, 1) if i else low, west)
                east = jnp.where(group == i, pltpu.roll(high, (8 * i + 8) % 128, 1), east)
            west_ref[at:at + rows, 128 * tile:128 * tile + 128] = west
            east_ref[at:at + rows, 128 * tile:128 * tile + 128] = east


def row_ok(shape):
    grp = lax.axis_index("grp")
    row = iota(shape, 0)
    return (row < ROWS) | ((row < ROWS + 8) & (grp < lax.axis_size("grp") - 1)) | ((row >= ROWS + 8) & (grp > 0))


def settle(pad_ref, lanes, ok):
    pad_ref[24, :, lanes] = jnp.where(ok, 1.0 / jnp.where(ok, pad_ref[24, :, lanes], 1.0), 0.0)
    for c in range(12):
        pad_ref[12 + c, :, lanes] = jnp.where(ok, pad_ref[12 + c, :, lanes], 0.0)


def fill_kernel(load_ref, prev_ref, scale_ref, south_ref, north_ref, pad_ref):
    for p in range(PLANES):
        pad_ref[p, 0:ROWS, 0:COLS] = scale_ref[...] if p == 24 else load_ref[p] if p < 12 else prev_ref[p - 12]
        pad_ref[p, ROWS:ROWS + 8, 0:COLS] = south_ref[p]
        pad_ref[p, ROWS + 8:PAD_R, 0:COLS] = north_ref[p]
        pad_ref[p, :, COLS:PAD_C] = jnp.zeros((PAD_R, PAD_C - COLS), F32)
    settle(pad_ref, slice(0, COLS), row_ok((PAD_R, COLS)))


def sweep_kernel(pad_in, from_east_ref, from_west_ref, mat_ref, mark_ref,
                 out_ref, ret_ref, pad_ref, x_ref, hl_ref, turned_ref):
    del pad_in
    lane = iota((PAD_R, 128), 1)
    for p in range(PLANES):
        tile = slice(128 * (p // 16), 128 * (p // 16) + 128)
        low = pltpu.roll(from_east_ref[:, tile], (128 - 8 * (p % 16)) % 128, 1)
        high = pltpu.roll(from_west_ref[:, tile], (248 - 8 * (p % 16)) % 128, 1)
        pad_ref[p, :, COLS:PAD_C] = jnp.where(lane < 8, low, jnp.where(lane >= 120, high, 0.0))
    dev = lax.axis_index("dev")
    ok = row_ok((PAD_R, 128)) & (
        ((lane < 8) & (dev < lax.axis_size("dev") - 1)) | ((lane >= 120) & (dev > 0))
    )
    settle(pad_ref, slice(COLS, PAD_C), ok)
    along = ((1, 1), (0, PAD_C - 1), (3, 1), (2, PAD_C - 1))
    across = ((2, 1), (3, 1), (0, PAD_R - 1), (1, PAD_R - 1))

    def right_side(at):
        n, c = divmod(at, 3)
        return (
            pad_ref[at]
            + pltpu.roll(pad_ref[12 + 3 * along[n][0] + c], along[n][1], 1)
            + pltpu.roll(pad_ref[12 + 3 * across[n][0] + c], across[n][1], 0)
        )

    def sweep(turn, carry):
        for at in range(0, 12, 2):
            first, second = right_side(at), right_side(at + 1)
            for b in range(PAD_R // 8):
                rows = slice(8 * b, 8 * b + 8)
                top, rest = split(jnp.concatenate([first[rows], second[rows]], axis=0))
                lanes = slice(PAD_C * (b % 2), PAD_C * (b % 2) + PAD_C)
                x_ref[b // 2, 8 * at:8 * at + 16, lanes] = top
                x_ref[b // 2, 96 + 8 * at:96 + 8 * at + 16, lanes] = rest
        for b in range(PAD_R // 16):
            solved = dot(mat_ref[...], x_ref[b])
            for h in range(2):
                rows = slice(16 * b + 8 * h, 16 * b + 8 * h + 8)
                lanes = slice(PAD_C * h, PAD_C * h + PAD_C)
                factor = pad_ref[24, rows]
                for at in range(12):
                    pad_ref[12 + at, rows] = (
                        solved[8 * at:8 * at + 8, lanes] + solved[96 + 8 * at:96 + 8 * at + 8, lanes]
                    ) * factor
        return carry

    lax.fori_loop(0, SWEEPS, sweep, 0, unroll=2)
    for c in range(12):
        value = pad_ref[12 + c, 0:ROWS, 0:COLS]
        out_ref[c] = value
        top, rest = split(value)
        for b in range(2):
            part = slice(HALF * b, HALF * (b + 1))
            hl_ref[c * HALF:(c + 1) * HALF, COLS * b:COLS * (b + 1)] = top[part]
            hl_ref[c * HALF:(c + 1) * HALF, 512 + COLS * b:512 + COLS * (b + 1)] = rest[part]

    def gather(q, carry):
        markers = mark_ref[pl.ds(pl.multiple_of(16 * q, 16), 16), :]
        row, columns = places(jnp.concatenate([markers[k:k + 1] for k in range(16)], axis=1))
        columns = jnp.concatenate(columns, axis=0)
        found = dot(hl_ref[:, :512], columns) + dot(hl_ref[:, 512:], columns)
        here = iota((HALF, 2048), 0).astype(F32) == row
        for c in range(12):
            value = jnp.sum(jnp.where(here, found[c * HALF:(c + 1) * HALF], 0.0), axis=0, keepdims=True)
            value = jnp.concatenate([value[:, 128 * k:128 * k + 128] for k in range(16)], axis=0)
            turned_ref[2 * q + c // 8, 16 * (c % 8):16 * (c % 8) + 16, :] = value
        return carry

    lax.fori_loop(0, 4, gather, 0)
    for j in range(8):
        ret_ref[:, j, :] = jnp.transpose(turned_ref[j])


def return_kernel(ret_ref, owner_ref, rank_ref, transfer_ref, out_ref, l_ref, hot_ref, faces_ref, sems):
    for q in range(4):
        for t in range(2):
            count = 128 if t == 0 else 64
            top, rest = split(jnp.transpose(ret_ref[:, 2 * q + t, :])[:count])
            l_ref[128 * t:128 * t + count, 128 * q:128 * q + 128] = top
            l_ref[128 * t:128 * t + count, 512 + 128 * q:512 + 128 * q + 128] = rest
    pick = (iota((80, 10), 0) // 8 == iota((80, 10), 1)).astype(F32)
    spread = lax.dot_general(pick, transfer_ref[...], NT, precision=HIGHEST, preferred_element_type=F32)
    spread = exact(spread, (iota((4, 16), 1) // 3 == iota((4, 16), 0)).astype(F32))
    spread = jnp.where(iota((80, 16), 0) % 8 == iota((80, 16), 1) % 3, spread, 0.0)
    high, low = split(spread)
    copies = []
    for i in range(FACES // STEP):
        part = slice(i * STEP, (i + 1) * STEP)
        rank = rank_ref[:, part].astype(I32)
        for at, piece in quarters(owner_ref[:, part].astype(F32), (rank >> 4).astype(F32)):
            hot_ref[at:at + 16, :] = piece
        found = dot(l_ref[:, :512], hot_ref[...]) + dot(l_ref[:, 512:], hot_ref[...])
        here = iota((16, STEP), 0) == (rank & 15)
        node = jnp.concatenate(
            [jnp.sum(jnp.where(here, found[16 * c:16 * c + 16], 0.0), axis=0, keepdims=True) for c in range(12)]
            + [jnp.zeros((4, STEP), F32)],
            axis=0,
        )
        top, rest = split(node)
        result = dot(high, top) + (dot(high, rest) + dot(low, top))
        for k in range(10):
            faces_ref[k, :, part] = result[8 * k:8 * k + 3]
        copy = pltpu.make_async_copy(faces_ref.at[:, :, part], out_ref.at[:, :, part], sems.at[i])
        copy.start()
        copies.append(copy)
    for copy in copies:
        copy.wait()


VMEM = pl.BlockSpec(memory_space=pltpu.VMEM)
HBM = pl.BlockSpec(memory_space=pl.ANY)


def call(kernel, outs, scratch, *args, hbm=(), out_specs=None, limit=28, alias=None):
    single = not isinstance(outs, (list, tuple))
    shapes = [outs] if single else list(outs)
    result = pl.pallas_call(
        kernel,
        out_shape=shapes,
        in_specs=[HBM if i in hbm else VMEM for i in range(len(args))],
        out_specs=out_specs or [VMEM] * len(shapes),
        scratch_shapes=scratch,
        input_output_aliases=alias or {},
        compiler_params=pltpu.CompilerParams(vmem_limit_bytes=limit * 1024 * 1024),
    )(*args)
    return result[0] if single else result


def arr(*shape, dtype=F32):
    return jax.ShapeDtypeStruct(shape, dtype)


def ring(axis, step):
    count = lax.axis_size(axis)
    return [(i, (i + step) % count) for i in range(count)]


def shift_pair(toward_low, toward_high, axis):
    return lax.ppermute(toward_low, axis, ring(axis, -1)), lax.ppermute(toward_high, axis, ring(axis, 1))


def local(face_owner, face_element, element_state, lift, face_scale, transfer, stiffness_ref, element_scale, displacement_prev):
    owner = face_owner.reshape(1, FACES)
    element = face_element.reshape(1, FACES)
    scale = face_scale.reshape(1, FACES)
    prev = displacement_prev.reshape(12, ROWS, COLS)

    msg, rank, strip = call(
        face_kernel,
        [arr(OWNERS, 8, 128), arr(1, FACES), arr(2, 13, 8, COLS)],
        [
            pltpu.VMEM((1, FACES), I32), pltpu.VMEM((1, FACES), I32), pltpu.VMEM((110, FACES), BF16),
            pltpu.VMEM((1, FACES), F32), pltpu.VMEM((30, 110), BF16), pltpu.VMEM((4, 10), F32),
            pltpu.VMEM((256, 2 * STEP), BF16), pltpu.VMEM((4 * OWNERS, STEP), BF16), pltpu.VMEM((4 * OWNERS, 256), F32),
            pltpu.SemaphoreType.DMA((10,)),
        ],
        owner, element, element_state, scale, lift, transfer, prev, element_scale,
        hbm=(0, 1, 2, 3, 4, 5, 6, 7), limit=LIMIT,
    )
    got = lax.all_to_all(msg, ("grp", "dev"), split_axis=0, concat_axis=0)
    mat = call(matrix_kernel, arr(192, 192, dtype=BF16), [], stiffness_ref)

    north, south, turned, mark = call(
        edge_scatter_kernel,
        [arr(PLANES, 8, COLS), arr(PLANES, 8, COLS), arr(2, 8, 128, 128), arr(64, 128)],
        [
            pltpu.VMEM((24 * 16, 2048), BF16),
            pltpu.VMEM((COLS, 2048), BF16),
            pltpu.VMEM((24 * 16, COLS), F32),
        ],
        got, strip,
    )
    below, above = shift_pair(north, south, "grp")
    load = call(
        scatter_kernel,
        arr(12, ROWS, COLS),
        [
            pltpu.VMEM((24 * INNER, 2048), BF16),
            pltpu.VMEM((COLS, 2048), BF16),
            pltpu.VMEM((24 * INNER, COLS), F32),
        ],
        turned, mark, north, south,
    )
    west, east = call(
        columns_kernel, [arr(PAD_R, 256), arr(PAD_R, 256)], [], load, prev, element_scale, below, above
    )
    from_east, from_west = shift_pair(west, east, "dev")
    pad = call(fill_kernel, arr(PLANES, PAD_R, PAD_C), [], load, prev, element_scale, below, above)

    shell, back, _ = call(
        sweep_kernel,
        [arr(12, ROWS, COLS), arr(OWNERS, 8, 128), arr(PLANES, PAD_R, PAD_C)],
        [
            pltpu.VMEM((PAD_R // 16, 192, 2 * PAD_C), BF16),
            pltpu.VMEM((12 * HALF, 1024), BF16),
            pltpu.VMEM((8, 128, 128), F32),
        ],
        pad, from_east, from_west, mat, mark,
        alias={0: 2},
    )
    returned = lax.all_to_all(back, ("grp", "dev"), split_axis=0, concat_axis=0)
    faces = call(
        return_kernel,
        arr(10, 3, FACES),
        [
            pltpu.VMEM((192, 1024), BF16),
            pltpu.VMEM((4 * OWNERS, STEP), BF16),
            pltpu.VMEM((10, 3, FACES), F32),
            pltpu.SemaphoreType.DMA((FACES // STEP,)),
        ],
        returned, owner, rank, transfer,
        out_specs=[HBM],
    )
    return shell.reshape(4, 3, ROWS, COLS), jnp.transpose(faces, (1, 0, 2))


def solution(mesh):
    placed = (
        P(("grp", "dev"), None),
        P(("grp", "dev")),
        P(None, ("grp", "dev")),
        P(),
        P(("grp", "dev")),
        P(),
        P(),
        P("grp", "dev"),
        P(None, None, "grp", "dev"),
    )
    return jax.shard_map(
        local,
        mesh=mesh,
        in_specs=placed,
        out_specs=(P(None, None, "grp", "dev"), P(None, None, ("grp", "dev"))),
        check_vma=False,
    )
```

time: 99.8 us -> 91.1 us (0.913)
  waiting for transfers between devices: 5.21 us -> 0.01 us
  Pallas kernels: 41.9 us -> 38.4 us
  blocking collectives: 48.1 us -> 47.1 us
    pallas_call x6 -> x8, Pallas kernels: 41.9 us -> 38.4 us  [call(): pl.pallas_call(kernel, out_shape=shapes, in_specs=[HBM if i in hbm else V...]
    ppermute x2, waiting for transfers between devices: 3.49 us -> 0.01 us  [shift_pair(): lax.ppermute(toward_low, axis, ring(axis, -1))]
    ppermute x2, waiting for transfers between devices: 1.72 us -> 0.01 us  [shift_pair(): lax.ppermute(toward_high, axis, ring(axis, 1))]
    all_to_all x1, blocking collectives: 22.9 us -> 21.8 us  [local(): returned = lax.all_to_all(back, ('grp', 'dev'), split_axis=0, concat_axis=0)]
  transfers between devices with their start and end apart: 4 -> 4, of which waited for: 3 -> 0; matrix products, arithmetic and copies ran while one was open for 0% -> 0% of each run, Pallas kernels for 2% -> 9%
where the time goes in v4:
time: 91.1 us; the launch traced here: 90.9 us
  blocking collectives  47.1 us (52%)
  Pallas kernels  38.4 us (42%)
  starting transfers between devices  3.48 us (4%)
  local copies, waits for them, and re-layouts  0.96 us (1%)
  between operations  0.94 us (1%)
    pallas_call x8, Pallas kernels, call(): pl.pallas_call(kernel, out_shape=shapes, in_specs=[HBM if i in hbm else V...  38.4 us
    all_to_all x1, blocking collectives, local(): got = lax.all_to_all(msg, ('grp', 'dev'), split_axis=0, concat_axis=0)  25.2 us
    all_to_all x1, blocking collectives, local(): returned = lax.all_to_all(back, ('grp', 'dev'), split_axis=0, concat_axis=0)  21.8 us
    ppermute x2, starting transfers between devices, shift_pair(): lax.ppermute(toward_low, axis, ring(axis, -1))  2.08 us
  transfers between devices with their start and end apart: 4, of which 0 were waited for; matrix products, arithmetic and copies ran while one was open for 0% of the time, Pallas kernels for 9%

profile of v4, /device:TPU:1, one launch (start us, length us, event | category | flops | bytes accessed | tf_op | source)
XLA Modules:
  0.0 90.9 jit_solution(9856630875234311243)
XLA Ops:
  0.6 0.0 copy-start.1
  0.6 0.0 copy-start
  0.7 6.4 %shard_map.104 = (f32[128,8,128]{2,1,0:T(8,128)}, f32[1,4096]{1,0:T(1,128)}, f32[2,13,8,256]{3,2,1,0:T(8,128)}) custom-call(s32[1,4096]{1,0:T(1,128)} %bitcast.9, s32[1,4096]{1,0:T(1,128)} %bitcast.12, bf16[110,4096]{1,0:T(8,128)(2,1)} %state_hbm.1, f32[1,4096]{1,0:T(1,128)} %bitcast.13, bf16[30,110]{1,0:T(8,128)(2,1)} %lift_hbm.1, f32[4,10]{1,0:T(4,128)} %transfer_ref.1, ...), custom_call_target="tpu_custom_call" | custom-call | tf_op jit(solution)/shard_map/pallas_call | solution.py:394
  7.1 0.0 copy-start.5
  7.1 25.2 %all_to_all.10.msg_ref = f32[128,8,128]{2,1,0:T(8,128)S(1)} all-to-all(f32[128,8,128]{2,1,0:T(8,128)} %get-tuple-element.13), channel_id=1, replica_groups=mesh['grp'=4,'dev'=32] {'grp','dev'}, dimensions={0} | all-to-all | bytes 1048576 | tf_op jit(solution)/shard_map/all_to_all | solution.py:437
  32.3 0.0 copy-start.2
  32.3 0.9 %copy-done.2 = f32[2,13,8,256]{3,2,1,0:T(8,128)S(1)} copy-done((f32[2,13,8,256]{3,2,1,0:T(8,128)S(1)}, f32[2,13,8,256]{3,2,1,0:T(8,128)}, u32[]{:S(2)}) %copy-start.2) | copy-done | bytes 213016
  33.3 3.9 %shard_map.105 = (f32[25,8,256]{2,1,0:T(8,128)S(1)}, f32[25,8,256]{2,1,0:T(8,128)S(1)}, f32[2,8,128,128]{3,2,1,0:T(8,128)S(1)}, f32[64,128]{1,0:T(8,128)S(1)}) custom-call(f32[128,8,128]{2,1,0:T(8,128)S(1)} %all_to_all.10.msg_ref, f32[2,13,8,256]{3,2,1,0:T(8,128)S(1)} %copy-done.2), custom_call_target="tpu_custom_call" | custom-call | tf_op jit(solution)/shard_map/pallas_call | solution.py:394
  37.2 0.6 collective-permute-start
  37.7 1.0 %collective-permute-start.1 = (f32[25,8,256]{2,1,0:T(8,128)S(1)}, f32[25,8,256]{2,1,0:T(8,128)S(1)}, u32[]{:S(2)}, u32[]{:S(2)}) collective-permute-start(f32[25,8,256]{2,1,0:T(8,128)S(1)} %get-tuple-element.18.south_ref), channel_id=1, source_target_pairs={{0,32},{32,64},{64,96},{96,0},{1,33},{33,65},{65,97},{97,1},{2,34}... | collective-permute-start | bytes 614408 | tf_op jit(solution)/shard_map/ppermute | solution.py:416
  38.7 6.4 %shard_map.106.load_ref = f32[12,64,256]{2,1,0:T(8,128)S(1)} custom-call(f32[2,8,128,128]{3,2,1,0:T(8,128)S(1)} %get-tuple-element.15.turned_ref, f32[64,128]{1,0:T(8,128)S(1)} %get-tuple-element.16.mark_ref, f32[25,8,256]{2,1,0:T(8,128)S(1)} %get-tuple-element.17.north_ref, f32[25,8,256]{2,1,0:T(8,128)S(1)} %get-tuple-element.18.south_ref), custom_call_target="tpu_custom_call" | custom-call | tf_op jit(solution)/shard_map/pallas_call | solution.py:394
  45.1 0.0 collective-permute-done.south_ref
  45.1 0.0 collective-permute-done.1.north_ref
  45.1 0.0 copy-done.1
  45.1 0.0 copy-done
  45.2 0.6 shard_map.108
  45.7 1.5 %collective-permute-start.2 = (f32[80,256]{1,0:T(8,128)S(1)}, f32[80,256]{1,0:T(8,128)S(1)}, u32[]{:S(2)}, u32[]{:S(2)}) collective-permute-start(f32[80,256]{1,0:T(8,128)S(1)} %get-tuple-element.19), channel_id=1, source_target_pairs={{0,31},{1,0},{2,1},{3,2},{4,3},{5,4},{6,5},{7,6},{8,7},{9,8},{10,9... | collective-permute-start | bytes 245768 | tf_op jit(solution)/shard_map/ppermute | solution.py:416
  47.2 0.4 collective-permute-start.3
  47.7 0.0 copy-done.5
  47.7 1.8 %shard_map.109.mat_ref = bf16[192,192]{1,0:T(8,128)(2,1)S(1)} custom-call(f32[12,12]{1,0:T(8,128)S(1)} %copy-done.5), custom_call_target="tpu_custom_call" | custom-call | tf_op jit(solution)/shard_map/pallas_call | solution.py:394
  49.4 0.2 shard_map.107.pad_in
  49.7 0.0 copy-start.3
  49.7 0.0 copy-start.4
  49.7 0.0 copy-start.6
  49.7 0.0 collective-permute-done.2.from_east_ref
  49.7 0.0 collective-permute-done.3.from_west_ref
  49.7 15.5 %shard_map.110 = (f32[12,64,256]{2,1,0:T(8,128)}, f32[128,8,128]{2,1,0:T(8,128)S(1)}, f32[25,80,384]{2,1,0:T(8,128)S(1)}) custom-call(f32[25,80,384]{2,1,0:T(8,128)S(1)} %shard_map.107.pad_in, f32[80,256]{1,0:T(8,128)S(1)} %collective-permute-done.2.from_east_ref, ...), custom_call_target="tpu_custom_call", output_to_operand_aliasing={{2}: (0, {})} | custom-call | tf_op jit(solution)/shard_map/pallas_call | solution.py:394
  65.2 21.8 %all_to_all.11.ret_ref = f32[128,8,128]{2,1,0:T(8,128)S(1)} all-to-all(f32[128,8,128]{2,1,0:T(8,128)S(1)} %get-tuple-element.22), channel_id=1, replica_groups=mesh['grp'=4,'dev'=32] {'grp','dev'}, dimensions={0} | all-to-all | bytes 1048576 | tf_op jit(solution)/shard_map/all_to_all | solution.py:478
  87.1 0.0 copy-done.3
  87.1 0.0 copy-done.4
  87.1 0.0 copy-done.6
  87.1 3.6 %shard_map.111 = f32[10,3,4096]{2,1,0:T(4,128)} custom-call(f32[128,8,128]{2,1,0:T(8,128)S(1)} %all_to_all.11.ret_ref, s32[1,4096]{1,0:T(1,128)S(1)} %bitcast.10, f32[1,4096]{1,0:T(1,128)S(1)} %copy-done.4, f32[4,10]{1,0:T(4,128)S(1)} %copy-done.6), custom_call_target="tpu_custom_call" | custom-call | tf_op jit(solution)/shard_map/pallas_call | solution.py:394
Async XLA Ops:
  0.6 44.5 %copy-start.1 = (f32[64,256]{1,0:T(8,128)S(1)}, f32[64,256]{1,0:T(8,128)}, u32[]{:S(2)}) copy-start(f32[64,256]{1,0:T(8,128)} %scale_ref.3) | copy-start | bytes 196612
  0.6 44.5 %copy-start = (f32[4,3,64,256]{3,2,1,0:T(8,128)S(1)}, f32[4,3,64,256]{3,2,1,0:T(8,128)}, u32[]{:S(2)}) copy-start(f32[4,3,64,256]{3,2,1,0:T(8,128)} %param.17) | copy-start | bytes 2359300
  7.1 40.6 %copy-start.5 = (f32[12,12]{1,0:T(8,128)S(1)}, f32[12,12]{1,0:T(8,128)}, u32[]{:S(2)}) copy-start(f32[12,12]{1,0:T(8,128)} %stiff_ref.1) | copy-start | bytes 1732
  32.3 0.9 %copy-start.2 = (f32[2,13,8,256]{3,2,1,0:T(8,128)S(1)}, f32[2,13,8,256]{3,2,1,0:T(8,128)}, u32[]{:S(2)}) copy-start(f32[2,13,8,256]{3,2,1,0:T(8,128)} %get-tuple-element.14.strip_ref) | copy-start | bytes 638980
  37.2 7.9 %collective-permute-start = (f32[25,8,256]{2,1,0:T(8,128)S(1)}, f32[25,8,256]{2,1,0:T(8,128)S(1)}, u32[]{:S(2)}, u32[]{:S(2)}) collective-permute-start(f32[25,8,256]{2,1,0:T(8,128)S(1)} %get-tuple-element.17.north_ref), channel_id=1, source_target_pairs={{0,96},{32,0},{64,32},{96,64},{1,97},{33,1},{65,33},{97,65},{2,98}... | collective-permute-start | bytes 614408 | tf_op jit(solution)/shard_map/ppermute | solution.py:416
  37.7 7.4 %collective-permute-start.1 = (f32[25,8,256]{2,1,0:T(8,128)S(1)}, f32[25,8,256]{2,1,0:T(8,128)S(1)}, u32[]{:S(2)}, u32[]{:S(2)}) collective-permute-start(f32[25,8,256]{2,1,0:T(8,128)S(1)} %get-tuple-element.18.south_ref), channel_id=1, source_target_pairs={{0,32},{32,64},{64,96},{96,0},{1,33},{33,65},{65,97},{97,1},{2,34}... | collective-permute-start | bytes 614408 | tf_op jit(solution)/shard_map/ppermute | solution.py:416
  45.7 4.0 %collective-permute-start.2 = (f32[80,256]{1,0:T(8,128)S(1)}, f32[80,256]{1,0:T(8,128)S(1)}, u32[]{:S(2)}, u32[]{:S(2)}) collective-permute-start(f32[80,256]{1,0:T(8,128)S(1)} %get-tuple-element.19), channel_id=1, source_target_pairs={{0,31},{1,0},{2,1},{3,2},{4,3},{5,4},{6,5},{7,6},{8,7},{9,8},{10,9... | collective-permute-start | bytes 245768 | tf_op jit(solution)/shard_map/ppermute | solution.py:416
  47.2 2.5 %collective-permute-start.3 = (f32[80,256]{1,0:T(8,128)S(1)}, f32[80,256]{1,0:T(8,128)S(1)}, u32[]{:S(2)}, u32[]{:S(2)}) collective-permute-start(f32[80,256]{1,0:T(8,128)S(1)} %get-tuple-element.20), channel_id=1, source_target_pairs={{0,1},{1,2},{2,3},{3,4},{4,5},{5,6},{6,7},{7,8},{8,9},{9,10},{10,1... | collective-permute-start | bytes 245768 | tf_op jit(solution)/shard_map/ppermute | solution.py:416
  49.7 37.4 %copy-start.3 = (s32[4096,1]{0,1:T(1,128)S(1)}, s32[4096,1]{0,1:T(1,128)}, u32[]{:S(2)}) copy-start(s32[4096,1]{0,1:T(1,128)} %param.9) | copy-start | bytes 49156
  49.7 37.4 %copy-start.4 = (f32[1,4096]{1,0:T(1,128)S(1)}, f32[1,4096]{1,0:T(1,128)}, u32[]{:S(2)}) copy-start(f32[1,4096]{1,0:T(1,128)} %get-tuple-element.23.rank_ref) | copy-start | bytes 49156
  49.7 37.4 %copy-start.6 = (f32[4,10]{1,0:T(4,128)S(1)}, f32[4,10]{1,0:T(4,128)}, u32[]{:S(2)}) copy-start(f32[4,10]{1,0:T(4,128)} %transfer_ref.1) | copy-start | bytes 484

commit v5 on v4

--- a/solution.py
+++ b/solution.py
@@ -135,9 +135,19 @@
         return carry
 
     lax.fori_loop(0, FACES // STEP, body, 0)
+    lane = iota((OWNERS, 128), 1)
+    marks = jnp.zeros((OWNERS, 128), F32)
+    last = None
     for q in range(4):
-        for t in range(2):
-            msg_ref[:, 2 * q + t, :] = acc_ref[q * OWNERS:(q + 1) * OWNERS, 128 * t:128 * t + 128]
+        mine = slice(q * OWNERS, (q + 1) * OWNERS)
+        msg_ref[:, 0, 128 * q:128 * q + 128] = acc_ref[mine, 0:128]
+        late = acc_ref[mine, 128:256]
+        marks = jnp.where(lane // 16 == q, pltpu.roll(late, 64 + 16 * q, 1), marks)
+        if q % 2:
+            at = 512 + 128 * (q // 2)
+            msg_ref[:, 0, at:at + 128] = jnp.where(lane < 64, last, pltpu.roll(late, 64, 1))
+        last = late
+    msg_ref[:, 0, 768:896] = marks
     for copy in copies[6:]:
         copy.wait()
 
@@ -175,14 +185,16 @@
     north_ref[12:PLANES] = strip_ref[0]
     south_ref[12:PLANES] = strip_ref[1]
     acc_ref[...] = jnp.zeros_like(acc_ref)
-    for j in range(8):
-        turned = jnp.transpose(msg_ref[:, j, :])
-        if j % 2:
-            mark_ref[8 * j - 8:8 * j + 8, :] = turned[64:80]
-        turned = turned * (1.0 / WEIGHT)
+    mark_ref[...] = jnp.transpose(msg_ref[:, 0, 768:896])[:64]
+    for j in range(6):
+        turned = jnp.transpose(msg_ref[:, 0, 128 * j:128 * j + 128]) * (1.0 / WEIGHT)
         top = turned.astype(BF16).astype(F32)
-        turned_ref[0, j] = top
-        turned_ref[1, j] = turned - top
+        for part, value in enumerate((top, turned - top)):
+            if j < 4:
+                turned_ref[part, 2 * j] = value
+            else:
+                turned_ref[part, 4 * j - 15, 0:64] = value[0:64]
+                turned_ref[part, 4 * j - 13, 0:64] = value[64:128]
 
     def body(q, carry):
         build(
@@ -344,17 +356,24 @@
         return carry
 
     lax.fori_loop(0, 4, gather, 0)
-    for j in range(8):
-        ret_ref[:, j, :] = jnp.transpose(turned_ref[j])
+    for q in range(4):
+        ret_ref[:, 0, 128 * q:128 * q + 128] = jnp.transpose(turned_ref[2 * q])
+    for j in range(2):
+        late = jnp.concatenate([turned_ref[4 * j + 1, 0:64], turned_ref[4 * j + 3, 0:64]], axis=0)
+        ret_ref[:, 0, 512 + 128 * j:640 + 128 * j] = jnp.transpose(late)
 
 
 def return_kernel(ret_ref, owner_ref, rank_ref, transfer_ref, out_ref, l_ref, hot_ref, faces_ref, sems):
-    for q in range(4):
-        for t in range(2):
-            count = 128 if t == 0 else 64
-            top, rest = split(jnp.transpose(ret_ref[:, 2 * q + t, :])[:count])
-            l_ref[128 * t:128 * t + count, 128 * q:128 * q + 128] = top
-            l_ref[128 * t:128 * t + count, 512 + 128 * q:512 + 128 * q + 128] = rest
+    for j in range(6):
+        top, rest = split(jnp.transpose(ret_ref[:, 0, 128 * j:128 * j + 128]))
+        for part, value in enumerate((top, rest)):
+            if j < 4:
+                at = 512 * part + 128 * j
+                l_ref[0:128, at:at + 128] = value
+            else:
+                at = 512 * part + 256 * (j - 4)
+                l_ref[128:192, at:at + 128] = value[0:64]
+                l_ref[128:192, at + 128:at + 256] = value[64:128]
     pick = (iota((80, 10), 0) // 8 == iota((80, 10), 1)).astype(F32)
     spread = lax.dot_general(pick, transfer_ref[...], NT, precision=HIGHEST, preferred_element_type=F32)
     spread = exact(spread, (iota((4, 16), 1) // 3 == iota((4, 16), 0)).astype(F32))
@@ -424,7 +443,7 @@
 
     msg, rank, strip = call(
         face_kernel,
-        [arr(OWNERS, 8, 128), arr(1, FACES), arr(2, 13, 8, COLS)],
+        [arr(OWNERS, 1, 896), arr(1, FACES), arr(2, 13, 8, COLS)],
         [
             pltpu.VMEM((1, FACES), I32), pltpu.VMEM((1, FACES), I32), pltpu.VMEM((110, FACES), BF16),
             pltpu.VMEM((1, FACES), F32), pltpu.VMEM((30, 110), BF16), pltpu.VMEM((4, 10), F32),
@@ -466,7 +485,7 @@
 
     shell, back, _ = call(
         sweep_kernel,
-        [arr(12, ROWS, COLS), arr(OWNERS, 8, 128), arr(PLANES, PAD_R, PAD_C)],
+        [arr(12, ROWS, COLS), arr(OWNERS, 1, 768), arr(PLANES, PAD_R, PAD_C)],
         [
             pltpu.VMEM((PAD_R // 16, 192, 2 * PAD_C), BF16),
             pltpu.VMEM((12 * HALF, 1024), BF16),

time: 91.1 us -> 88.8 us (0.975)
  blocking collectives: 47.1 us -> 45.1 us
    all_to_all x1, blocking collectives: 21.8 us -> 20.5 us  [local(): returned = lax.all_to_all(back, ('grp', 'dev'), split_axis=0, concat_axis=0)]
where the time goes in v5:
time: 88.8 us; the launch traced here: 88.6 us
  blocking collectives  45.1 us (51%)
  Pallas kernels  38.1 us (43%)
  starting transfers between devices  3.48 us (4%)
  local copies, waits for them, and re-layouts  0.96 us (1%)
  between operations  0.94 us (1%)
    pallas_call x8, Pallas kernels, call(): pl.pallas_call(kernel, out_shape=shapes, in_specs=[HBM if i in hbm else V...  38.1 us
    all_to_all x1, blocking collectives, local(): got = lax.all_to_all(msg, ('grp', 'dev'), split_axis=0, concat_axis=0)  24.5 us
    all_to_all x1, blocking collectives, local(): returned = lax.all_to_all(back, ('grp', 'dev'), split_axis=0, concat_axis=0)  20.5 us
    ppermute x2, starting transfers between devices, shift_pair(): lax.ppermute(toward_low, axis, ring(axis, -1))  2.08 us
  transfers between devices with their start and end apart: 4, of which 0 were waited for; matrix products, arithmetic and copies ran while one was open for 0% of the time, Pallas kernels for 9%

profile of v5, /device:TPU:1, one launch (start us, length us, event | category | flops | bytes accessed | tf_op | source)
XLA Modules:
  0.0 88.6 jit_solution(7672810680523060551)
XLA Ops:
  0.6 0.0 copy-start.1
  0.6 0.0 copy-start
  0.7 6.5 %shard_map.104 = (f32[128,1,896]{2,1,0:T(1,128)}, f32[1,4096]{1,0:T(1,128)}, f32[2,13,8,256]{3,2,1,0:T(8,128)}) custom-call(s32[1,4096]{1,0:T(1,128)} %bitcast.9, s32[1,4096]{1,0:T(1,128)} %bitcast.12, bf16[110,4096]{1,0:T(8,128)(2,1)} %state_hbm.1, f32[1,4096]{1,0:T(1,128)} %bitcast.13, bf16[30,110]{1,0:T(8,128)(2,1)} %lift_hbm.1, f32[4,10]{1,0:T(4,128)} %transfer_ref.1, ...), custom_call_target="tpu_custom_call" | custom-call | tf_op jit(solution)/shard_map/pallas_call | solution.py:413
  7.1 0.0 copy-start.5
  7.1 24.5 %all_to_all.10.msg_ref = f32[128,1,896]{2,1,0:T(1,128)S(1)} all-to-all(f32[128,1,896]{2,1,0:T(1,128)} %get-tuple-element.13), channel_id=1, replica_groups=mesh['grp'=4,'dev'=32] {'grp','dev'}, dimensions={0} | all-to-all | bytes 917504 | tf_op jit(solution)/shard_map/all_to_all | solution.py:456
  31.7 0.0 copy-start.2
  31.7 0.9 %copy-done.2 = f32[2,13,8,256]{3,2,1,0:T(8,128)S(1)} copy-done((f32[2,13,8,256]{3,2,1,0:T(8,128)S(1)}, f32[2,13,8,256]{3,2,1,0:T(8,128)}, u32[]{:S(2)}) %copy-start.2) | copy-done | bytes 213016
  32.6 3.8 %shard_map.105 = (f32[25,8,256]{2,1,0:T(8,128)S(1)}, f32[25,8,256]{2,1,0:T(8,128)S(1)}, f32[2,8,128,128]{3,2,1,0:T(8,128)S(1)}, f32[64,128]{1,0:T(8,128)S(1)}) custom-call(f32[128,1,896]{2,1,0:T(1,128)S(1)} %all_to_all.10.msg_ref, f32[2,13,8,256]{3,2,1,0:T(8,128)S(1)} %copy-done.2), custom_call_target="tpu_custom_call" | custom-call | tf_op jit(solution)/shard_map/pallas_call | solution.py:413
  36.4 0.6 collective-permute-start
  37.0 1.0 %collective-permute-start.1 = (f32[25,8,256]{2,1,0:T(8,128)S(1)}, f32[25,8,256]{2,1,0:T(8,128)S(1)}, u32[]{:S(2)}, u32[]{:S(2)}) collective-permute-start(f32[25,8,256]{2,1,0:T(8,128)S(1)} %get-tuple-element.18.south_ref), channel_id=1, source_target_pairs={{0,32},{32,64},{64,96},{96,0},{1,33},{33,65},{65,97},{97,1},{2,34}... | collective-permute-start | bytes 614408 | tf_op jit(solution)/shard_map/ppermute | solution.py:435
  37.9 6.4 %shard_map.106.load_ref = f32[12,64,256]{2,1,0:T(8,128)S(1)} custom-call(f32[2,8,128,128]{3,2,1,0:T(8,128)S(1)} %get-tuple-element.15.turned_ref, f32[64,128]{1,0:T(8,128)S(1)} %get-tuple-element.16.mark_ref, f32[25,8,256]{2,1,0:T(8,128)S(1)} %get-tuple-element.17.north_ref, f32[25,8,256]{2,1,0:T(8,128)S(1)} %get-tuple-element.18.south_ref), custom_call_target="tpu_custom_call" | custom-call | tf_op jit(solution)/shard_map/pallas_call | solution.py:413
  44.3 0.0 collective-permute-done.south_ref
  44.3 0.0 collective-permute-done.1.north_ref
  44.3 0.0 copy-done.1
  44.4 0.0 copy-done
  44.4 0.6 shard_map.108
  44.9 1.5 %collective-permute-start.2 = (f32[80,256]{1,0:T(8,128)S(1)}, f32[80,256]{1,0:T(8,128)S(1)}, u32[]{:S(2)}, u32[]{:S(2)}) collective-permute-start(f32[80,256]{1,0:T(8,128)S(1)} %get-tuple-element.19), channel_id=1, source_target_pairs={{0,31},{1,0},{2,1},{3,2},{4,3},{5,4},{6,5},{7,6},{8,7},{9,8},{10,9... | collective-permute-start | bytes 245768 | tf_op jit(solution)/shard_map/ppermute | solution.py:435
  46.4 0.4 collective-permute-start.3
  46.9 0.0 copy-done.5
  46.9 1.8 %shard_map.109.mat_ref = bf16[192,192]{1,0:T(8,128)(2,1)S(1)} custom-call(f32[12,12]{1,0:T(8,128)S(1)} %copy-done.5), custom_call_target="tpu_custom_call" | custom-call | tf_op jit(solution)/shard_map/pallas_call | solution.py:413
  48.7 0.2 shard_map.107.pad_in
  48.9 0.0 copy-start.3
  48.9 0.0 copy-start.4
  48.9 0.0 copy-start.6
  48.9 0.0 collective-permute-done.2.from_east_ref
  48.9 0.0 collective-permute-done.3.from_west_ref
  48.9 15.4 %shard_map.110 = (f32[12,64,256]{2,1,0:T(8,128)}, f32[128,1,768]{2,1,0:T(1,128)S(1)}, f32[25,80,384]{2,1,0:T(8,128)S(1)}) custom-call(f32[25,80,384]{2,1,0:T(8,128)S(1)} %shard_map.107.pad_in, f32[80,256]{1,0:T(8,128)S(1)} %collective-permute-done.2.from_east_ref, ...), custom_call_target="tpu_custom_call", output_to_operand_aliasing={{2}: (0, {})} | custom-call | tf_op jit(solution)/shard_map/pallas_call | solution.py:413
  64.4 20.5 %all_to_all.11.ret_ref = f32[128,1,768]{2,1,0:T(1,128)S(1)} all-to-all(f32[128,1,768]{2,1,0:T(1,128)S(1)} %get-tuple-element.22), channel_id=1, replica_groups=mesh['grp'=4,'dev'=32] {'grp','dev'}, dimensions={0} | all-to-all | bytes 786432 | tf_op jit(solution)/shard_map/all_to_all | solution.py:497
  84.9 0.0 copy-done.3
  84.9 0.0 copy-done.4
  84.9 0.0 copy-done.6
  84.9 3.5 %shard_map.111 = f32[10,3,4096]{2,1,0:T(4,128)} custom-call(f32[128,1,768]{2,1,0:T(1,128)S(1)} %all_to_all.11.ret_ref, s32[1,4096]{1,0:T(1,128)S(1)} %bitcast.10, f32[1,4096]{1,0:T(1,128)S(1)} %copy-done.4, f32[4,10]{1,0:T(4,128)S(1)} %copy-done.6), custom_call_target="tpu_custom_call" | custom-call | tf_op jit(solution)/shard_map/pallas_call | solution.py:413
Async XLA Ops:
  0.6 43.7 %copy-start.1 = (f32[64,256]{1,0:T(8,128)S(1)}, f32[64,256]{1,0:T(8,128)}, u32[]{:S(2)}) copy-start(f32[64,256]{1,0:T(8,128)} %scale_ref.3) | copy-start | bytes 196612
  0.6 43.7 %copy-start = (f32[4,3,64,256]{3,2,1,0:T(8,128)S(1)}, f32[4,3,64,256]{3,2,1,0:T(8,128)}, u32[]{:S(2)}) copy-start(f32[4,3,64,256]{3,2,1,0:T(8,128)} %param.17) | copy-start | bytes 2359300
  7.1 39.8 %copy-start.5 = (f32[12,12]{1,0:T(8,128)S(1)}, f32[12,12]{1,0:T(8,128)}, u32[]{:S(2)}) copy-start(f32[12,12]{1,0:T(8,128)} %stiff_ref.1) | copy-start | bytes 1732
  31.7 0.9 %copy-start.2 = (f32[2,13,8,256]{3,2,1,0:T(8,128)S(1)}, f32[2,13,8,256]{3,2,1,0:T(8,128)}, u32[]{:S(2)}) copy-start(f32[2,13,8,256]{3,2,1,0:T(8,128)} %get-tuple-element.14.strip_ref) | copy-start | bytes 638980
  36.4 7.9 %collective-permute-start = (f32[25,8,256]{2,1,0:T(8,128)S(1)}, f32[25,8,256]{2,1,0:T(8,128)S(1)}, u32[]{:S(2)}, u32[]{:S(2)}) collective-permute-start(f32[25,8,256]{2,1,0:T(8,128)S(1)} %get-tuple-element.17.north_ref), channel_id=1, source_target_pairs={{0,96},{32,0},{64,32},{96,64},{1,97},{33,1},{65,33},{97,65},{2,98}... | collective-permute-start | bytes 614408 | tf_op jit(solution)/shard_map/ppermute | solution.py:435
  37.0 7.4 %collective-permute-start.1 = (f32[25,8,256]{2,1,0:T(8,128)S(1)}, f32[25,8,256]{2,1,0:T(8,128)S(1)}, u32[]{:S(2)}, u32[]{:S(2)}) collective-permute-start(f32[25,8,256]{2,1,0:T(8,128)S(1)} %get-tuple-element.18.south_ref), channel_id=1, source_target_pairs={{0,32},{32,64},{64,96},{96,0},{1,33},{33,65},{65,97},{97,1},{2,34}... | collective-permute-start | bytes 614408 | tf_op jit(solution)/shard_map/ppermute | solution.py:435
  44.9 4.0 %collective-permute-start.2 = (f32[80,256]{1,0:T(8,128)S(1)}, f32[80,256]{1,0:T(8,128)S(1)}, u32[]{:S(2)}, u32[]{:S(2)}) collective-permute-start(f32[80,256]{1,0:T(8,128)S(1)} %get-tuple-element.19), channel_id=1, source_target_pairs={{0,31},{1,0},{2,1},{3,2},{4,3},{5,4},{6,5},{7,6},{8,7},{9,8},{10,9... | collective-permute-start | bytes 245768 | tf_op jit(solution)/shard_map/ppermute | solution.py:435
  46.4 2.5 %collective-permute-start.3 = (f32[80,256]{1,0:T(8,128)S(1)}, f32[80,256]{1,0:T(8,128)S(1)}, u32[]{:S(2)}, u32[]{:S(2)}) collective-permute-start(f32[80,256]{1,0:T(8,128)S(1)} %get-tuple-element.20), channel_id=1, source_target_pairs={{0,1},{1,2},{2,3},{3,4},{4,5},{5,6},{6,7},{7,8},{8,9},{9,10},{10,1... | collective-permute-start | bytes 245768 | tf_op jit(solution)/shard_map/ppermute | solution.py:435
  48.9 36.0 %copy-start.3 = (s32[4096,1]{0,1:T(1,128)S(1)}, s32[4096,1]{0,1:T(1,128)}, u32[]{:S(2)}) copy-start(s32[4096,1]{0,1:T(1,128)} %param.9) | copy-start | bytes 49156
  48.9 36.0 %copy-start.4 = (f32[1,4096]{1,0:T(1,128)S(1)}, f32[1,4096]{1,0:T(1,128)}, u32[]{:S(2)}) copy-start(f32[1,4096]{1,0:T(1,128)} %get-tuple-element.23.rank_ref) | copy-start | bytes 49156
  48.9 36.0 %copy-start.6 = (f32[4,10]{1,0:T(4,128)S(1)}, f32[4,10]{1,0:T(4,128)}, u32[]{:S(2)}) copy-start(f32[4,10]{1,0:T(4,128)} %transfer_ref.1) | copy-start | bytes 484

commit v6 on v5

--- a/solution.py
+++ b/solution.py
@@ -25,6 +25,7 @@
 STEP = 2048
 HALF = 32
 PLANES = 25
+STRIP = 4096
 LIMIT = 60
 NT = (((1,), (1,)), ((), ()))
 
@@ -79,16 +80,17 @@
 
 def face_kernel(owner_hbm, elem_hbm, state_hbm, scale_hbm, lift_hbm, transfer_hbm, prev_hbm, shell_hbm,
                 msg_ref, rank_ref, strip_ref,
-                owner_ref, elem_ref, state_ref, scale_ref, lift_ref, transfer_ref, x_ref, hot_ref, acc_ref, sems):
+                owner_ref, elem_ref, state_ref, scale_ref, lift_ref, transfer_ref, stage_ref, x_ref, hot_ref, acc_ref,
+                sems):
     copies = [
         pltpu.make_async_copy(src, dst, sems.at[i])
         for i, (src, dst) in enumerate((
             (owner_hbm, owner_ref), (transfer_hbm, transfer_ref), (lift_hbm, lift_ref),
             (elem_hbm, elem_ref), (scale_hbm, scale_ref), (state_hbm, state_ref),
-            (prev_hbm.at[:, 0:8, :], strip_ref.at[0, 0:12]),
-            (prev_hbm.at[:, ROWS - 8:ROWS, :], strip_ref.at[1, 0:12]),
-            (shell_hbm.at[0:8, :], strip_ref.at[0, 12]),
-            (shell_hbm.at[ROWS - 8:ROWS, :], strip_ref.at[1, 12]),
+            (prev_hbm.at[:, 0:8, :], stage_ref.at[0, 0:12]),
+            (prev_hbm.at[:, ROWS - 8:ROWS, :], stage_ref.at[1, 0:12]),
+            (shell_hbm.at[0:8, :], stage_ref.at[0, 12]),
+            (shell_hbm.at[ROWS - 8:ROWS, :], stage_ref.at[1, 12]),
         ))
     ]
     for copy in copies:
@@ -108,8 +110,11 @@
         return base + counts[:, CHUNK:]
 
     lax.fori_loop(0, FACES // CHUNK, ranks, jnp.zeros((OWNERS, CHUNK), F32), unroll=True)
-    for copy in copies[1:6]:
+    for copy in copies[1:]:
         copy.wait()
+    keeps = [pltpu.make_async_copy(stage_ref.at[i], strip_ref.at[i, 0:13], sems.at[10 + i]) for i in range(2)]
+    for copy in keeps:
+        copy.start()
     spread = jnp.concatenate(
         [jnp.pad(transfer_ref[...], ((0, 0), (10 * c, 20 - 10 * c))) for c in range(3)], axis=0
     )
@@ -148,7 +153,7 @@
             msg_ref[:, 0, at:at + 128] = jnp.where(lane < 64, last, pltpu.roll(late, 64, 1))
         last = late
     msg_ref[:, 0, 768:896] = marks
-    for copy in copies[6:]:
+    for copy in keeps:
         copy.wait()
 
 
@@ -181,9 +186,14 @@
                         a_ref[at + 16 * b:at + 16 * b + 16, lanes] = piece * value
 
 
-def edge_scatter_kernel(msg_ref, strip_ref, north_ref, south_ref, turned_ref, mark_ref, a_ref, col_ref, acc_ref):
-    north_ref[12:PLANES] = strip_ref[0]
-    south_ref[12:PLANES] = strip_ref[1]
+def edge_scatter_kernel(msg_ref, strip_ref, north_ref, south_ref, turned_ref, mark_ref,
+                        a_ref, col_ref, acc_ref, sems):
+    copies = [
+        pltpu.make_async_copy(strip_ref.at[i, 0:13], ref.at[12:PLANES], sems.at[i])
+        for i, ref in enumerate((north_ref, south_ref))
+    ]
+    for copy in copies:
+        copy.start()
     acc_ref[...] = jnp.zeros_like(acc_ref)
     mark_ref[...] = jnp.transpose(msg_ref[:, 0, 768:896])[:64]
     for j in range(6):
@@ -209,6 +219,8 @@
         strip = acc_ref[16 * c:16 * c + 16] + acc_ref[192 + 16 * c:208 + 16 * c]
         north_ref[c] = strip[0:8]
         south_ref[c] = strip[8:16]
+    for copy in copies:
+        copy.wait()
 
 
 INNER = ROWS - 16
@@ -367,13 +379,13 @@
     for j in range(6):
         top, rest = split(jnp.transpose(ret_ref[:, 0, 128 * j:128 * j + 128]))
         for part, value in enumerate((top, rest)):
+            at = 192 * part
             if j < 4:
-                at = 512 * part + 128 * j
-                l_ref[0:128, at:at + 128] = value
+                l_ref[at:at + 128, 128 * j:128 * j + 128] = value
             else:
-                at = 512 * part + 256 * (j - 4)
-                l_ref[128:192, at:at + 128] = value[0:64]
-                l_ref[128:192, at + 128:at + 256] = value[64:128]
+                lane = 256 * (j - 4)
+                l_ref[at + 128:at + 192, lane:lane + 128] = value[0:64]
+                l_ref[at + 128:at + 192, lane + 128:lane + 256] = value[64:128]
     pick = (iota((80, 10), 0) // 8 == iota((80, 10), 1)).astype(F32)
     spread = lax.dot_general(pick, transfer_ref[...], NT, precision=HIGHEST, preferred_element_type=F32)
     spread = exact(spread, (iota((4, 16), 1) // 3 == iota((4, 16), 0)).astype(F32))
@@ -385,7 +397,8 @@
         rank = rank_ref[:, part].astype(I32)
         for at, piece in quarters(owner_ref[:, part].astype(F32), (rank >> 4).astype(F32)):
             hot_ref[at:at + 16, :] = piece
-        found = dot(l_ref[:, :512], hot_ref[...]) + dot(l_ref[:, 512:], hot_ref[...])
+        found = dot(l_ref[...], hot_ref[...])
+        found = found[:192] + found[192:]
         here = iota((16, STEP), 0) == (rank & 15)
         node = jnp.concatenate(
             [jnp.sum(jnp.where(here, found[16 * c:16 * c + 16], 0.0), axis=0, keepdims=True) for c in range(12)]
@@ -443,15 +456,16 @@
 
     msg, rank, strip = call(
         face_kernel,
-        [arr(OWNERS, 1, 896), arr(1, FACES), arr(2, 13, 8, COLS)],
+        [arr(OWNERS, 1, 896), arr(1, FACES), arr(2, STRIP, 8, COLS)],
         [
             pltpu.VMEM((1, FACES), I32), pltpu.VMEM((1, FACES), I32), pltpu.VMEM((110, FACES), BF16),
             pltpu.VMEM((1, FACES), F32), pltpu.VMEM((30, 110), BF16), pltpu.VMEM((4, 10), F32),
+            pltpu.VMEM((2, 13, 8, COLS), F32),
             pltpu.VMEM((256, 2 * STEP), BF16), pltpu.VMEM((4 * OWNERS, STEP), BF16), pltpu.VMEM((4 * OWNERS, 256), F32),
-            pltpu.SemaphoreType.DMA((10,)),
+            pltpu.SemaphoreType.DMA((12,)),
         ],
         owner, element, element_state, scale, lift, transfer, prev, element_scale,
-        hbm=(0, 1, 2, 3, 4, 5, 6, 7), limit=LIMIT,
+        hbm=(0, 1, 2, 3, 4, 5, 6, 7), limit=LIMIT, out_specs=[VMEM, VMEM, HBM],
     )
     got = lax.all_to_all(msg, ("grp", "dev"), split_axis=0, concat_axis=0)
     mat = call(matrix_kernel, arr(192, 192, dtype=BF16), [], stiffness_ref)
@@ -463,8 +477,10 @@
             pltpu.VMEM((24 * 16, 2048), BF16),
             pltpu.VMEM((COLS, 2048), BF16),
             pltpu.VMEM((24 * 16, COLS), F32),
+            pltpu.SemaphoreType.DMA((2,)),
         ],
         got, strip,
+        hbm=(1,),
     )
     below, above = shift_pair(north, south, "grp")
     load = call(
@@ -499,7 +515,7 @@
         return_kernel,
         arr(10, 3, FACES),
         [
-            pltpu.VMEM((192, 1024), BF16),
+            pltpu.VMEM((384, 512), BF16),
             pltpu.VMEM((4 * OWNERS, STEP), BF16),
             pltpu.VMEM((10, 3, FACES), F32),
             pltpu.SemaphoreType.DMA((FACES // STEP,)),

time: 88.8 us -> 87.8 us (0.989)
  local copies, waits for them, and re-layouts: 0.96 us -> 0.03 us
    unnamed x14 -> x12, local copies, waits for them, and re-layouts: 0.96 us -> 0.03 us
  transfers between devices with their start and end apart: 4 -> 4, of which waited for: 0 -> 0; matrix products, arithmetic and copies ran while one was open for 0% -> 0% of each run, Pallas kernels for 9% -> 10%
where the time goes in v6:
time: 87.8 us; the launch traced here: 87.5 us
  blocking collectives  45 us (51%)
  Pallas kernels  38 us (43%)
  starting transfers between devices  3.48 us (4%)
  between operations  0.93 us (1%)
    pallas_call x8, Pallas kernels, call(): pl.pallas_call(kernel, out_shape=shapes, in_specs=[HBM if i in hbm else V...  38 us
    all_to_all x1, blocking collectives, local(): got = lax.all_to_all(msg, ('grp', 'dev'), split_axis=0, concat_axis=0)  24.5 us
    all_to_all x1, blocking collectives, local(): returned = lax.all_to_all(back, ('grp', 'dev'), split_axis=0, concat_axis=0)  20.5 us
    ppermute x2, starting transfers between devices, shift_pair(): lax.ppermute(toward_low, axis, ring(axis, -1))  2.08 us
  transfers between devices with their start and end apart: 4, of which 0 were waited for; matrix products, arithmetic and copies ran while one was open for 0% of the time, Pallas kernels for 10%

profile of v6, /device:TPU:1, one launch (start us, length us, event | category | flops | bytes accessed | tf_op | source)
XLA Modules:
  0.0 87.5 jit_solution(7316345272362816538)
XLA Ops:
  0.6 6.3 %shard_map.104 = (f32[128,1,896]{2,1,0:T(1,128)}, f32[1,4096]{1,0:T(1,128)}, f32[2,4096,8,256]{3,2,1,0:T(8,128)}) custom-call(s32[1,4096]{1,0:T(1,128)} %bitcast.9, s32[1,4096]{1,0:T(1,128)} %bitcast.12, bf16[110,4096]{1,0:T(8,128)(2,1)} %state_hbm.1, f32[1,4096]{1,0:T(1,128)} %bitcast.13, bf16[30,110]{1,0:T(8,128)(2,1)} %lift_hbm.1, f32[4,10]{1,0:T(4,128)} %transfer_ref.1, ...), custom_call_target="tpu_custom_call" | custom-call | tf_op jit(solution)/shard_map/pallas_call | solution.py:426
  7.0 24.5 %all_to_all.10.msg_ref = f32[128,1,896]{2,1,0:T(1,128)S(1)} all-to-all(f32[128,1,896]{2,1,0:T(1,128)} %get-tuple-element.13), channel_id=1, replica_groups=mesh['grp'=4,'dev'=32] {'grp','dev'}, dimensions={0} | all-to-all | bytes 917504 | tf_op jit(solution)/shard_map/all_to_all | solution.py:470
  31.5 0.0 copy-start
  31.5 0.0 copy-start.1
  31.5 3.8 %shard_map.105 = (f32[25,8,256]{2,1,0:T(8,128)S(1)}, f32[25,8,256]{2,1,0:T(8,128)S(1)}, f32[2,8,128,128]{3,2,1,0:T(8,128)S(1)}, f32[64,128]{1,0:T(8,128)S(1)}) custom-call(f32[128,1,896]{2,1,0:T(1,128)S(1)} %all_to_all.10.msg_ref, f32[2,4096,8,256]{3,2,1,0:T(8,128)} %get-tuple-element.14.strip_ref), custom_call_target="tpu_custom_call" | custom-call | tf_op jit(solution)/shard_map/pallas_call | solution.py:426
  35.3 0.0 copy-start.4
  35.3 0.6 collective-permute-start
  35.9 1.0 %collective-permute-start.1 = (f32[25,8,256]{2,1,0:T(8,128)S(1)}, f32[25,8,256]{2,1,0:T(8,128)S(1)}, u32[]{:S(2)}, u32[]{:S(2)}) collective-permute-start(f32[25,8,256]{2,1,0:T(8,128)S(1)} %get-tuple-element.18.south_ref), channel_id=1, source_target_pairs={{0,32},{32,64},{64,96},{96,0},{1,33},{33,65},{65,97},{97,1},{2,34}... | collective-permute-start | bytes 614408 | tf_op jit(solution)/shard_map/ppermute | solution.py:448
  36.9 6.4 %shard_map.106.load_ref = f32[12,64,256]{2,1,0:T(8,128)S(1)} custom-call(f32[2,8,128,128]{3,2,1,0:T(8,128)S(1)} %get-tuple-element.15.turned_ref, f32[64,128]{1,0:T(8,128)S(1)} %get-tuple-element.16.mark_ref, f32[25,8,256]{2,1,0:T(8,128)S(1)} %get-tuple-element.17.north_ref, f32[25,8,256]{2,1,0:T(8,128)S(1)} %get-tuple-element.18.south_ref), custom_call_target="tpu_custom_call" | custom-call | tf_op jit(solution)/shard_map/pallas_call | solution.py:426
  43.3 0.0 collective-permute-done.south_ref
  43.3 0.0 collective-permute-done.1.north_ref
  43.3 0.0 copy-done
  43.3 0.0 copy-done.1
  43.3 0.6 shard_map.108
  43.9 1.5 %collective-permute-start.2 = (f32[80,256]{1,0:T(8,128)S(1)}, f32[80,256]{1,0:T(8,128)S(1)}, u32[]{:S(2)}, u32[]{:S(2)}) collective-permute-start(f32[80,256]{1,0:T(8,128)S(1)} %get-tuple-element.19), channel_id=1, source_target_pairs={{0,31},{1,0},{2,1},{3,2},{4,3},{5,4},{6,5},{7,6},{8,7},{9,8},{10,9... | collective-permute-start | bytes 245768 | tf_op jit(solution)/shard_map/ppermute | solution.py:448
  45.4 0.4 collective-permute-start.3
  45.8 0.0 copy-done.4
  45.8 1.8 %shard_map.109.mat_ref = bf16[192,192]{1,0:T(8,128)(2,1)S(1)} custom-call(f32[12,12]{1,0:T(8,128)S(1)} %copy-done.4), custom_call_target="tpu_custom_call" | custom-call | tf_op jit(solution)/shard_map/pallas_call | solution.py:426
  47.6 0.2 shard_map.107.pad_in
  47.8 0.0 copy-start.2
  47.8 0.0 copy-start.3
  47.8 0.0 copy-start.5
  47.9 0.0 collective-permute-done.2.from_east_ref
  47.9 0.0 collective-permute-done.3.from_west_ref
  47.9 15.4 %shard_map.110 = (f32[12,64,256]{2,1,0:T(8,128)}, f32[128,1,768]{2,1,0:T(1,128)S(1)}, f32[25,80,384]{2,1,0:T(8,128)S(1)}) custom-call(f32[25,80,384]{2,1,0:T(8,128)S(1)} %shard_map.107.pad_in, f32[80,256]{1,0:T(8,128)S(1)} %collective-permute-done.2.from_east_ref, ...), custom_call_target="tpu_custom_call", output_to_operand_aliasing={{2}: (0, {})} | custom-call | tf_op jit(solution)/shard_map/pallas_call | solution.py:426
  63.3 20.5 %all_to_all.11.ret_ref = f32[128,1,768]{2,1,0:T(1,128)S(1)} all-to-all(f32[128,1,768]{2,1,0:T(1,128)S(1)} %get-tuple-element.22), channel_id=1, replica_groups=mesh['grp'=4,'dev'=32] {'grp','dev'}, dimensions={0} | all-to-all | bytes 786432 | tf_op jit(solution)/shard_map/all_to_all | solution.py:513
  83.8 0.0 copy-done.2
  83.8 0.0 copy-done.3
  83.8 0.0 copy-done.5
  83.8 3.5 %shard_map.111 = f32[10,3,4096]{2,1,0:T(4,128)} custom-call(f32[128,1,768]{2,1,0:T(1,128)S(1)} %all_to_all.11.ret_ref, s32[1,4096]{1,0:T(1,128)S(1)} %bitcast.10, f32[1,4096]{1,0:T(1,128)S(1)} %copy-done.3, f32[4,10]{1,0:T(4,128)S(1)} %copy-done.5), custom_call_target="tpu_custom_call" | custom-call | tf_op jit(solution)/shard_map/pallas_call | solution.py:426
Async XLA Ops:
  31.5 11.8 %copy-start = (f32[4,3,64,256]{3,2,1,0:T(8,128)S(1)}, f32[4,3,64,256]{3,2,1,0:T(8,128)}, u32[]{:S(2)}) copy-start(f32[4,3,64,256]{3,2,1,0:T(8,128)} %param.17) | copy-start | bytes 2359300
  31.5 11.8 %copy-start.1 = (f32[64,256]{1,0:T(8,128)S(1)}, f32[64,256]{1,0:T(8,128)}, u32[]{:S(2)}) copy-start(f32[64,256]{1,0:T(8,128)} %scale_ref.3) | copy-start | bytes 196612
  35.3 10.5 %copy-start.4 = (f32[12,12]{1,0:T(8,128)S(1)}, f32[12,12]{1,0:T(8,128)}, u32[]{:S(2)}) copy-start(f32[12,12]{1,0:T(8,128)} %stiff_ref.1) | copy-start | bytes 1732
  35.3 7.9 %collective-permute-start = (f32[25,8,256]{2,1,0:T(8,128)S(1)}, f32[25,8,256]{2,1,0:T(8,128)S(1)}, u32[]{:S(2)}, u32[]{:S(2)}) collective-permute-start(f32[25,8,256]{2,1,0:T(8,128)S(1)} %get-tuple-element.17.north_ref), channel_id=1, source_target_pairs={{0,96},{32,0},{64,32},{96,64},{1,97},{33,1},{65,33},{97,65},{2,98}... | collective-permute-start | bytes 614408 | tf_op jit(solution)/shard_map/ppermute | solution.py:448
  35.9 7.4 %collective-permute-start.1 = (f32[25,8,256]{2,1,0:T(8,128)S(1)}, f32[25,8,256]{2,1,0:T(8,128)S(1)}, u32[]{:S(2)}, u32[]{:S(2)}) collective-permute-start(f32[25,8,256]{2,1,0:T(8,128)S(1)} %get-tuple-element.18.south_ref), channel_id=1, source_target_pairs={{0,32},{32,64},{64,96},{96,0},{1,33},{33,65},{65,97},{97,1},{2,34}... | collective-permute-start | bytes 614408 | tf_op jit(solution)/shard_map/ppermute | solution.py:448
  43.9 4.0 %collective-permute-start.2 = (f32[80,256]{1,0:T(8,128)S(1)}, f32[80,256]{1,0:T(8,128)S(1)}, u32[]{:S(2)}, u32[]{:S(2)}) collective-permute-start(f32[80,256]{1,0:T(8,128)S(1)} %get-tuple-element.19), channel_id=1, source_target_pairs={{0,31},{1,0},{2,1},{3,2},{4,3},{5,4},{6,5},{7,6},{8,7},{9,8},{10,9... | collective-permute-start | bytes 245768 | tf_op jit(solution)/shard_map/ppermute | solution.py:448
  45.4 2.5 %collective-permute-start.3 = (f32[80,256]{1,0:T(8,128)S(1)}, f32[80,256]{1,0:T(8,128)S(1)}, u32[]{:S(2)}, u32[]{:S(2)}) collective-permute-start(f32[80,256]{1,0:T(8,128)S(1)} %get-tuple-element.20), channel_id=1, source_target_pairs={{0,1},{1,2},{2,3},{3,4},{4,5},{5,6},{6,7},{7,8},{8,9},{9,10},{10,1... | collective-permute-start | bytes 245768 | tf_op jit(solution)/shard_map/ppermute | solution.py:448
  47.8 36.0 %copy-start.2 = (s32[4096,1]{0,1:T(1,128)S(1)}, s32[4096,1]{0,1:T(1,128)}, u32[]{:S(2)}) copy-start(s32[4096,1]{0,1:T(1,128)} %param.9) | copy-start | bytes 49156
  47.8 36.0 %copy-start.3 = (f32[1,4096]{1,0:T(1,128)S(1)}, f32[1,4096]{1,0:T(1,128)}, u32[]{:S(2)}) copy-start(f32[1,4096]{1,0:T(1,128)} %get-tuple-element.23.rank_ref) | copy-start | bytes 49156
  47.8 36.0 %copy-start.5 = (f32[4,10]{1,0:T(4,128)S(1)}, f32[4,10]{1,0:T(4,128)}, u32[]{:S(2)}) copy-start(f32[4,10]{1,0:T(4,128)} %transfer_ref.1) | copy-start | bytes 484

commit v7 on v6

--- a/solution.py
+++ b/solution.py
@@ -345,7 +345,7 @@
                     ) * factor
         return carry
 
-    lax.fori_loop(0, SWEEPS, sweep, 0, unroll=2)
+    lax.fori_loop(0, SWEEPS, sweep, 0, unroll=8)
     for c in range(12):
         value = pad_ref[12 + c, 0:ROWS, 0:COLS]
         out_ref[c] = value
@@ -367,7 +367,7 @@
             turned_ref[2 * q + c // 8, 16 * (c % 8):16 * (c % 8) + 16, :] = value
         return carry
 
-    lax.fori_loop(0, 4, gather, 0)
+    lax.fori_loop(0, 4, gather, 0, unroll=2)
     for q in range(4):
         ret_ref[:, 0, 128 * q:128 * q + 128] = jnp.transpose(turned_ref[2 * q])
     for j in range(2):

time: 87.8 us -> 86.9 us (0.990)
  no operation moved by 1% of the time
where the time goes in v7:
time: 86.9 us; the launch traced here: 86.7 us
  blocking collectives  45 us (52%)
  Pallas kernels  37.2 us (43%)
  starting transfers between devices  3.48 us (4%)
  between operations  0.93 us (1%)
    pallas_call x8, Pallas kernels, call(): pl.pallas_call(kernel, out_shape=shapes, in_specs=[HBM if i in hbm else V...  37.2 us
    all_to_all x1, blocking collectives, local(): got = lax.all_to_all(msg, ('grp', 'dev'), split_axis=0, concat_axis=0)  24.5 us
    all_to_all x1, blocking collectives, local(): returned = lax.all_to_all(back, ('grp', 'dev'), split_axis=0, concat_axis=0)  20.5 us
    ppermute x2, starting transfers between devices, shift_pair(): lax.ppermute(toward_low, axis, ring(axis, -1))  2.08 us
  transfers between devices with their start and end apart: 4, of which 0 were waited for; matrix products, arithmetic and copies ran while one was open for 0% of the time, Pallas kernels for 10%

profile of v7, /device:TPU:1, one launch (start us, length us, event | category | flops | bytes accessed | tf_op | source)
XLA Modules:
  0.0 86.7 jit_solution(4413141970474689786)
XLA Ops:
  0.6 6.3 %shard_map.104 = (f32[128,1,896]{2,1,0:T(1,128)}, f32[1,4096]{1,0:T(1,128)}, f32[2,4096,8,256]{3,2,1,0:T(8,128)}) custom-call(s32[1,4096]{1,0:T(1,128)} %bitcast.9, s32[1,4096]{1,0:T(1,128)} %bitcast.12, bf16[110,4096]{1,0:T(8,128)(2,1)} %state_hbm.1, f32[1,4096]{1,0:T(1,128)} %bitcast.13, bf16[30,110]{1,0:T(8,128)(2,1)} %lift_hbm.1, f32[4,10]{1,0:T(4,128)} %transfer_ref.1, ...), custom_call_target="tpu_custom_call" | custom-call | tf_op jit(solution)/shard_map/pallas_call | solution.py:426
  7.0 24.5 %all_to_all.10.msg_ref = f32[128,1,896]{2,1,0:T(1,128)S(1)} all-to-all(f32[128,1,896]{2,1,0:T(1,128)} %get-tuple-element.13), channel_id=1, replica_groups=mesh['grp'=4,'dev'=32] {'grp','dev'}, dimensions={0} | all-to-all | bytes 917504 | tf_op jit(solution)/shard_map/all_to_all | solution.py:470
  31.5 0.0 copy-start
  31.5 0.0 copy-start.1
  31.5 3.8 %shard_map.105 = (f32[25,8,256]{2,1,0:T(8,128)S(1)}, f32[25,8,256]{2,1,0:T(8,128)S(1)}, f32[2,8,128,128]{3,2,1,0:T(8,128)S(1)}, f32[64,128]{1,0:T(8,128)S(1)}) custom-call(f32[128,1,896]{2,1,0:T(1,128)S(1)} %all_to_all.10.msg_ref, f32[2,4096,8,256]{3,2,1,0:T(8,128)} %get-tuple-element.14.strip_ref), custom_call_target="tpu_custom_call" | custom-call | tf_op jit(solution)/shard_map/pallas_call | solution.py:426
  35.3 0.0 copy-start.4
  35.3 0.6 collective-permute-start
  35.9 1.0 %collective-permute-start.1 = (f32[25,8,256]{2,1,0:T(8,128)S(1)}, f32[25,8,256]{2,1,0:T(8,128)S(1)}, u32[]{:S(2)}, u32[]{:S(2)}) collective-permute-start(f32[25,8,256]{2,1,0:T(8,128)S(1)} %get-tuple-element.18.south_ref), channel_id=1, source_target_pairs={{0,32},{32,64},{64,96},{96,0},{1,33},{33,65},{65,97},{97,1},{2,34}... | collective-permute-start | bytes 614408 | tf_op jit(solution)/shard_map/ppermute | solution.py:448
  36.9 6.4 %shard_map.106.load_ref = f32[12,64,256]{2,1,0:T(8,128)S(1)} custom-call(f32[2,8,128,128]{3,2,1,0:T(8,128)S(1)} %get-tuple-element.15.turned_ref, f32[64,128]{1,0:T(8,128)S(1)} %get-tuple-element.16.mark_ref, f32[25,8,256]{2,1,0:T(8,128)S(1)} %get-tuple-element.17.north_ref, f32[25,8,256]{2,1,0:T(8,128)S(1)} %get-tuple-element.18.south_ref), custom_call_target="tpu_custom_call" | custom-call | tf_op jit(solution)/shard_map/pallas_call | solution.py:426
  43.3 0.0 collective-permute-done.south_ref
  43.3 0.0 collective-permute-done.1.north_ref
  43.3 0.0 copy-done
  43.3 0.0 copy-done.1
  43.3 0.6 shard_map.108
  43.9 1.5 %collective-permute-start.2 = (f32[80,256]{1,0:T(8,128)S(1)}, f32[80,256]{1,0:T(8,128)S(1)}, u32[]{:S(2)}, u32[]{:S(2)}) collective-permute-start(f32[80,256]{1,0:T(8,128)S(1)} %get-tuple-element.19), channel_id=1, source_target_pairs={{0,31},{1,0},{2,1},{3,2},{4,3},{5,4},{6,5},{7,6},{8,7},{9,8},{10,9... | collective-permute-start | bytes 245768 | tf_op jit(solution)/shard_map/ppermute | solution.py:448
  45.4 0.4 collective-permute-start.3
  45.8 0.0 copy-done.4
  45.8 1.8 %shard_map.109.mat_ref = bf16[192,192]{1,0:T(8,128)(2,1)S(1)} custom-call(f32[12,12]{1,0:T(8,128)S(1)} %copy-done.4), custom_call_target="tpu_custom_call" | custom-call | tf_op jit(solution)/shard_map/pallas_call | solution.py:426
  47.6 0.2 shard_map.107.pad_in
  47.8 0.0 copy-start.2
  47.8 0.0 copy-start.3
  47.8 0.0 copy-start.5
  47.9 0.0 collective-permute-done.2.from_east_ref
  47.9 0.0 collective-permute-done.3.from_west_ref
  47.9 14.6 %shard_map.110 = (f32[12,64,256]{2,1,0:T(8,128)}, f32[128,1,768]{2,1,0:T(1,128)S(1)}, f32[25,80,384]{2,1,0:T(8,128)S(1)}) custom-call(f32[25,80,384]{2,1,0:T(8,128)S(1)} %shard_map.107.pad_in, f32[80,256]{1,0:T(8,128)S(1)} %collective-permute-done.2.from_east_ref, ...), custom_call_target="tpu_custom_call", output_to_operand_aliasing={{2}: (0, {})} | custom-call | tf_op jit(solution)/shard_map/pallas_call | solution.py:426
  62.5 20.5 %all_to_all.11.ret_ref = f32[128,1,768]{2,1,0:T(1,128)S(1)} all-to-all(f32[128,1,768]{2,1,0:T(1,128)S(1)} %get-tuple-element.22), channel_id=1, replica_groups=mesh['grp'=4,'dev'=32] {'grp','dev'}, dimensions={0} | all-to-all | bytes 786432 | tf_op jit(solution)/shard_map/all_to_all | solution.py:513
  83.0 0.0 copy-done.2
  83.0 0.0 copy-done.3
  83.0 0.0 copy-done.5
  83.0 3.5 %shard_map.111 = f32[10,3,4096]{2,1,0:T(4,128)} custom-call(f32[128,1,768]{2,1,0:T(1,128)S(1)} %all_to_all.11.ret_ref, s32[1,4096]{1,0:T(1,128)S(1)} %bitcast.10, f32[1,4096]{1,0:T(1,128)S(1)} %copy-done.3, f32[4,10]{1,0:T(4,128)S(1)} %copy-done.5), custom_call_target="tpu_custom_call" | custom-call | tf_op jit(solution)/shard_map/pallas_call | solution.py:426
Async XLA Ops:
  31.5 11.8 %copy-start = (f32[4,3,64,256]{3,2,1,0:T(8,128)S(1)}, f32[4,3,64,256]{3,2,1,0:T(8,128)}, u32[]{:S(2)}) copy-start(f32[4,3,64,256]{3,2,1,0:T(8,128)} %param.17) | copy-start | bytes 2359300
  31.5 11.8 %copy-start.1 = (f32[64,256]{1,0:T(8,128)S(1)}, f32[64,256]{1,0:T(8,128)}, u32[]{:S(2)}) copy-start(f32[64,256]{1,0:T(8,128)} %scale_ref.3) | copy-start | bytes 196612
  35.3 10.5 %copy-start.4 = (f32[12,12]{1,0:T(8,128)S(1)}, f32[12,12]{1,0:T(8,128)}, u32[]{:S(2)}) copy-start(f32[12,12]{1,0:T(8,128)} %stiff_ref.1) | copy-start | bytes 1732
  35.3 7.9 %collective-permute-start = (f32[25,8,256]{2,1,0:T(8,128)S(1)}, f32[25,8,256]{2,1,0:T(8,128)S(1)}, u32[]{:S(2)}, u32[]{:S(2)}) collective-permute-start(f32[25,8,256]{2,1,0:T(8,128)S(1)} %get-tuple-element.17.north_ref), channel_id=1, source_target_pairs={{0,96},{32,0},{64,32},{96,64},{1,97},{33,1},{65,33},{97,65},{2,98}... | collective-permute-start | bytes 614408 | tf_op jit(solution)/shard_map/ppermute | solution.py:448
  35.9 7.4 %collective-permute-start.1 = (f32[25,8,256]{2,1,0:T(8,128)S(1)}, f32[25,8,256]{2,1,0:T(8,128)S(1)}, u32[]{:S(2)}, u32[]{:S(2)}) collective-permute-start(f32[25,8,256]{2,1,0:T(8,128)S(1)} %get-tuple-element.18.south_ref), channel_id=1, source_target_pairs={{0,32},{32,64},{64,96},{96,0},{1,33},{33,65},{65,97},{97,1},{2,34}... | collective-permute-start | bytes 614408 | tf_op jit(solution)/shard_map/ppermute | solution.py:448
  43.9 4.0 %collective-permute-start.2 = (f32[80,256]{1,0:T(8,128)S(1)}, f32[80,256]{1,0:T(8,128)S(1)}, u32[]{:S(2)}, u32[]{:S(2)}) collective-permute-start(f32[80,256]{1,0:T(8,128)S(1)} %get-tuple-element.19), channel_id=1, source_target_pairs={{0,31},{1,0},{2,1},{3,2},{4,3},{5,4},{6,5},{7,6},{8,7},{9,8},{10,9... | collective-permute-start | bytes 245768 | tf_op jit(solution)/shard_map/ppermute | solution.py:448
  45.4 2.5 %collective-permute-start.3 = (f32[80,256]{1,0:T(8,128)S(1)}, f32[80,256]{1,0:T(8,128)S(1)}, u32[]{:S(2)}, u32[]{:S(2)}) collective-permute-start(f32[80,256]{1,0:T(8,128)S(1)} %get-tuple-element.20), channel_id=1, source_target_pairs={{0,1},{1,2},{2,3},{3,4},{4,5},{5,6},{6,7},{7,8},{8,9},{9,10},{10,1... | collective-permute-start | bytes 245768 | tf_op jit(solution)/shard_map/ppermute | solution.py:448
  47.8 35.2 %copy-start.2 = (s32[4096,1]{0,1:T(1,128)S(1)}, s32[4096,1]{0,1:T(1,128)}, u32[]{:S(2)}) copy-start(s32[4096,1]{0,1:T(1,128)} %param.9) | copy-start | bytes 49156
  47.8 35.2 %copy-start.3 = (f32[1,4096]{1,0:T(1,128)S(1)}, f32[1,4096]{1,0:T(1,128)}, u32[]{:S(2)}) copy-start(f32[1,4096]{1,0:T(1,128)} %get-tuple-element.23.rank_ref) | copy-start | bytes 49156
  47.8 35.1 %copy-start.5 = (f32[4,10]{1,0:T(4,128)S(1)}, f32[4,10]{1,0:T(4,128)}, u32[]{:S(2)}) copy-start(f32[4,10]{1,0:T(4,128)} %transfer_ref.1) | copy-start | bytes 484
